TPU v7x, 32 devices: a whole 2x2x4 slice. The times are simulated.
32 devices in a mesh: section: 4 (over x, core), expert: 8 (over z, y).
Axes of the slice: x: 2, y: 2, z: 4, core: 2. Of those that a mesh axis runs over, the one named last changes fastest.
Arguments:
- inputs: bfloat16 [2, 1024, 1024], P(None, 'expert'), may hold values from -6 to 6
- norm_gain: float32 [4, 1024], P('section'), may hold values from 0.25 to 1.75
- w_up: bfloat16 [4, 8, 1024, 2048], P('section', 'expert'), may hold values from -0.1875 to 0.1875
- w_down: bfloat16 [4, 8, 2048, 1024], P('section', 'expert'), may hold values from -0.125 to 0.125
- expert_ids: int32 [4, 2, 1024, 2], P('section', None, 'expert'), may hold values from 0 to 7, as said below
- gates: float32 [4, 2, 1024, 2], P('section', None, 'expert'), may hold values from 0.1 to 1
- out_grad: bfloat16 [2, 1024, 1024], P(None, 'expert'), may hold values from -6 to 6
Outputs:
- section_out: bfloat16 [4, 2, 1024, 1024], P('section', None, 'expert')
- in_grad: bfloat16 [4, 2, 1024, 1024], P('section', None, 'expert')
Inputs may be any that keep to these rules, and one draw needn't show every extreme that they name: `expert_ids`: for every layer and micro-batch the two experts of a row differ; in each aligned block of 128 rows (the rows of one device) no expert is named more than 40 times, and one expert, the same in every block of that layer and micro-batch, is named exactly 40 times.
All inputs are finite; a program needn't handle non-finite values.
Results may differ from a plain program's by a relative error of at most 0.012.
Values may be sent and summed in bfloat16 or wider, within the bound.
No kernel may reach another device: no remote copies, remote signals or barrier semaphores. Data moves between devices by JAX's collectives and lax.ppermute only.
A program may use at most 64 MiB of HBM per device.

v0:
```python
import jax
import jax.numpy as jnp
from jax import lax
from jax.sharding import PartitionSpec as P

epsilon = 1e-05
gelu_coef = 0.7978845608028654
cubic_coef = 0.044715
contract_last = (((1,), (1,)), ((), ()))


def shifted(x, axis, by):
    size = lax.axis_size(axis)
    pairs = [(i, i + by) for i in range(size) if 0 <= i + by < size]
    return lax.ppermute(x, axis, pairs)


def gelu_value(pre_act):
    tanh_arg = gelu_coef * (pre_act + cubic_coef * pre_act * pre_act * pre_act)
    return 0.5 * pre_act * (1.0 + jnp.tanh(tanh_arg))


def gelu_slope(pre_act):
    tanh_arg = gelu_coef * (pre_act + cubic_coef * pre_act * pre_act * pre_act)
    tangent = jnp.tanh(tanh_arg)
    return 0.5 * (1.0 + tangent) + 0.5 * pre_act * (1.0 - tangent * tangent) * gelu_coef * (
        1.0 + 3.0 * cubic_coef * pre_act * pre_act
    )


def normalize(state_rows, gain_row):
    values = state_rows.astype(jnp.float32)
    inv_rms = lax.rsqrt(jnp.mean(values * values, axis=-1, keepdims=True) + epsilon)
    return (values * inv_rms * gain_row).astype(jnp.bfloat16)


def norm_backward(upstream, state_rows, normed_grad, gain_row):
    values = state_rows.astype(jnp.float32)
    inv_rms = lax.rsqrt(jnp.mean(values * values, axis=-1, keepdims=True) + epsilon)
    spread = normed_grad * gain_row
    along = jnp.mean(spread * values, axis=-1, keepdims=True)
    return (
        upstream.astype(jnp.float32)
        + inv_rms * spread
        - values * inv_rms * inv_rms * inv_rms * along
    ).astype(jnp.bfloat16)


def slot_targets(block_picks, experts, capacity):
    flat_picks = block_picks.reshape(-1)
    onehot = (flat_picks[:, None] == jnp.arange(experts, dtype=jnp.int32)[None, :]).astype(
        jnp.int32
    )
    earlier = jnp.cumsum(onehot, axis=0) - onehot
    slot_index = jnp.sum(earlier * onehot, axis=1)
    return flat_picks * capacity + slot_index


def pack_pairs(pair_rows, targets, experts, capacity):
    features = pair_rows.shape[1]
    buffer = jnp.zeros((experts * capacity, features), pair_rows.dtype)
    return buffer.at[targets].set(pair_rows).reshape(experts, capacity, features)


def expert_forward(received, up_matrix, down_matrix):
    sources, count_rows, features = received.shape
    pre_act = jnp.dot(
        received.reshape(sources * count_rows, features),
        up_matrix,
        preferred_element_type=jnp.float32,
    )
    active = gelu_value(pre_act).astype(jnp.bfloat16)
    output_rows = jnp.dot(active, down_matrix, preferred_element_type=jnp.float32).astype(
        jnp.bfloat16
    )
    return (
        output_rows.reshape(sources, count_rows, features),
        pre_act.reshape(sources, count_rows, -1),
    )


def expert_backward(grad_rows, pre_act, up_matrix, down_matrix):
    sources, count_rows, features = grad_rows.shape
    flat_pre = pre_act.reshape(sources * count_rows, -1)
    act_grad = lax.dot_general(
        grad_rows.reshape(sources * count_rows, features),
        down_matrix,
        contract_last,
        preferred_element_type=jnp.float32,
    )
    pre_grad = (act_grad * gelu_slope(flat_pre)).astype(jnp.bfloat16)
    input_grad = lax.dot_general(
        pre_grad, up_matrix, contract_last, preferred_element_type=jnp.float32
    ).astype(jnp.bfloat16)
    return input_grad.reshape(sources, count_rows, features)


def keep_slot(stack_rows, value_rows, slot_at, active_now):
    old_rows = lax.dynamic_index_in_dim(stack_rows, slot_at, 0, keepdims=False)
    new_rows = jnp.where(active_now, value_rows, old_rows)
    return lax.dynamic_update_index_in_dim(stack_rows, new_rows, slot_at, 0)


def local(inputs, norm_gain, w_up, w_down, expert_ids, gates, out_grad):
    sections = lax.axis_size("section")
    section_index = lax.axis_index("section")
    experts = lax.axis_size("expert")
    batches, rows_dev, features = inputs.shape
    capacity = max(2, 5 * rows_dev // (2 * experts))
    gain_row = norm_gain[0]
    up_matrix = w_up[0, 0]
    down_matrix = w_down[0, 0]
    hidden = up_matrix.shape[1]
    picks_all = expert_ids[0]
    weights_all = gates[0]
    ticks = sections + batches - 1

    def run_forward(received):
        return expert_forward(received, up_matrix, down_matrix)

    def skip_forward(received):
        return (jnp.zeros_like(received), jnp.zeros((experts, capacity, hidden), jnp.float32))

    pre_shape = (1,)

    def forward_tick(step_index, state_tuple):
        incoming, section_outs, saved_in, saved_pre = state_tuple
        batch_index = step_index - section_index
        active_now = (batch_index >= 0) & (batch_index < batches)
        clipped = jnp.clip(batch_index, 0, batches - 1)
        first_rows = lax.dynamic_index_in_dim(inputs, clipped, 0, keepdims=False)
        state_rows = jnp.where(section_index == 0, first_rows, incoming)
        picks = lax.dynamic_index_in_dim(picks_all, clipped, 0, keepdims=False)
        weights = lax.dynamic_index_in_dim(weights_all, clipped, 0, keepdims=False)
        targets = slot_targets(picks, experts, capacity)
        normed = normalize(state_rows, gain_row)
        send_buffer = pack_pairs(jnp.repeat(normed, 2, axis=0), targets, experts, capacity)
        received = lax.all_to_all(send_buffer, "expert", split_axis=0, concat_axis=0, tiled=True)
        output_rows, pre_act = lax.cond(active_now, run_forward, skip_forward, received)
        returned = lax.all_to_all(
            output_rows, "expert", split_axis=0, concat_axis=0, tiled=True
        ).reshape(experts * capacity, features)
        pair_rows = returned[targets].reshape(rows_dev, 2, features).astype(jnp.float32)
        mixed_rows = (
            state_rows.astype(jnp.float32) + jnp.sum(weights[:, :, None] * pair_rows, axis=1)
        ).astype(jnp.bfloat16)
        mixed_rows = jnp.where(active_now, mixed_rows, jnp.zeros_like(mixed_rows))
        section_outs = keep_slot(section_outs, mixed_rows, clipped, active_now)
        saved_in = keep_slot(saved_in, state_rows, clipped, active_now)
        incoming = shifted(mixed_rows, "section", 1)
        return (incoming, section_outs, saved_in, saved_pre)

    start_rows = jnp.zeros((rows_dev, features), jnp.bfloat16)
    start_stack = jnp.zeros((batches, rows_dev, features), jnp.bfloat16)
    start_pre = jnp.zeros(pre_shape, jnp.float32)
    forward_state = lax.fori_loop(
        0, ticks, forward_tick, (start_rows, start_stack, start_stack, start_pre)
    )
    section_outs = forward_state[1]
    saved_in = forward_state[2]
    saved_pre = forward_state[3]

    def run_replay(operands):
        rows_in, grad_rows = operands
        sources, count_rows, width_in = rows_in.shape
        pre_act = jnp.dot(
            rows_in.reshape(sources * count_rows, width_in),
            up_matrix,
            preferred_element_type=jnp.float32,
        )
        return expert_backward(
            grad_rows, pre_act.reshape(sources, count_rows, -1), up_matrix, down_matrix
        )

    def skip_backward(operands):
        return jnp.zeros_like(operands[0])

    def backward_tick(step_index, state_tuple):
        incoming, grad_stack = state_tuple
        batch_index = step_index - (sections - 1 - section_index)
        active_now = (batch_index >= 0) & (batch_index < batches)
        clipped = jnp.clip(batch_index, 0, batches - 1)
        last_rows = lax.dynamic_index_in_dim(out_grad, clipped, 0, keepdims=False)
        upstream = jnp.where(section_index == sections - 1, last_rows, incoming)
        picks = lax.dynamic_index_in_dim(picks_all, clipped, 0, keepdims=False)
        weights = lax.dynamic_index_in_dim(weights_all, clipped, 0, keepdims=False)
        targets = slot_targets(picks, experts, capacity)
        state_rows = lax.dynamic_index_in_dim(saved_in, clipped, 0, keepdims=False)
        pair_grad = (weights[:, :, None] * upstream.astype(jnp.float32)[:, None, :]).astype(
            jnp.bfloat16
        )
        grad_send = pack_pairs(
            pair_grad.reshape(rows_dev * 2, features), targets, experts, capacity
        )
        normed = normalize(state_rows, gain_row)
        row_send = pack_pairs(jnp.repeat(normed, 2, axis=0), targets, experts, capacity)
        rows_in, grad_rows = (
            lax.all_to_all(row_send, "expert", split_axis=0, concat_axis=0, tiled=True),
            lax.all_to_all(grad_send, "expert", split_axis=0, concat_axis=0, tiled=True),
        )
        back_rows = lax.cond(active_now, run_replay, skip_backward, (rows_in, grad_rows))
        returned = lax.all_to_all(
            back_rows, "expert", split_axis=0, concat_axis=0, tiled=True
        ).reshape(experts * capacity, features)
        normed_grad = jnp.sum(
            returned[targets].reshape(rows_dev, 2, features).astype(jnp.float32), axis=1
        )
        result = norm_backward(upstream, state_rows, normed_grad, gain_row)
        result = jnp.where(active_now, result, jnp.zeros_like(result))
        grad_stack = keep_slot(grad_stack, result, clipped, active_now)
        incoming = shifted(result, "section", -1)
        return (incoming, grad_stack)

    backward_state = lax.fori_loop(0, ticks, backward_tick, (start_rows, start_stack))
    grad_stack = backward_state[1]
    return (section_outs[None], grad_stack[None])


def solution(mesh):
    return jax.shard_map(
        local,
        mesh=mesh,
        in_specs=(
            P(None, "expert", None),
            P("section", None),
            P("section", "expert", None, None),
            P("section", "expert", None, None),
            P("section", None, "expert", None),
            P("section", None, "expert", None),
            P(None, "expert", None),
        ),
        out_specs=(P("section", None, "expert", None), P("section", None, "expert", None)),
        check_vma=False,
    )
```

profile of v0, /device:TPU:0, one launch (start us, length us, event | category | flops | bytes accessed | tf_op | source)
XLA Modules:
  0.0 730.3 jit_solution(15233968557195992638)
XLA Ops:
  3.2 296.3 %while.35 = (s32[]{:T(128)}, bf16[128,1024]{1,0:T(8,128)(2,1)S(1)}, bf16[2,128,1024]{2,1,0:T(8,128)(2,1)}, bf16[2,128,1024]{2,1,0:T(8,128)(2,1)S(1)}, s32[]{:T(1...) while((s32[]{:T(128)}, bf16[128,1024]{1,0:T(8,128)(2,1)S(1)}, ...), condition=%wide.region_9.10_spmd, body=%wide.region_0.9_spmd.sunk | while | flops 2693087488 | bytes 26147680 | solution.py:156
  9.8 7.3 all-to-all-start
  17.1 17.3 %all-to-all-done = bf16[8,40,1024]{2,1,0:T(8,128)(2,1)S(1)} async-done(((bf16[8,40,1024]{2,1,0:T(8,128)(2,1)}), bf16[8,40,1024]{2,1,0:T(8,128)(2,1)S(1)}, u32[]{:S(2)}, u32[]{:S(2)}) %all-to-all-start) | async-done | bytes 655392 | tf_op jit(solution)/shard_map/while/body/eval_jaxpr/all_to_all | solution.py:138
  34.4 7.3 %conditional.4 = (bf16[8,40,1024]{2,1,0:T(8,128)(2,1)}) conditional(s32[]{:T(128)} %convert_element_type.218, () %tuple.95, (bf16[8,40,1024]{2,1,0:T(8,128)(2,1)S(1)}, bf16[1024,2048]{1,0:T(8,128)(2,1)}, bf16[2048,1024]{1,0:T(8,128)(2,1)}) %tuple.96), branch_computations={%region_6.6_spmd, %region_7.7_spmd} | conditional | flops 2690580480 | bytes 9699336 | solution.py:139
  34.4 7.3 %convolution_convert_fusion = bf16[320,1024]{1,0:T(8,128)(2,1)} fusion(bf16[2048,1024]{1,0:T(8,128)(2,1)} %get-tuple-element.497, bf16[320,1024]{1,0:T(8,128)(2,1)S(1)} %bitcast.131, bf16[1024,2048]{1,0:T(8,128)(2,1)} %get-tuple-element.496), kind=kOutput, calls=%fused_computation.11 | convolution fusion | flops 2690580480 | bytes 9699328 | tf_op jit(solution)/shard_map/while/body/eval_jaxpr/cond/branch_1_fun/dot_general | solution.py:73
  46.3 10.7 %all-to-all-done.1 = bf16[8,40,1024]{2,1,0:T(8,128)(2,1)S(1)} async-done(((bf16[8,40,1024]{2,1,0:T(8,128)(2,1)}), bf16[8,40,1024]{2,1,0:T(8,128)(2,1)S(1)}, u32[]{:S(2)}, u32[]{:S(2)}) %all-to-all-start.1) | async-done | bytes 655392 | tf_op jit(solution)/shard_map/while/body/eval_jaxpr/all_to_all | solution.py:140
  70.0 3.7 all-to-all-start
  73.7 16.8 %all-to-all-done = bf16[8,40,1024]{2,1,0:T(8,128)(2,1)S(1)} async-done(((bf16[8,40,1024]{2,1,0:T(8,128)(2,1)}), bf16[8,40,1024]{2,1,0:T(8,128)(2,1)S(1)}, u32[]{:S(2)}, u32[]{:S(2)}) %all-to-all-start) | async-done | bytes 655392 | tf_op jit(solution)/shard_map/while/body/eval_jaxpr/all_to_all | solution.py:138
  90.5 7.3 %conditional.4 = (bf16[8,40,1024]{2,1,0:T(8,128)(2,1)}) conditional(s32[]{:T(128)} %convert_element_type.218, () %tuple.95, (bf16[8,40,1024]{2,1,0:T(8,128)(2,1)S(1)}, bf16[1024,2048]{1,0:T(8,128)(2,1)}, bf16[2048,1024]{1,0:T(8,128)(2,1)}) %tuple.96), branch_computations={%region_6.6_spmd, %region_7.7_spmd} | conditional | flops 2690580480 | bytes 9699336 | solution.py:139
  90.5 7.3 %convolution_convert_fusion = bf16[320,1024]{1,0:T(8,128)(2,1)} fusion(bf16[2048,1024]{1,0:T(8,128)(2,1)} %get-tuple-element.497, bf16[320,1024]{1,0:T(8,128)(2,1)S(1)} %bitcast.131, bf16[1024,2048]{1,0:T(8,128)(2,1)} %get-tuple-element.496), kind=kOutput, calls=%fused_computation.11 | convolution fusion | flops 2690580480 | bytes 9699328 | tf_op jit(solution)/shard_map/while/body/eval_jaxpr/cond/branch_1_fun/dot_general | solution.py:73
  97.8 4.7 all-to-all-start.1
  103.6 17.3 %all-to-all-done.1 = bf16[8,40,1024]{2,1,0:T(8,128)(2,1)S(1)} async-done(((bf16[8,40,1024]{2,1,0:T(8,128)(2,1)}), bf16[8,40,1024]{2,1,0:T(8,128)(2,1)S(1)}, u32[]{:S(2)}, u32[]{:S(2)}) %all-to-all-start.1) | async-done | bytes 655392 | tf_op jit(solution)/shard_map/while/body/eval_jaxpr/all_to_all | solution.py:140
  134.1 4.0 all-to-all-start
  138.1 17.8 %all-to-all-done = bf16[8,40,1024]{2,1,0:T(8,128)(2,1)S(1)} async-done(((bf16[8,40,1024]{2,1,0:T(8,128)(2,1)}), bf16[8,40,1024]{2,1,0:T(8,128)(2,1)S(1)}, u32[]{:S(2)}, u32[]{:S(2)}) %all-to-all-start) | async-done | bytes 655392 | tf_op jit(solution)/shard_map/while/body/eval_jaxpr/all_to_all | solution.py:138
  156.8 4.5 all-to-all-start.1
  162.3 12.2 %all-to-all-done.1 = bf16[8,40,1024]{2,1,0:T(8,128)(2,1)S(1)} async-done(((bf16[8,40,1024]{2,1,0:T(8,128)(2,1)}), bf16[8,40,1024]{2,1,0:T(8,128)(2,1)S(1)}, u32[]{:S(2)}, u32[]{:S(2)}) %all-to-all-start.1) | async-done | bytes 655392 | tf_op jit(solution)/shard_map/while/body/eval_jaxpr/all_to_all | solution.py:140
  178.6 7.2 collective-permute-start
  193.4 3.7 all-to-all-start
  197.1 13.3 %all-to-all-done = bf16[8,40,1024]{2,1,0:T(8,128)(2,1)S(1)} async-done(((bf16[8,40,1024]{2,1,0:T(8,128)(2,1)}), bf16[8,40,1024]{2,1,0:T(8,128)(2,1)S(1)}, u32[]{:S(2)}, u32[]{:S(2)}) %all-to-all-start) | async-done | bytes 655392 | tf_op jit(solution)/shard_map/while/body/eval_jaxpr/all_to_all | solution.py:138
  211.3 7.2 all-to-all-start.1
  219.5 17.4 %all-to-all-done.1 = bf16[8,40,1024]{2,1,0:T(8,128)(2,1)S(1)} async-done(((bf16[8,40,1024]{2,1,0:T(8,128)(2,1)}), bf16[8,40,1024]{2,1,0:T(8,128)(2,1)S(1)}, u32[]{:S(2)}, u32[]{:S(2)}) %all-to-all-start.1) | async-done | bytes 655392 | tf_op jit(solution)/shard_map/while/body/eval_jaxpr/all_to_all | solution.py:140
  250.9 3.7 all-to-all-start
  254.6 11.7 %all-to-all-done = bf16[8,40,1024]{2,1,0:T(8,128)(2,1)S(1)} async-done(((bf16[8,40,1024]{2,1,0:T(8,128)(2,1)}), bf16[8,40,1024]{2,1,0:T(8,128)(2,1)S(1)}, u32[]{:S(2)}, u32[]{:S(2)}) %all-to-all-start) | async-done | bytes 655392 | tf_op jit(solution)/shard_map/while/body/eval_jaxpr/all_to_all | solution.py:138
  267.2 3.7 all-to-all-start.1
  271.9 10.8 %all-to-all-done.1 = bf16[8,40,1024]{2,1,0:T(8,128)(2,1)S(1)} async-done(((bf16[8,40,1024]{2,1,0:T(8,128)(2,1)}), bf16[8,40,1024]{2,1,0:T(8,128)(2,1)S(1)}, u32[]{:S(2)}, u32[]{:S(2)}) %all-to-all-start.1) | async-done | bytes 655392 | tf_op jit(solution)/shard_map/while/body/eval_jaxpr/all_to_all | solution.py:140
  286.7 11.7 %collective-permute-start = (bf16[128,1024]{1,0:T(8,128)(2,1)S(1)}, bf16[128,1024]{1,0:T(8,128)(2,1)S(1)}, u32[]{:S(2)}, u32[]{:S(2)}) collective-permute-start(bf16[128,1024]{1,0:T(8,128)(2,1)S(1)} %get-tuple-element.753), channel_id=1, source_target_pairs={{0,8},{8,16},{16,24},{1,9},{9,17},{17,25},{2,10},{10,18},{18,26},{... | collective-permute-start | bytes 786440 | tf_op jit(solution)/shard_map/while/body/eval_jaxpr/ppermute | solution.py:15
  300.4 429.9 %while.36 = (s32[]{:T(128)}, bf16[128,1024]{1,0:T(8,128)(2,1)S(1)}, bf16[2,128,1024]{2,1,0:T(8,128)(2,1)}, s32[]{:T(128)}, pred[]{:T(512)}, /*index=5*/bf16[2,12...) while((s32[]{:T(128)}, bf16[128,1024]{1,0:T(8,128)(2,1)S(1)}, ...), condition=%wide.region_21.22_spmd, body=%wide.region_10.21_spmd.sunk | while | flops 4043522048 | bytes 48344616 | solution.py:214
  306.0 4.2 all-to-all-start.3
  315.0 6.9 all-to-all-done.3
  321.9 3.7 all-to-all-start.2
  325.6 14.5 %all-to-all-done.2 = bf16[8,40,1024]{2,1,0:T(8,128)(2,1)S(1)} async-done(((bf16[8,40,1024]{2,1,0:T(8,128)(2,1)}), bf16[8,40,1024]{2,1,0:T(8,128)(2,1)S(1)}, u32[]{:S(2)}, u32[]{:S(2)}) %all-to-all-start.2) | async-done | bytes 655392 | tf_op jit(solution)/shard_map/while/body/eval_jaxpr/all_to_all | solution.py:199
  341.0 3.7 all-to-all-start.4
  344.7 15.1 %all-to-all-done.4 = bf16[8,40,1024]{2,1,0:T(8,128)(2,1)S(1)} async-done(((bf16[8,40,1024]{2,1,0:T(8,128)(2,1)}), bf16[8,40,1024]{2,1,0:T(8,128)(2,1)S(1)}, u32[]{:S(2)}, u32[]{:S(2)}) %all-to-all-start.4) | async-done | bytes 655392 | tf_op jit(solution)/shard_map/while/body/eval_jaxpr/all_to_all | solution.py:202
  365.3 15.3 %collective-permute-done.1 = bf16[128,1024]{1,0:T(8,128)(2,1)S(1)} collective-permute-done((bf16[128,1024]{1,0:T(8,128)(2,1)S(1)}, bf16[128,1024]{1,0:T(8,128)(2,1)S(1)}, u32[]{:S(2)}, u32[]{:S(2)}) %collective-permute-start.1) | collective-permute-done | bytes 262176 | tf_op jit(solution)/shard_map/while/body/eval_jaxpr/ppermute | solution.py:15
  386.1 4.2 all-to-all-start.3
  395.0 8.5 %all-to-all-done.3 = bf16[8,40,1024]{2,1,0:T(8,128)(2,1)} async-done(((bf16[8,40,1024]{2,1,0:T(8,128)(2,1)}), bf16[8,40,1024]{2,1,0:T(8,128)(2,1)}, u32[]{:S(2)}, u32[]{:S(2)}) %all-to-all-start.3) | async-done | bytes 655392 | tf_op jit(solution)/shard_map/while/body/eval_jaxpr/all_to_all | solution.py:198
  403.5 7.2 all-to-all-start.2
  410.7 18.4 %all-to-all-done.2 = bf16[8,40,1024]{2,1,0:T(8,128)(2,1)S(1)} async-done(((bf16[8,40,1024]{2,1,0:T(8,128)(2,1)}), bf16[8,40,1024]{2,1,0:T(8,128)(2,1)S(1)}, u32[]{:S(2)}, u32[]{:S(2)}) %all-to-all-start.2) | async-done | bytes 655392 | tf_op jit(solution)/shard_map/while/body/eval_jaxpr/all_to_all | solution.py:199
  430.1 3.9 all-to-all-start.4
  434.1 17.5 %all-to-all-done.4 = bf16[8,40,1024]{2,1,0:T(8,128)(2,1)S(1)} async-done(((bf16[8,40,1024]{2,1,0:T(8,128)(2,1)}), bf16[8,40,1024]{2,1,0:T(8,128)(2,1)S(1)}, u32[]{:S(2)}, u32[]{:S(2)}) %all-to-all-start.4) | async-done | bytes 655392 | tf_op jit(solution)/shard_map/while/body/eval_jaxpr/all_to_all | solution.py:202
  464.7 4.2 all-to-all-start.3
  473.6 6.9 all-to-all-done.3
  484.2 11.7 %all-to-all-done.2 = bf16[8,40,1024]{2,1,0:T(8,128)(2,1)S(1)} async-done(((bf16[8,40,1024]{2,1,0:T(8,128)(2,1)}), bf16[8,40,1024]{2,1,0:T(8,128)(2,1)S(1)}, u32[]{:S(2)}, u32[]{:S(2)}) %all-to-all-start.2) | async-done | bytes 655392 | tf_op jit(solution)/shard_map/while/body/eval_jaxpr/all_to_all | solution.py:199
  496.8 3.7 all-to-all-start.4
  500.6 14.4 %all-to-all-done.4 = bf16[8,40,1024]{2,1,0:T(8,128)(2,1)S(1)} async-done(((bf16[8,40,1024]{2,1,0:T(8,128)(2,1)}), bf16[8,40,1024]{2,1,0:T(8,128)(2,1)S(1)}, u32[]{:S(2)}, u32[]{:S(2)}) %all-to-all-start.4) | async-done | bytes 655392 | tf_op jit(solution)/shard_map/while/body/eval_jaxpr/all_to_all | solution.py:202
  520.5 42.0 %collective-permute-done.1 = bf16[128,1024]{1,0:T(8,128)(2,1)S(1)} collective-permute-done((bf16[128,1024]{1,0:T(8,128)(2,1)S(1)}, bf16[128,1024]{1,0:T(8,128)(2,1)S(1)}, u32[]{:S(2)}, u32[]{:S(2)}) %collective-permute-start.1) | collective-permute-done | bytes 262176 | tf_op jit(solution)/shard_map/while/body/eval_jaxpr/ppermute | solution.py:15
  568.0 4.2 all-to-all-start.3
  576.9 6.9 all-to-all-done.3
  583.9 3.7 all-to-all-start.2
  587.5 12.1 %all-to-all-done.2 = bf16[8,40,1024]{2,1,0:T(8,128)(2,1)S(1)} async-done(((bf16[8,40,1024]{2,1,0:T(8,128)(2,1)}), bf16[8,40,1024]{2,1,0:T(8,128)(2,1)S(1)}, u32[]{:S(2)}, u32[]{:S(2)}) %all-to-all-start.2) | async-done | bytes 655392 | tf_op jit(solution)/shard_map/while/body/eval_jaxpr/all_to_all | solution.py:199
  599.7 14.1 %conditional.5 = (bf16[8,40,1024]{2,1,0:T(8,128)(2,1)}) conditional(s32[]{:T(128)} %convert_element_type.224, () %tuple.100, (bf16[8,40,1024]{2,1,0:T(8,128)(2,1)S(1)}, bf16[2048,1024]{1,0:T(8,128)(2,1)}, bf16[8,40,1024]{2,1,0:T(8,128)(2,1)}, bf16[1024,2048]{1,0:T(8,128)(2,1)}) %tuple.101), branch_computations={%region_17.17_spmd, %region_18.18_spmd} | conditional | flops 4039311360 | bytes 19791880 | solution.py:201
  599.7 5.5 fusion.58
  605.1 8.6 %convolution_convert_fusion.1 = bf16[320,1024]{1,0:T(8,128)(2,1)} fusion(bf16[1024,2048]{1,0:T(8,128)(2,1)} %get-tuple-element.514, bf16[320,1024]{1,0:T(8,128)(2,1)S(1)} %bitcast.130, bf16[2048,1024]{1,0:T(8,128)(2,1)} %get-tuple-element.512, f32[320,2048]{1,0:T(8,128)} %fusion.58), kind=kOutput, calls=%fused_computation.29 | convolution fusion | flops 2697134080 | bytes 12320768 | tf_op jit(solution)/shard_map/while/body/eval_jaxpr/cond/branch_1_fun/dot_general | solution.py:92
  613.7 3.7 all-to-all-start.4
  617.5 11.6 %all-to-all-done.4 = bf16[8,40,1024]{2,1,0:T(8,128)(2,1)S(1)} async-done(((bf16[8,40,1024]{2,1,0:T(8,128)(2,1)}), bf16[8,40,1024]{2,1,0:T(8,128)(2,1)S(1)}, u32[]{:S(2)}, u32[]{:S(2)}) %all-to-all-start.4) | async-done | bytes 655392 | tf_op jit(solution)/shard_map/while/body/eval_jaxpr/all_to_all | solution.py:202
  634.7 9.4 %collective-permute-done.1 = bf16[128,1024]{1,0:T(8,128)(2,1)S(1)} collective-permute-done((bf16[128,1024]{1,0:T(8,128)(2,1)S(1)}, bf16[128,1024]{1,0:T(8,128)(2,1)S(1)}, u32[]{:S(2)}, u32[]{:S(2)}) %collective-permute-start.1) | collective-permute-done | bytes 262176 | tf_op jit(solution)/shard_map/while/body/eval_jaxpr/ppermute | solution.py:15
  649.5 4.2 all-to-all-start.3
  658.5 8.5 %all-to-all-done.3 = bf16[8,40,1024]{2,1,0:T(8,128)(2,1)} async-done(((bf16[8,40,1024]{2,1,0:T(8,128)(2,1)}), bf16[8,40,1024]{2,1,0:T(8,128)(2,1)}, u32[]{:S(2)}, u32[]{:S(2)}) %all-to-all-start.3) | async-done | bytes 655392 | tf_op jit(solution)/shard_map/while/body/eval_jaxpr/all_to_all | solution.py:198
  667.0 7.5 %all-to-all-start.2 = ((bf16[8,40,1024]{2,1,0:T(8,128)(2,1)}), bf16[8,40,1024]{2,1,0:T(8,128)(2,1)S(1)}, u32[]{:S(2)}, u32[]{:S(2)}) async-start(bf16[8,40,1024]{2,1,0:T(8,128)(2,1)} %bitcast.124), calls=%async_computation.2 | async-start | bytes 1310720 | tf_op jit(solution)/shard_map/while/body/eval_jaxpr/all_to_all | solution.py:199
  674.5 18.8 %all-to-all-done.2 = bf16[8,40,1024]{2,1,0:T(8,128)(2,1)S(1)} async-done(((bf16[8,40,1024]{2,1,0:T(8,128)(2,1)}), bf16[8,40,1024]{2,1,0:T(8,128)(2,1)S(1)}, u32[]{:S(2)}, u32[]{:S(2)}) %all-to-all-start.2) | async-done | bytes 655392 | tf_op jit(solution)/shard_map/while/body/eval_jaxpr/all_to_all | solution.py:199
  693.3 14.1 %conditional.5 = (bf16[8,40,1024]{2,1,0:T(8,128)(2,1)}) conditional(s32[]{:T(128)} %convert_element_type.224, () %tuple.100, (bf16[8,40,1024]{2,1,0:T(8,128)(2,1)S(1)}, bf16[2048,1024]{1,0:T(8,128)(2,1)}, bf16[8,40,1024]{2,1,0:T(8,128)(2,1)}, bf16[1024,2048]{1,0:T(8,128)(2,1)}) %tuple.101), branch_computations={%region_17.17_spmd, %region_18.18_spmd} | conditional | flops 4039311360 | bytes 19791880 | solution.py:201
  693.3 5.5 fusion.58
  698.7 8.6 %convolution_convert_fusion.1 = bf16[320,1024]{1,0:T(8,128)(2,1)} fusion(bf16[1024,2048]{1,0:T(8,128)(2,1)} %get-tuple-element.514, bf16[320,1024]{1,0:T(8,128)(2,1)S(1)} %bitcast.130, bf16[2048,1024]{1,0:T(8,128)(2,1)} %get-tuple-element.512, f32[320,2048]{1,0:T(8,128)} %fusion.58), kind=kOutput, calls=%fused_computation.29 | convolution fusion | flops 2697134080 | bytes 12320768 | tf_op jit(solution)/shard_map/while/body/eval_jaxpr/cond/branch_1_fun/dot_general | solution.py:92
  711.0 11.6 %all-to-all-done.4 = bf16[8,40,1024]{2,1,0:T(8,128)(2,1)S(1)} async-done(((bf16[8,40,1024]{2,1,0:T(8,128)(2,1)}), bf16[8,40,1024]{2,1,0:T(8,128)(2,1)S(1)}, u32[]{:S(2)}, u32[]{:S(2)}) %all-to-all-start.4) | async-done | bytes 655392 | tf_op jit(solution)/shard_map/while/body/eval_jaxpr/all_to_all | solution.py:202
  (372 shorter events, 175.7 us)
Async XLA Ops:
  9.8 24.6 %all-to-all-start = ((bf16[8,40,1024]{2,1,0:T(8,128)(2,1)}), bf16[8,40,1024]{2,1,0:T(8,128)(2,1)S(1)}, u32[]{:S(2)}, u32[]{:S(2)}) async-start(bf16[8,40,1024]{2,1,0:T(8,128)(2,1)} %bitcast.113), calls=%async_computation | async-start | bytes 1310720 | tf_op jit(solution)/shard_map/while/body/eval_jaxpr/all_to_all | solution.py:138
  41.7 15.3 %all-to-all-start.1 = ((bf16[8,40,1024]{2,1,0:T(8,128)(2,1)}), bf16[8,40,1024]{2,1,0:T(8,128)(2,1)S(1)}, u32[]{:S(2)}, u32[]{:S(2)}) async-start(bf16[8,40,1024]{2,1,0:T(8,128)(2,1)} %get-tuple-element.871), calls=%async_computation.1 | async-start | bytes 1310720 | tf_op jit(solution)/shard_map/while/body/eval_jaxpr/all_to_all | solution.py:140
  61.0 2.4 collective-permute-start
  70.0 20.5 %all-to-all-start = ((bf16[8,40,1024]{2,1,0:T(8,128)(2,1)}), bf16[8,40,1024]{2,1,0:T(8,128)(2,1)S(1)}, u32[]{:S(2)}, u32[]{:S(2)}) async-start(bf16[8,40,1024]{2,1,0:T(8,128)(2,1)} %bitcast.113), calls=%async_computation | async-start | bytes 1310720 | tf_op jit(solution)/shard_map/while/body/eval_jaxpr/all_to_all | solution.py:138
  97.8 23.0 %all-to-all-start.1 = ((bf16[8,40,1024]{2,1,0:T(8,128)(2,1)}), bf16[8,40,1024]{2,1,0:T(8,128)(2,1)S(1)}, u32[]{:S(2)}, u32[]{:S(2)}) async-start(bf16[8,40,1024]{2,1,0:T(8,128)(2,1)} %get-tuple-element.871), calls=%async_computation.1 | async-start | bytes 1310720 | tf_op jit(solution)/shard_map/while/body/eval_jaxpr/all_to_all | solution.py:140
  124.9 2.7 collective-permute-start
  134.1 21.8 %all-to-all-start = ((bf16[8,40,1024]{2,1,0:T(8,128)(2,1)}), bf16[8,40,1024]{2,1,0:T(8,128)(2,1)S(1)}, u32[]{:S(2)}, u32[]{:S(2)}) async-start(bf16[8,40,1024]{2,1,0:T(8,128)(2,1)} %bitcast.113), calls=%async_computation | async-start | bytes 1310720 | tf_op jit(solution)/shard_map/while/body/eval_jaxpr/all_to_all | solution.py:138
  156.8 17.7 %all-to-all-start.1 = ((bf16[8,40,1024]{2,1,0:T(8,128)(2,1)}), bf16[8,40,1024]{2,1,0:T(8,128)(2,1)S(1)}, u32[]{:S(2)}, u32[]{:S(2)}) async-start(bf16[8,40,1024]{2,1,0:T(8,128)(2,1)} %get-tuple-element.871), calls=%async_computation.1 | async-start | bytes 1310720 | tf_op jit(solution)/shard_map/while/body/eval_jaxpr/all_to_all | solution.py:140
  178.6 8.3 %collective-permute-start = (bf16[128,1024]{1,0:T(8,128)(2,1)S(1)}, bf16[128,1024]{1,0:T(8,128)(2,1)S(1)}, u32[]{:S(2)}, u32[]{:S(2)}) collective-permute-start(bf16[128,1024]{1,0:T(8,128)(2,1)S(1)} %get-tuple-element.753), channel_id=1, source_target_pairs={{0,8},{8,16},{16,24},{1,9},{9,17},{17,25},{2,10},{10,18},{18,26},{... | collective-permute-start | bytes 786440 | tf_op jit(solution)/shard_map/while/body/eval_jaxpr/ppermute | solution.py:15
  193.4 16.9 %all-to-all-start = ((bf16[8,40,1024]{2,1,0:T(8,128)(2,1)}), bf16[8,40,1024]{2,1,0:T(8,128)(2,1)S(1)}, u32[]{:S(2)}, u32[]{:S(2)}) async-start(bf16[8,40,1024]{2,1,0:T(8,128)(2,1)} %bitcast.113), calls=%async_computation | async-start | bytes 1310720 | tf_op jit(solution)/shard_map/while/body/eval_jaxpr/all_to_all | solution.py:138
  211.3 25.7 %all-to-all-start.1 = ((bf16[8,40,1024]{2,1,0:T(8,128)(2,1)}), bf16[8,40,1024]{2,1,0:T(8,128)(2,1)S(1)}, u32[]{:S(2)}, u32[]{:S(2)}) async-start(bf16[8,40,1024]{2,1,0:T(8,128)(2,1)} %get-tuple-element.871), calls=%async_computation.1 | async-start | bytes 1310720 | tf_op jit(solution)/shard_map/while/body/eval_jaxpr/all_to_all | solution.py:140
  241.0 3.3 collective-permute-start
  250.9 15.4 %all-to-all-start = ((bf16[8,40,1024]{2,1,0:T(8,128)(2,1)}), bf16[8,40,1024]{2,1,0:T(8,128)(2,1)S(1)}, u32[]{:S(2)}, u32[]{:S(2)}) async-start(bf16[8,40,1024]{2,1,0:T(8,128)(2,1)} %bitcast.113), calls=%async_computation | async-start | bytes 1310720 | tf_op jit(solution)/shard_map/while/body/eval_jaxpr/all_to_all | solution.py:138
  267.2 15.5 %all-to-all-start.1 = ((bf16[8,40,1024]{2,1,0:T(8,128)(2,1)}), bf16[8,40,1024]{2,1,0:T(8,128)(2,1)S(1)}, u32[]{:S(2)}, u32[]{:S(2)}) async-start(bf16[8,40,1024]{2,1,0:T(8,128)(2,1)} %get-tuple-element.871), calls=%async_computation.1 | async-start | bytes 1310720 | tf_op jit(solution)/shard_map/while/body/eval_jaxpr/all_to_all | solution.py:140
  286.7 12.8 %collective-permute-start = (bf16[128,1024]{1,0:T(8,128)(2,1)S(1)}, bf16[128,1024]{1,0:T(8,128)(2,1)S(1)}, u32[]{:S(2)}, u32[]{:S(2)}) collective-permute-start(bf16[128,1024]{1,0:T(8,128)(2,1)S(1)} %get-tuple-element.753), channel_id=1, source_target_pairs={{0,8},{8,16},{16,24},{1,9},{9,17},{17,25},{2,10},{10,18},{18,26},{... | collective-permute-start | bytes 786440 | tf_op jit(solution)/shard_map/while/body/eval_jaxpr/ppermute | solution.py:15
  300.6 9.7 %copy-start.1 = (f32[2,128,2]{2,1,0:T(8,128)}, f32[2,128,2]{2,1,0:T(8,128)S(1)}, u32[]{:S(2)}) copy-start(f32[2,128,2]{2,1,0:T(8,128)S(1)} %get-tuple-element.863) | copy-start | bytes 6148 | tf_op jit(solution)/shard_map/while
  300.6 9.7 %copy-start.3 = (bf16[2,128,1024]{2,1,0:T(8,128)(2,1)S(1)}, bf16[2,128,1024]{2,1,0:T(8,128)(2,1)}, u32[]{:S(2)}) copy-start(bf16[2,128,1024]{2,1,0:T(8,128)(2,1)} %get-tuple-element.859) | copy-start | bytes 1572868 | tf_op jit(solution)/shard_map/while
  306.0 15.9 %all-to-all-start.3 = ((bf16[8,40,1024]{2,1,0:T(8,128)(2,1)}), bf16[8,40,1024]{2,1,0:T(8,128)(2,1)}, u32[]{:S(2)}, u32[]{:S(2)}) async-start(bf16[8,40,1024]{2,1,0:T(8,128)(2,1)} %bitcast.126), calls=%async_computation.3 | async-start | bytes 1310720 | tf_op jit(solution)/shard_map/while/body/eval_jaxpr/all_to_all | solution.py:198
  321.9 18.2 %all-to-all-start.2 = ((bf16[8,40,1024]{2,1,0:T(8,128)(2,1)}), bf16[8,40,1024]{2,1,0:T(8,128)(2,1)S(1)}, u32[]{:S(2)}, u32[]{:S(2)}) async-start(bf16[8,40,1024]{2,1,0:T(8,128)(2,1)} %bitcast.124), calls=%async_computation.2 | async-start | bytes 1310720 | tf_op jit(solution)/shard_map/while/body/eval_jaxpr/all_to_all | solution.py:199
  340.0 4.6 copy-start
  341.0 18.8 %all-to-all-start.4 = ((bf16[8,40,1024]{2,1,0:T(8,128)(2,1)}), bf16[8,40,1024]{2,1,0:T(8,128)(2,1)S(1)}, u32[]{:S(2)}, u32[]{:S(2)}) async-start(bf16[8,40,1024]{2,1,0:T(8,128)(2,1)} %get-tuple-element.872), calls=%async_computation.4 | async-start | bytes 1310720 | tf_op jit(solution)/shard_map/while/body/eval_jaxpr/all_to_all | solution.py:202
  360.9 1.9 copy-start.4
  361.6 19.0 %copy-start.2 = (f32[2,128,2]{2,1,0:T(8,128)S(1)}, f32[2,128,2]{2,1,0:T(8,128)}, u32[]{:S(2)}) copy-start(f32[2,128,2]{2,1,0:T(8,128)} %copy-done.1) | copy-start | bytes 6148 | tf_op jit(solution)/shard_map/while
  364.0 16.6 %collective-permute-start.1 = (bf16[128,1024]{1,0:T(8,128)(2,1)S(1)}, bf16[128,1024]{1,0:T(8,128)(2,1)S(1)}, u32[]{:S(2)}, u32[]{:S(2)}) collective-permute-start(bf16[128,1024]{1,0:T(8,128)(2,1)S(1)} %get-tuple-element.770), channel_id=1, source_target_pairs={{8,0},{16,8},{24,16},{9,1},{17,9},{25,17},{10,2},{18,10},{26,18},{... | collective-permute-start | bytes 786440 | tf_op jit(solution)/shard_map/while/body/eval_jaxpr/ppermute | solution.py:15
  380.7 9.6 %copy-start.1 = (f32[2,128,2]{2,1,0:T(8,128)}, f32[2,128,2]{2,1,0:T(8,128)S(1)}, u32[]{:S(2)}) copy-start(f32[2,128,2]{2,1,0:T(8,128)S(1)} %get-tuple-element.863) | copy-start | bytes 6148 | tf_op jit(solution)/shard_map/while
  380.7 9.6 %copy-start.3 = (bf16[2,128,1024]{2,1,0:T(8,128)(2,1)S(1)}, bf16[2,128,1024]{2,1,0:T(8,128)(2,1)}, u32[]{:S(2)}) copy-start(bf16[2,128,1024]{2,1,0:T(8,128)(2,1)} %get-tuple-element.859) | copy-start | bytes 1572868 | tf_op jit(solution)/shard_map/while
  386.1 17.4 %all-to-all-start.3 = ((bf16[8,40,1024]{2,1,0:T(8,128)(2,1)}), bf16[8,40,1024]{2,1,0:T(8,128)(2,1)}, u32[]{:S(2)}, u32[]{:S(2)}) async-start(bf16[8,40,1024]{2,1,0:T(8,128)(2,1)} %bitcast.126), calls=%async_computation.3 | async-start | bytes 1310720 | tf_op jit(solution)/shard_map/while/body/eval_jaxpr/all_to_all | solution.py:198
  403.5 25.6 %all-to-all-start.2 = ((bf16[8,40,1024]{2,1,0:T(8,128)(2,1)}), bf16[8,40,1024]{2,1,0:T(8,128)(2,1)S(1)}, u32[]{:S(2)}, u32[]{:S(2)}) async-start(bf16[8,40,1024]{2,1,0:T(8,128)(2,1)} %bitcast.124), calls=%async_computation.2 | async-start | bytes 1310720 | tf_op jit(solution)/shard_map/while/body/eval_jaxpr/all_to_all | solution.py:199
  429.1 4.9 copy-start
  430.1 21.5 %all-to-all-start.4 = ((bf16[8,40,1024]{2,1,0:T(8,128)(2,1)}), bf16[8,40,1024]{2,1,0:T(8,128)(2,1)S(1)}, u32[]{:S(2)}, u32[]{:S(2)}) async-start(bf16[8,40,1024]{2,1,0:T(8,128)(2,1)} %get-tuple-element.872), calls=%async_computation.4 | async-start | bytes 1310720 | tf_op jit(solution)/shard_map/while/body/eval_jaxpr/all_to_all | solution.py:202
  452.8 1.9 copy-start.4
  453.4 5.8 copy-start.2
  455.9 3.4 collective-permute-start.1
  459.3 9.6 %copy-start.1 = (f32[2,128,2]{2,1,0:T(8,128)}, f32[2,128,2]{2,1,0:T(8,128)S(1)}, u32[]{:S(2)}) copy-start(f32[2,128,2]{2,1,0:T(8,128)S(1)} %get-tuple-element.863) | copy-start | bytes 6148 | tf_op jit(solution)/shard_map/while
  459.3 9.6 %copy-start.3 = (bf16[2,128,1024]{2,1,0:T(8,128)(2,1)S(1)}, bf16[2,128,1024]{2,1,0:T(8,128)(2,1)}, u32[]{:S(2)}) copy-start(bf16[2,128,1024]{2,1,0:T(8,128)(2,1)} %get-tuple-element.859) | copy-start | bytes 1572868 | tf_op jit(solution)/shard_map/while
  464.7 15.9 %all-to-all-start.3 = ((bf16[8,40,1024]{2,1,0:T(8,128)(2,1)}), bf16[8,40,1024]{2,1,0:T(8,128)(2,1)}, u32[]{:S(2)}, u32[]{:S(2)}) async-start(bf16[8,40,1024]{2,1,0:T(8,128)(2,1)} %bitcast.126), calls=%async_computation.3 | async-start | bytes 1310720 | tf_op jit(solution)/shard_map/while/body/eval_jaxpr/all_to_all | solution.py:198
  480.6 15.4 %all-to-all-start.2 = ((bf16[8,40,1024]{2,1,0:T(8,128)(2,1)}), bf16[8,40,1024]{2,1,0:T(8,128)(2,1)S(1)}, u32[]{:S(2)}, u32[]{:S(2)}) async-start(bf16[8,40,1024]{2,1,0:T(8,128)(2,1)} %bitcast.124), calls=%async_computation.2 | async-start | bytes 1310720 | tf_op jit(solution)/shard_map/while/body/eval_jaxpr/all_to_all | solution.py:199
  495.9 4.6 copy-start
  496.8 18.1 %all-to-all-start.4 = ((bf16[8,40,1024]{2,1,0:T(8,128)(2,1)}), bf16[8,40,1024]{2,1,0:T(8,128)(2,1)S(1)}, u32[]{:S(2)}, u32[]{:S(2)}) async-start(bf16[8,40,1024]{2,1,0:T(8,128)(2,1)} %get-tuple-element.872), calls=%async_computation.4 | async-start | bytes 1310720 | tf_op jit(solution)/shard_map/while/body/eval_jaxpr/all_to_all | solution.py:202
  516.1 1.9 copy-start.4
  516.8 45.8 %copy-start.2 = (f32[2,128,2]{2,1,0:T(8,128)S(1)}, f32[2,128,2]{2,1,0:T(8,128)}, u32[]{:S(2)}) copy-start(f32[2,128,2]{2,1,0:T(8,128)} %copy-done.1) | copy-start | bytes 6148 | tf_op jit(solution)/shard_map/while
  519.2 43.3 %collective-permute-start.1 = (bf16[128,1024]{1,0:T(8,128)(2,1)S(1)}, bf16[128,1024]{1,0:T(8,128)(2,1)S(1)}, u32[]{:S(2)}, u32[]{:S(2)}) collective-permute-start(bf16[128,1024]{1,0:T(8,128)(2,1)S(1)} %get-tuple-element.770), channel_id=1, source_target_pairs={{8,0},{16,8},{24,16},{9,1},{17,9},{25,17},{10,2},{18,10},{26,18},{... | collective-permute-start | bytes 786440 | tf_op jit(solution)/shard_map/while/body/eval_jaxpr/ppermute | solution.py:15
  562.6 9.6 %copy-start.1 = (f32[2,128,2]{2,1,0:T(8,128)}, f32[2,128,2]{2,1,0:T(8,128)S(1)}, u32[]{:S(2)}) copy-start(f32[2,128,2]{2,1,0:T(8,128)S(1)} %get-tuple-element.863) | copy-start | bytes 6148 | tf_op jit(solution)/shard_map/while
  562.6 9.6 %copy-start.3 = (bf16[2,128,1024]{2,1,0:T(8,128)(2,1)S(1)}, bf16[2,128,1024]{2,1,0:T(8,128)(2,1)}, u32[]{:S(2)}) copy-start(bf16[2,128,1024]{2,1,0:T(8,128)(2,1)} %get-tuple-element.859) | copy-start | bytes 1572868 | tf_op jit(solution)/shard_map/while
  568.0 15.9 %all-to-all-start.3 = ((bf16[8,40,1024]{2,1,0:T(8,128)(2,1)}), bf16[8,40,1024]{2,1,0:T(8,128)(2,1)}, u32[]{:S(2)}, u32[]{:S(2)}) async-start(bf16[8,40,1024]{2,1,0:T(8,128)(2,1)} %bitcast.126), calls=%async_computation.3 | async-start | bytes 1310720 | tf_op jit(solution)/shard_map/while/body/eval_jaxpr/all_to_all | solution.py:198
  583.9 15.8 %all-to-all-start.2 = ((bf16[8,40,1024]{2,1,0:T(8,128)(2,1)}), bf16[8,40,1024]{2,1,0:T(8,128)(2,1)S(1)}, u32[]{:S(2)}, u32[]{:S(2)}) async-start(bf16[8,40,1024]{2,1,0:T(8,128)(2,1)} %bitcast.124), calls=%async_computation.2 | async-start | bytes 1310720 | tf_op jit(solution)/shard_map/while/body/eval_jaxpr/all_to_all | solution.py:199
  599.7 17.8 %copy-start = (bf16[2,128,1024]{2,1,0:T(8,128)(2,1)S(1)}, bf16[2,128,1024]{2,1,0:T(8,128)(2,1)}, u32[]{:S(2)}) copy-start(bf16[2,128,1024]{2,1,0:T(8,128)(2,1)} %get-tuple-element.839) | copy-start | bytes 1572868 | tf_op jit(solution)/shard_map/while
  613.7 15.4 %all-to-all-start.4 = ((bf16[8,40,1024]{2,1,0:T(8,128)(2,1)}), bf16[8,40,1024]{2,1,0:T(8,128)(2,1)S(1)}, u32[]{:S(2)}, u32[]{:S(2)}) async-start(bf16[8,40,1024]{2,1,0:T(8,128)(2,1)} %get-tuple-element.872), calls=%async_computation.4 | async-start | bytes 1310720 | tf_op jit(solution)/shard_map/while/body/eval_jaxpr/all_to_all | solution.py:202
  630.3 1.9 copy-start.4
  631.0 13.2 %copy-start.2 = (f32[2,128,2]{2,1,0:T(8,128)S(1)}, f32[2,128,2]{2,1,0:T(8,128)}, u32[]{:S(2)}) copy-start(f32[2,128,2]{2,1,0:T(8,128)} %copy-done.1) | copy-start | bytes 6148 | tf_op jit(solution)/shard_map/while
  633.4 10.7 %collective-permute-start.1 = (bf16[128,1024]{1,0:T(8,128)(2,1)S(1)}, bf16[128,1024]{1,0:T(8,128)(2,1)S(1)}, u32[]{:S(2)}, u32[]{:S(2)}) collective-permute-start(bf16[128,1024]{1,0:T(8,128)(2,1)S(1)} %get-tuple-element.770), channel_id=1, source_target_pairs={{8,0},{16,8},{24,16},{9,1},{17,9},{25,17},{10,2},{18,10},{26,18},{... | collective-permute-start | bytes 786440 | tf_op jit(solution)/shard_map/while/body/eval_jaxpr/ppermute | solution.py:15
  644.1 9.6 %copy-start.1 = (f32[2,128,2]{2,1,0:T(8,128)}, f32[2,128,2]{2,1,0:T(8,128)S(1)}, u32[]{:S(2)}) copy-start(f32[2,128,2]{2,1,0:T(8,128)S(1)} %get-tuple-element.863) | copy-start | bytes 6148 | tf_op jit(solution)/shard_map/while
  644.1 9.6 %copy-start.3 = (bf16[2,128,1024]{2,1,0:T(8,128)(2,1)S(1)}, bf16[2,128,1024]{2,1,0:T(8,128)(2,1)}, u32[]{:S(2)}) copy-start(bf16[2,128,1024]{2,1,0:T(8,128)(2,1)} %get-tuple-element.859) | copy-start | bytes 1572868 | tf_op jit(solution)/shard_map/while
  649.5 17.4 %all-to-all-start.3 = ((bf16[8,40,1024]{2,1,0:T(8,128)(2,1)}), bf16[8,40,1024]{2,1,0:T(8,128)(2,1)}, u32[]{:S(2)}, u32[]{:S(2)}) async-start(bf16[8,40,1024]{2,1,0:T(8,128)(2,1)} %bitcast.126), calls=%async_computation.3 | async-start | bytes 1310720 | tf_op jit(solution)/shard_map/while/body/eval_jaxpr/all_to_all | solution.py:198
  667.0 26.3 %all-to-all-start.2 = ((bf16[8,40,1024]{2,1,0:T(8,128)(2,1)}), bf16[8,40,1024]{2,1,0:T(8,128)(2,1)S(1)}, u32[]{:S(2)}, u32[]{:S(2)}) async-start(bf16[8,40,1024]{2,1,0:T(8,128)(2,1)} %bitcast.124), calls=%async_computation.2 | async-start | bytes 1310720 | tf_op jit(solution)/shard_map/while/body/eval_jaxpr/all_to_all | solution.py:199
  693.3 17.7 %copy-start = (bf16[2,128,1024]{2,1,0:T(8,128)(2,1)S(1)}, bf16[2,128,1024]{2,1,0:T(8,128)(2,1)}, u32[]{:S(2)}) copy-start(bf16[2,128,1024]{2,1,0:T(8,128)(2,1)} %get-tuple-element.839) | copy-start | bytes 1572868 | tf_op jit(solution)/shard_map/while
  707.3 15.3 %all-to-all-start.4 = ((bf16[8,40,1024]{2,1,0:T(8,128)(2,1)}), bf16[8,40,1024]{2,1,0:T(8,128)(2,1)S(1)}, u32[]{:S(2)}, u32[]{:S(2)}) async-start(bf16[8,40,1024]{2,1,0:T(8,128)(2,1)} %get-tuple-element.872), calls=%async_computation.4 | async-start | bytes 1310720 | tf_op jit(solution)/shard_map/while/body/eval_jaxpr/all_to_all | solution.py:202
  723.8 1.9 copy-start.4
  724.5 5.8 copy-start.2
  726.9 3.4 collective-permute-start.1
where the time goes:
time: 733 us; the launch traced here: 730 us
  waiting for transfers between devices  405 us (55%)
  starting transfers between devices  142 us (19%)
  local copies, waits for them, and re-layouts  79.2 us (11%)
  other arithmetic  58.7 us (8%)
  matrix products  42.7 us (6%)
    all_to_all x5, waiting for transfers between devices, forward_tick(): lax.all_to_all(send_buffer, 'expert', split_axis=0, concat_axis=0, tiled=...  76.8 us
    ppermute x10, waiting for transfers between devices, shifted(): return lax.ppermute(x, axis, pairs)  76.7 us
    all_to_all x5, waiting for transfers between devices, backward_tick(): lax.all_to_all(grad_send, 'expert', split_axis=0, concat_axis=0, tiled=True)  75.5 us
    all_to_all x5, waiting for transfers between devices, backward_tick(): lax.all_to_all(back_rows, 'expert', split_axis=0, concat_axis=0, tiled=True)  70.2 us
    all_to_all x5, waiting for transfers between devices, forward_tick(): lax.all_to_all(output_rows, 'expert', split_axis=0, concat_axis=0, tiled=...  68.4 us
    all_to_all x5, waiting for transfers between devices, backward_tick(): lax.all_to_all(row_send, 'expert', split_axis=0, concat_axis=0, tiled=True)  37.8 us
    ppermute x10, starting transfers between devices, shifted(): return lax.ppermute(x, axis, pairs)  30.3 us
    all_to_all x5, starting transfers between devices, backward_tick(): lax.all_to_all(grad_send, 'expert', split_axis=0, concat_axis=0, tiled=True)  25.7 us
  transfers between devices with their start and end apart: 35, of which 35 were waited for; matrix products, arithmetic and copies ran while one was open for 4% of the time, Pallas kernels for 0%

commit v1 on v0

v1 whole, which is shorter than its diff:
```python
import functools
import jax
import jax.numpy as jnp
from jax import lax
from jax.experimental import pallas as pl
from jax.experimental.pallas import tpu as pltpu
from jax.sharding import PartitionSpec as P

epsilon = 1e-05
gelu_coef = 0.7978845608028654
cubic_coef = 0.044715
contract_last = (((1,), (1,)), ((), ()))
f32 = jnp.float32
bf16 = jnp.bfloat16
vmem_spec = pl.BlockSpec(memory_space=pltpu.VMEM)
any_spec = pl.BlockSpec(memory_space=pl.ANY)


def gelu_parts(pre):
    square = pre * pre
    tangent = jnp.tanh(gelu_coef * pre * (1.0 + cubic_coef * square))
    half = 0.5 * (1.0 + tangent)
    slope = half + 0.5 * pre * (1.0 - tangent * tangent) * gelu_coef * (
        1.0 + 3.0 * cubic_coef * square
    )
    return pre * half, slope


def inverse_rms(values):
    return lax.rsqrt(jnp.mean(values * values, axis=-1, keepdims=True) + epsilon)


def normalize(values, gain_row):
    return (values * inverse_rms(values) * gain_row).astype(bf16)


def chip_index():
    return lax.axis_index("section") // 2


def core_index():
    return lax.axis_index("section") % 2


def unpack_pairs(returned, targets):
    rows, slots = targets.shape[0], returned.shape[0]
    lanes = lax.broadcasted_iota(jnp.int32, (rows, slots), 1)
    picked = []
    for k in range(2):
        chosen = (targets[:, k : k + 1] == lanes).astype(f32).astype(bf16)
        picked.append(jnp.dot(chosen, returned, preferred_element_type=f32))
    return picked


def slot_hits(targets_t, slots):
    rows = targets_t.shape[1]
    sublanes = lax.broadcasted_iota(jnp.int32, (slots, rows), 0)
    return [targets_t[k : k + 1, :] == sublanes for k in range(2)]


def pack_rows(rows, hits):
    chosen = jnp.where(hits[0] | hits[1], 1.0, 0.0).astype(bf16)
    return jnp.dot(chosen, rows, preferred_element_type=f32)


def slot_gates(hits, gates_t):
    total = jnp.where(hits[0], gates_t[0:1, :], 0.0) + jnp.where(hits[1], gates_t[1:2, :], 0.0)
    return jnp.sum(total, axis=1, keepdims=True)


def small_call(body, out_shapes, args):
    return pl.pallas_call(
        body,
        out_shape=out_shapes,
        in_specs=[vmem_spec] * len(args),
        out_specs=[vmem_spec] * len(out_shapes),
        compiler_params=pltpu.CompilerParams(vmem_limit_bytes=32 * 1024 * 1024),
    )(*args)


def shape_of(rows, columns, kind=bf16):
    return jax.ShapeDtypeStruct((rows, columns), kind)


def first_pack(state, gain, targets_t, grad, grad_targets_t, grad_gates_t, slots, last_chip):
    def body(state_ref, gain_ref, tt_ref, grad_ref, gtt_ref, ggt_ref, out_ref):
        is_last = chip_index() == last_chip

        @pl.when(is_last)
        def _():
            hits = slot_hits(gtt_ref[...], slots)
            out_ref[...] = (
                pack_rows(grad_ref[...], hits) * slot_gates(hits, ggt_ref[...])
            ).astype(bf16)

        @pl.when(jnp.logical_not(is_last))
        def _():
            normed = normalize(state_ref[...].astype(f32), gain_ref[...])
            out_ref[...] = pack_rows(normed, slot_hits(tt_ref[...], slots)).astype(bf16)

    return small_call(
        body,
        [shape_of(slots, state.shape[1])],
        (state, gain, targets_t, grad, grad_targets_t, grad_gates_t),
    )[0]


def select_pack(arrived, state, gain, targets_t, slots, chip):
    def body(arrived_ref, state_ref, gain_ref, tt_ref, state_out, out_ref):
        mine = chip_index() == chip

        @pl.when(mine)
        def _():
            state_out[...] = arrived_ref[...]

        @pl.when(jnp.logical_not(mine))
        def _():
            state_out[...] = state_ref[...]

        normed = normalize(state_out[...].astype(f32), gain_ref[...])
        out_ref[...] = pack_rows(normed, slot_hits(tt_ref[...], slots)).astype(bf16)

    return small_call(
        body,
        [shape_of(*state.shape), shape_of(slots, state.shape[1])],
        (arrived, state, gain, targets_t),
    )


def mix(returned, state, targets, gates):
    first, second = unpack_pairs(returned, targets)
    return (state.astype(f32) + (gates[:, 0:1] * first + gates[:, 1:2] * second)).astype(bf16)


def combine(returned, state, targets, gates):
    def body(ret_ref, state_ref, t_ref, g_ref, out_ref):
        out_ref[...] = mix(ret_ref[...], state_ref[...], t_ref[...], g_ref[...])

    return small_call(body, [shape_of(*state.shape)], (returned, state, targets, gates))[0]


def combine_pack(returned, state, targets, gates, gain, targets_t):
    slots = returned.shape[0]

    def body(ret_ref, state_ref, t_ref, g_ref, gain_ref, tt_ref, state_out, out_ref):
        mixed = mix(ret_ref[...], state_ref[...], t_ref[...], g_ref[...])
        state_out[...] = mixed
        normed = normalize(mixed.astype(f32), gain_ref[...])
        out_ref[...] = pack_rows(normed, slot_hits(tt_ref[...], slots)).astype(bf16)

    return small_call(
        body,
        [shape_of(*state.shape), shape_of(slots, state.shape[1])],
        (returned, state, targets, gates, gain, targets_t),
    )


def grad_mix(returned, upstream, state, targets, gain_row):
    first, second = unpack_pairs(returned, targets)
    values = state.astype(f32)
    inv_rms = inverse_rms(values)
    spread = (first + second) * gain_row
    along = jnp.mean(spread * values, axis=-1, keepdims=True)
    return (
        upstream.astype(f32) + inv_rms * spread - values * inv_rms * inv_rms * inv_rms * along
    ).astype(bf16)


def grad_combine(returned, upstream, state, targets, gain):
    def body(ret_ref, up_ref, state_ref, t_ref, gain_ref, out_ref):
        out_ref[...] = grad_mix(
            ret_ref[...], up_ref[...], state_ref[...], t_ref[...], gain_ref[...]
        )

    return small_call(
        body, [shape_of(*state.shape)], (returned, upstream, state, targets, gain)
    )[0]


def grad_combine_pack(returned, upstream, state, targets, gain, targets_t, gates_t):
    slots = returned.shape[0]

    def body(ret_ref, up_ref, state_ref, t_ref, gain_ref, tt_ref, gt_ref, grad_out, out_ref):
        mixed = grad_mix(ret_ref[...], up_ref[...], state_ref[...], t_ref[...], gain_ref[...])
        grad_out[...] = mixed
        hits = slot_hits(tt_ref[...], slots)
        out_ref[...] = (pack_rows(mixed, hits) * slot_gates(hits, gt_ref[...])).astype(bf16)

    return small_call(
        body,
        [shape_of(*state.shape), shape_of(slots, state.shape[1])],
        (returned, upstream, state, targets, gain, targets_t, gates_t),
    )


def grad_pack(upstream, targets_t, gates_t, slots):
    def body(up_ref, tt_ref, gt_ref, out_ref):
        hits = slot_hits(tt_ref[...], slots)
        out_ref[...] = (pack_rows(up_ref[...], hits) * slot_gates(hits, gt_ref[...])).astype(bf16)

    return small_call(body, [shape_of(slots, upstream.shape[1])], (upstream, targets_t, gates_t))[0]


def tile_width(hidden):
    return 512 if hidden % 512 == 0 else hidden


def weight_copies(parity, own_up, own_down, sib_up, sib_down, up_buf, down_buf, up_sem, down_sem):
    tiles, _, width = up_buf.shape
    own_layer = core_index() == parity

    def up_copy(source, i):
        return pltpu.make_async_copy(
            source.at[:, pl.ds(i * width, width)], up_buf.at[i], up_sem.at[i]
        )

    def down_copy(source, i):
        return pltpu.make_async_copy(
            source.at[pl.ds(i * width, width), :], down_buf.at[i], down_sem.at[i]
        )

    def start_all(up_source, down_source, down_first):
        for i in range(tiles):
            if down_first:
                down_copy(down_source, i).start()
                up_copy(up_source, i).start()
            else:
                up_copy(up_source, i).start()
                down_copy(down_source, i).start()

    def start(down_first):
        @pl.when(own_layer)
        def _():
            start_all(own_up, own_down, down_first)

        @pl.when(jnp.logical_not(own_layer))
        def _():
            start_all(sib_up, sib_down, down_first)

    return start, lambda i: up_copy(own_up, i).wait(), lambda i: down_copy(own_down, i).wait()


def mlp_scratch(features, hidden):
    width = tile_width(hidden)
    tiles = hidden // width
    return [
        pltpu.VMEM((tiles, features, width), bf16),
        pltpu.VMEM((tiles, width, features), bf16),
        pltpu.SemaphoreType.DMA((tiles,)),
        pltpu.SemaphoreType.DMA((tiles,)),
    ]


def mlp_call(body, out_shapes, out_specs, arrays, weights, scratch, flops, moved):
    return pl.pallas_call(
        body,
        out_shape=out_shapes,
        in_specs=[vmem_spec] * len(arrays) + [any_spec] * 4,
        out_specs=out_specs,
        scratch_shapes=scratch,
        compiler_params=pltpu.CompilerParams(vmem_limit_bytes=44 * 1024 * 1024),
        cost_estimate=pl.CostEstimate(flops=flops, bytes_accessed=moved, transcendentals=0),
    )(*arrays, *weights)


def expert_forward(rows, weights, parity, keep_slope):
    slots, features = rows.shape
    hidden = weights[0].shape[1]
    width = tile_width(hidden)
    tiles = hidden // width

    def body(x_ref, *refs):
        hbm, refs = refs[:4], refs[4:]
        if keep_slope:
            out_ref, slope_ref = refs[:2]
            up_buf, down_buf, up_sem, down_sem, acc = refs[2:]
        else:
            out_ref = refs[0]
            up_buf, down_buf, up_sem, down_sem, acc = refs[1:]
        start, wait_up, wait_down = weight_copies(
            parity, *hbm, up_buf, down_buf, up_sem, down_sem
        )
        start(False)
        for i in range(tiles):
            wait_up(i)
            pre = jnp.dot(x_ref[...], up_buf[i], preferred_element_type=f32)
            active, slope = gelu_parts(pre)
            if keep_slope:
                slope_ref[:, i * width : (i + 1) * width] = slope
            wait_down(i)
            part = jnp.dot(active.astype(bf16), down_buf[i], preferred_element_type=f32)
            if i == 0:
                acc[...] = part
            elif i < tiles - 1:
                acc[...] += part
            else:
                out_ref[...] = (acc[...] + part).astype(bf16)

    out_shapes = [shape_of(slots, features)]
    if keep_slope:
        out_shapes.append(shape_of(slots, hidden, f32))
    return mlp_call(
        body,
        out_shapes,
        [vmem_spec] * len(out_shapes),
        (rows,),
        weights,
        mlp_scratch(features, hidden) + [pltpu.VMEM((slots, features), f32)],
        4 * slots * features * hidden,
        4 * features * hidden + 4 * slots * features + 4 * slots * hidden * int(keep_slope),
    )


def expert_backward(grads, slope, weights, parity, other=None, other_chip=None):
    slots, features = grads.shape
    hidden = weights[0].shape[1]
    width = tile_width(hidden)
    tiles = hidden // width
    arrays = (grads, slope) if other is None else (grads, slope, other)

    def body(g_ref, slope_ref, *refs):
        if other is not None:
            other_ref, refs = refs[0], refs[1:]
        hbm, refs = refs[:4], refs[4:]
        out_ref, up_buf, down_buf, up_sem, down_sem, acc = refs
        start, wait_up, wait_down = weight_copies(
            parity, *hbm, up_buf, down_buf, up_sem, down_sem
        )
        start(True)
        for i in range(tiles):
            wait_down(i)
            act_grad = lax.dot_general(
                g_ref[...], down_buf[i], contract_last, preferred_element_type=f32
            )
            pre_grad = (act_grad * slope_ref[:, i * width : (i + 1) * width]).astype(bf16)
            wait_up(i)
            part = lax.dot_general(
                pre_grad, up_buf[i], contract_last, preferred_element_type=f32
            )
            if i == 0:
                acc[...] = part
            elif i < tiles - 1:
                acc[...] += part
            else:
                out_ref[...] = (acc[...] + part).astype(bf16)
        if other is not None:
            @pl.when(chip_index() == other_chip)
            def _():
                out_ref[...] = other_ref[...]

    return mlp_call(
        body,
        [shape_of(slots, features)],
        [vmem_spec],
        arrays,
        weights,
        mlp_scratch(features, hidden) + [pltpu.VMEM((slots, features), f32)],
        4 * slots * features * hidden,
        4 * features * hidden + 4 * slots * features + 4 * slots * hidden,
    )[0]


def act_gradient(grads, weights, parity):
    slots, features = grads.shape
    hidden = weights[0].shape[1]
    width = tile_width(hidden)
    tiles = hidden // width

    def body(g_ref, own_down, sib_down, out_ref, buf, sem):
        own_layer = core_index() == parity

        def copy(source, i):
            return pltpu.make_async_copy(
                source.at[pl.ds(i * width, width), :], buf.at[i], sem.at[i]
            )

        @pl.when(own_layer)
        def _():
            for i in range(tiles):
                copy(own_down, i).start()

        @pl.when(jnp.logical_not(own_layer))
        def _():
            for i in range(tiles):
                copy(sib_down, i).start()

        for i in range(tiles):
            copy(own_down, i).wait()
            out_ref[:, i * width : (i + 1) * width] = lax.dot_general(
                g_ref[...], buf[i], contract_last, preferred_element_type=f32
            )

    return pl.pallas_call(
        body,
        out_shape=shape_of(slots, hidden, f32),
        in_specs=[vmem_spec, any_spec, any_spec],
        out_specs=vmem_spec,
        scratch_shapes=[
            pltpu.VMEM((tiles, width, features), bf16),
            pltpu.SemaphoreType.DMA((tiles,)),
        ],
        compiler_params=pltpu.CompilerParams(vmem_limit_bytes=32 * 1024 * 1024),
        cost_estimate=pl.CostEstimate(
            flops=2 * slots * features * hidden,
            bytes_accessed=2 * features * hidden + 4 * slots * hidden,
            transcendentals=0,
        ),
    )(grads, weights[1], weights[3])


def turn_around(rows, act_grad, weights, parity):
    slots, features = rows.shape
    hidden = weights[0].shape[1]
    width = tile_width(hidden)
    tiles = hidden // width

    def body(x_ref, ag_ref, own_up, sib_up, out_ref, slope_ref, active_ref, buf, sem, acc):
        own_layer = core_index() == parity

        def copy(source, i):
            return pltpu.make_async_copy(
                source.at[:, pl.ds(i * width, width)], buf.at[i], sem.at[i]
            )

        @pl.when(own_layer)
        def _():
            for i in range(tiles):
                copy(own_up, i).start()

        @pl.when(jnp.logical_not(own_layer))
        def _():
            for i in range(tiles):
                copy(sib_up, i).start()

        for i in range(tiles):
            copy(own_up, i).wait()
            columns = slice(i * width, (i + 1) * width)
            pre = jnp.dot(x_ref[...], buf[i], preferred_element_type=f32)
            active, slope = gelu_parts(pre)
            slope_ref[:, columns] = slope
            active_ref[:, columns] = active.astype(bf16)
            pre_grad = (ag_ref[:, columns] * slope).astype(bf16)
            part = lax.dot_general(pre_grad, buf[i], contract_last, preferred_element_type=f32)
            if i == 0:
                acc[...] = part
            elif i < tiles - 1:
                acc[...] += part
            else:
                out_ref[...] = (acc[...] + part).astype(bf16)

    return pl.pallas_call(
        body,
        out_shape=[shape_of(slots, features), shape_of(slots, hidden, f32), shape_of(slots, hidden)],
        in_specs=[vmem_spec, vmem_spec, any_spec, any_spec],
        out_specs=[vmem_spec] * 3,
        scratch_shapes=[
            pltpu.VMEM((tiles, features, width), bf16),
            pltpu.SemaphoreType.DMA((tiles,)),
            pltpu.VMEM((slots, features), f32),
        ],
        compiler_params=pltpu.CompilerParams(vmem_limit_bytes=44 * 1024 * 1024),
        cost_estimate=pl.CostEstimate(
            flops=4 * slots * features * hidden,
            bytes_accessed=2 * features * hidden + 10 * slots * hidden,
            transcendentals=0,
        ),
    )(rows, act_grad, weights[0], weights[2])


def slot_targets(picks_t, experts, capacity):
    rows = picks_t.shape[1]
    onehot = (picks_t[:, :, None] == jnp.arange(experts, dtype=jnp.int32)[None, None, :])
    named = jnp.sum(onehot.astype(f32), axis=0).astype(bf16)
    at = jnp.arange(rows, dtype=jnp.int32)
    earlier = (at[None, :] < at[:, None]).astype(bf16)
    rank = jnp.dot(earlier, named, preferred_element_type=f32)
    rank_of_pick = jnp.sum(jnp.where(onehot, rank[None], 0.0), axis=2).astype(jnp.int32)
    return picks_t * capacity + rank_of_pick


def local(inputs, norm_gain, w_up, w_down, expert_ids, gates, out_grad):
    sections = lax.axis_size("section")
    experts = lax.axis_size("expert")
    chips = sections // 2
    last = chips - 1
    chip, core = chip_index(), core_index()
    batches, rows_dev, features = inputs.shape
    capacity = max(2, 5 * rows_dev // (2 * experts))
    slots = experts * capacity

    def swap_cores(x):
        return lax.ppermute(x, "section", [(s, s ^ 1) for s in range(sections)])

    def shift_chips(x, by):
        return lax.ppermute(
            x, "section", [(s, (s + 2 * by) % sections) for s in range(sections)]
        )

    def to_experts(x):
        return lax.all_to_all(x, "expert", split_axis=0, concat_axis=0, tiled=True)

    folds = features // rows_dev
    small = [
        jnp.concatenate(
            [
                expert_ids[0, m].T.astype(f32),
                gates[0, m].T,
                norm_gain[0].reshape(folds, rows_dev),
            ]
        )
        for m in range(2)
    ]
    own_small = jnp.where(core == 0, small[0], small[1])
    sib_small = swap_cores(jnp.where(core == 0, small[1], small[0]))
    params = []
    for parity in range(2):
        chosen = jnp.where(core == parity, own_small, sib_small)
        targets_t = slot_targets(chosen[:2].astype(jnp.int32), experts, capacity)
        gates_t = chosen[2:4]
        gain = chosen[4:].reshape(1, features)
        params.append((targets_t, targets_t.T, gates_t, gates_t.T, gain))
    (even_tt, even_t, even_gt, even_g, even_gain) = params[0]
    (odd_tt, odd_t, odd_gt, odd_g, odd_gain) = params[1]

    state = jnp.where(core == 0, inputs[0], inputs[1])
    last_grad = jnp.where(core == 0, out_grad[0], out_grad[1])
    own_up, own_down = w_up[0, 0], w_down[0, 0]
    weights = (own_up, own_down, swap_cores(own_up), swap_cores(own_down))

    send = first_pack(state, even_gain, even_tt, last_grad, odd_tt, odd_gt, slots, last)
    odd_out = None
    act_grad = None
    for turn in range(chips):
        if turn > 0:
            arrived = shift_chips(odd_out_now, 1)
            state, send = select_pack(arrived, state, even_gain, even_tt, slots, turn)
        received = to_experts(send)
        if turn < last:
            (outputs,) = expert_forward(received, weights, 0, False)
        else:
            outputs, even_slope = expert_forward(received, weights, 0, True)
        returned = to_experts(outputs)
        if turn == 0:
            act_grad = act_gradient(received, weights, 1)
        middle, send = combine_pack(returned, state, even_t, even_g, odd_gain, odd_tt)
        received = to_experts(send)
        if turn < last:
            (outputs,) = expert_forward(received, weights, 1, False)
            returned = to_experts(outputs)
            odd_out_now = combine(returned, middle, odd_t, odd_g)
            odd_out = (
                odd_out_now if odd_out is None else jnp.where(chip == turn, odd_out_now, odd_out)
            )

    back, odd_slope, odd_active = turn_around(received, act_grad, weights, 1)
    returned = to_experts(back)
    odd_down = jnp.dot(
        odd_active,
        jnp.where(core == 1, weights[1], weights[3]),
        preferred_element_type=f32,
    ).astype(bf16)
    upstream = last_grad
    even_grad = odd_grad = None
    for turn in range(last, -1, -1):
        if turn < last:
            upstream = shift_chips(even_now, -1)
            send = grad_pack(upstream, odd_tt, odd_gt, slots)
            received = to_experts(send)
            if turn == last - 1:
                back = expert_backward(received, odd_slope, weights, 1, odd_down, last)
            else:
                back = expert_backward(received, odd_slope, weights, 1)
            returned = to_experts(back)
            if turn == last - 1:
                final_out = combine(returned, middle, odd_t, odd_g)
                odd_out = jnp.where(chip == last, final_out, odd_out)
        odd_now, send = grad_combine_pack(
            returned, upstream, middle, odd_t, odd_gain, even_tt, even_gt
        )
        odd_grad = odd_now if odd_grad is None else jnp.where(chip == turn, odd_now, odd_grad)
        received = to_experts(send)
        back = expert_backward(received, even_slope, weights, 0)
        returned = to_experts(back)
        even_now = grad_combine(returned, odd_now, state, even_t, even_gain)
        even_grad = even_now if even_grad is None else jnp.where(chip == turn, even_now, even_grad)

    def gather_batches(even, odd):
        own = jnp.where(core == 0, even, odd)
        other = swap_cores(jnp.where(core == 0, odd, even))
        return jnp.where(core == 0, jnp.stack([own, other]), jnp.stack([other, own]))[None]

    return (gather_batches(middle, odd_out), gather_batches(even_grad, odd_grad))


def solution(mesh):
    return jax.shard_map(
        local,
        mesh=mesh,
        in_specs=(
            P(None, "expert", None),
            P("section", None),
            P("section", "expert", None, None),
            P("section", "expert", None, None),
            P("section", None, "expert", None),
            P("section", None, "expert", None),
            P(None, "expert", None),
        ),
        out_specs=(P("section", None, "expert", None), P("section", None, "expert", None)),
        check_vma=False,
    )
```

time: 733 us -> 393 us (0.54)
  waiting for transfers between devices: 405 us -> 79.3 us
  blocking collectives: 0 us -> 191 us
  starting transfers between devices: 142 us -> 23.3 us
  Pallas kernels: 0 us -> 52.8 us
  other arithmetic: 58.7 us -> 6.82 us
  local copies, waits for them, and re-layouts: 79.2 us -> 31.3 us
  matrix products: 42.7 us -> 6.49 us
    all_to_all x25 -> x5, waiting for transfers between devices: 329 us -> 65.6 us  [to_experts(): return lax.all_to_all(x, 'expert', split_axis=0, concat_axis=0, tiled=True)]
    all_to_all x0 -> x9, blocking collectives: none -> 191 us  [to_experts(): return lax.all_to_all(x, 'expert', split_axis=0, concat_axis=0, tiled=True)]
    all_to_all x25 -> x5, starting transfers between devices: 111 us -> 19.2 us  [to_experts(): return lax.all_to_all(x, 'expert', split_axis=0, concat_axis=0, tiled=True)]
    ppermute x10 -> x7, waiting for transfers between devices: 76.7 us -> 13.7 us  [the longest x2 10.1 us: shift_chips(): lax.ppermute(x, 'section', [(s, (s + 2 * by) % sections) for s in range(s...]
    pallas_call x0 -> x19, Pallas kernels: none -> 52.8 us  [the longest x6 34 us: mlp_call(): pl.pallas_call(body, out_shape=out_shapes, in_specs=[vmem_spec] * len(arr...]
    dot_general x6 -> x3, matrix products: 42.7 us -> 6.49 us  [the longest x1 6.22 us: local(): jnp.dot(odd_active, jnp.where(core == 1, weights[1], weights[3]), preferr...]
    unnamed x2 -> x92, local copies, waits for them, and re-layouts: 1.62 us -> 29.7 us
    ppermute x10 -> x7, starting transfers between devices: 30.3 us -> 4.1 us  [the longest x2 2.93 us: shift_chips(): lax.ppermute(x, 'section', [(s, (s + 2 * by) % sections) for s in range(s...]
  transfers between devices with their start and end apart: 35 -> 12, of which waited for: 35 -> 9; matrix products, arithmetic and copies ran while one was open for 4% -> 4% of each run, Pallas kernels for 0% -> 1%
where the time goes in v1:
time: 393 us; the launch traced here: 392 us
  blocking collectives  191 us (49%)
  waiting for transfers between devices  79.3 us (20%)
  Pallas kernels  52.8 us (13%)
  local copies, waits for them, and re-layouts  31.3 us (8%)
  starting transfers between devices  23.3 us (6%)
  other arithmetic  6.82 us (2%)
  matrix products  6.49 us (2%)
    all_to_all x9, blocking collectives, to_experts(): return lax.all_to_all(x, 'expert', split_axis=0, concat_axis=0, tiled=True)  191 us
    all_to_all x5, waiting for transfers between devices, to_experts(): return lax.all_to_all(x, 'expert', split_axis=0, concat_axis=0, tiled=True)  65.6 us
    pallas_call x6, Pallas kernels, mlp_call(): pl.pallas_call(body, out_shape=out_shapes, in_specs=[vmem_spec] * len(arr...  34 us
    unnamed x92, local copies, waits for them, and re-layouts  29.7 us
    all_to_all x5, starting transfers between devices, to_experts(): return lax.all_to_all(x, 'expert', split_axis=0, concat_axis=0, tiled=True)  19.2 us
    ppermute x2, waiting for transfers between devices, shift_chips(): lax.ppermute(x, 'section', [(s, (s + 2 * by) % sections) for s in range(s...  10.1 us
    pallas_call x11, Pallas kernels, small_call(): pl.pallas_call(body, out_shape=out_shapes, in_specs=[vmem_spec] * len(arg...  8.01 us
  transfers between devices with their start and end apart: 12, of which 9 were waited for; matrix products, arithmetic and copies ran while one was open for 4% of the time, Pallas kernels for 1%

profile of v1, /device:TPU:0, one launch (start us, length us, event | category | flops | bytes accessed | tf_op | source)
XLA Modules:
  0.0 391.9 jit_solution(17797628764965884336)
XLA Ops:
  1.2 0.7 convert_bitcast_fusion
  3.8 1.2 select_bitcast_fusion.2
  5.0 2.9 collective-permute-done
  8.0 0.7 broadcast_select_fusion.5
  10.8 25.0 %all_to_all.154 = bf16[8,40,1024]{2,1,0:T(8,128)(2,1)S(1)} all-to-all(bf16[8,40,1024]{2,1,0:T(8,128)(2,1)S(1)} %bitcast.104), channel_id=1, replica_groups=mesh['section'=4,'expert'=8] {'expert'}, dimensions={0} | all-to-all | bytes 1310720 | tf_op jit(solution)/shard_map/all_to_all | solution.py:500
  35.7 2.2 copy-done
  37.9 2.2 copy-done.5
  40.1 6.0 %shard_map.87 = bf16[320,1024]{1,0:T(8,128)(2,1)} custom-call(bf16[320,1024]{1,0:T(8,128)(2,1)S(1)} %bitcast.88, bf16[1024,2048]{1,0:T(8,128)(2,1)S(1)} %bitcast.74, bf16[2048,1024]{1,0:T(8,128)(2,1)S(1)} %bitcast.85, bf16[1024,2048]{1,0:T(8,128)(2,1)} %collective-permute-done.1.refs_2_.sib_up.refs_3_, ...), custom_call_target="tpu_custom_call" | custom-call | flops 2684354560 | bytes 9699328 | tf_op jit(solution)/shard_map/pallas_call | solution.py:255
  46.2 3.6 all-to-all-start.1
  49.9 17.0 %all-to-all-done.1 = bf16[8,40,1024]{2,1,0:T(8,128)(2,1)S(1)} async-done(((bf16[8,40,1024]{2,1,0:T(8,128)(2,1)}), bf16[8,40,1024]{2,1,0:T(8,128)(2,1)S(1)}, u32[]{:S(2)}, u32[]{:S(2)}) %all-to-all-start.1) | async-done | bytes 655392 | tf_op jit(solution)/shard_map/all_to_all | solution.py:500
  66.8 0.9 shard_map.88
  67.8 21.3 %all_to_all.155 = bf16[8,40,1024]{2,1,0:T(8,128)(2,1)S(1)} all-to-all(bf16[8,40,1024]{2,1,0:T(8,128)(2,1)S(1)} %bitcast.120), channel_id=1, replica_groups=mesh['section'=4,'expert'=8] {'expert'}, dimensions={0} | all-to-all | bytes 1310720 | tf_op jit(solution)/shard_map/all_to_all | solution.py:500
  89.1 2.2 copy-done.1
  91.2 2.2 copy-done.6
  93.4 6.3 %shard_map.89 = bf16[320,1024]{1,0:T(8,128)(2,1)} custom-call(bf16[320,1024]{1,0:T(8,128)(2,1)S(1)} %bitcast.96, bf16[1024,2048]{1,0:T(8,128)(2,1)S(1)} %bitcast.75, bf16[2048,1024]{1,0:T(8,128)(2,1)S(1)} %bitcast.86, bf16[1024,2048]{1,0:T(8,128)(2,1)} %collective-permute-done.1.refs_2_.sib_up.refs_3_, ...), custom_call_target="tpu_custom_call" | custom-call | flops 2684354560 | bytes 9699328 | tf_op jit(solution)/shard_map/pallas_call | solution.py:255
  99.8 3.6 all-to-all-start.3
  103.4 16.5 %all-to-all-done.3 = bf16[8,40,1024]{2,1,0:T(8,128)(2,1)S(1)} async-done(((bf16[8,40,1024]{2,1,0:T(8,128)(2,1)}), bf16[8,40,1024]{2,1,0:T(8,128)(2,1)S(1)}, u32[]{:S(2)}, u32[]{:S(2)}) %all-to-all-start.3) | async-done | bytes 655392 | tf_op jit(solution)/shard_map/all_to_all | solution.py:500
  120.4 1.5 collective-permute-start.3
  121.9 5.0 %collective-permute-done.3.arrived_ref = bf16[128,1024]{1,0:T(8,128)(2,1)S(1)} collective-permute-done((bf16[128,1024]{1,0:T(8,128)(2,1)S(1)}, bf16[128,1024]{1,0:T(8,128)(2,1)S(1)}, u32[]{:S(2)}, u32[]{:S(2)}) %collective-permute-start.3) | collective-permute-done | bytes 262176 | tf_op jit(solution)/shard_map/ppermute | solution.py:495
  127.3 22.0 %all_to_all.156 = bf16[8,40,1024]{2,1,0:T(8,128)(2,1)S(1)} all-to-all(bf16[8,40,1024]{2,1,0:T(8,128)(2,1)S(1)} %bitcast.118), channel_id=1, replica_groups=mesh['section'=4,'expert'=8] {'expert'}, dimensions={0} | all-to-all | bytes 1310720 | tf_op jit(solution)/shard_map/all_to_all | solution.py:500
  149.3 2.2 copy-done.2
  151.5 5.8 %shard_map.92 = (bf16[320,1024]{1,0:T(8,128)(2,1)S(1)}, f32[320,2048]{1,0:T(8,128)S(1)}) custom-call(bf16[320,1024]{1,0:T(8,128)(2,1)S(1)} %bitcast.94, bf16[1024,2048]{1,0:T(8,128)(2,1)S(1)} %bitcast.76, bf16[2048,1024]{1,0:T(8,128)(2,1)} %bitcast.81, bf16[1024,2048]{1,0:T(8,128)(2,1)} %collective-permute-done.1.refs_2_.sib_up.refs_3_, ...), custom_call_target="tpu_custom_call" | custom-call | flops 2684354560 | bytes 12320768 | tf_op jit(solution)/shard_map/pallas_call | solution.py:255
  157.4 20.7 %all_to_all.157 = bf16[8,40,1024]{2,1,0:T(8,128)(2,1)S(1)} all-to-all(bf16[8,40,1024]{2,1,0:T(8,128)(2,1)S(1)} %bitcast.121), channel_id=1, replica_groups=mesh['section'=4,'expert'=8] {'expert'}, dimensions={0} | all-to-all | bytes 1310720 | tf_op jit(solution)/shard_map/all_to_all | solution.py:500
  178.0 0.9 shard_map.93
  179.0 0.9 copy-done.35
  179.8 4.2 %all-to-all-start.6 = ((bf16[8,40,1024]{2,1,0:T(8,128)(2,1)}), bf16[8,40,1024]{2,1,0:T(8,128)(2,1)}, u32[]{:S(2)}, u32[]{:S(2)}) async-start(bf16[8,40,1024]{2,1,0:T(8,128)(2,1)} %bitcast.115), calls=%async_computation.6 | async-start | bytes 1310720 | tf_op jit(solution)/shard_map/all_to_all | solution.py:500
  184.1 2.2 copy-done.7
  186.2 3.4 shard_map.94.ag_ref
  189.7 1.5 copy-done.8
  191.1 9.1 %all-to-all-done.6 = bf16[8,40,1024]{2,1,0:T(8,128)(2,1)} async-done(((bf16[8,40,1024]{2,1,0:T(8,128)(2,1)}), bf16[8,40,1024]{2,1,0:T(8,128)(2,1)}, u32[]{:S(2)}, u32[]{:S(2)}) %all-to-all-start.6) | async-done | bytes 655392 | tf_op jit(solution)/shard_map/all_to_all | solution.py:500
  200.3 1.7 copy-done.9
  202.0 7.4 %shard_map.95 = (bf16[320,1024]{1,0:T(8,128)(2,1)S(1)}, f32[320,2048]{1,0:T(8,128)S(1)}, bf16[320,2048]{1,0:T(8,128)(2,1)S(1)}) custom-call(bf16[320,1024]{1,0:T(8,128)(2,1)} %bitcast.32.x_ref, f32[320,2048]{1,0:T(8,128)S(1)} %copy-done.9, bf16[1024,2048]{1,0:T(8,128)(2,1)} %bitcast.73, bf16[1024,2048]{1,0:T(8,128)(2,1)} %collective-permute-done.1.refs_2_.sib_up.refs_3_), custom_call_target="tpu_custom_call" | custom-call | flops 2684354560 | bytes 10747904 | tf_op jit(solution)/shard_map/pallas_call | solution.py:451
  209.4 1.5 copy-done.11
  210.9 20.6 %all_to_all.158 = bf16[8,40,1024]{2,1,0:T(8,128)(2,1)S(1)} all-to-all(bf16[8,40,1024]{2,1,0:T(8,128)(2,1)S(1)} %bitcast.117), channel_id=1, replica_groups=mesh['section'=4,'expert'=8] {'expert'}, dimensions={0} | all-to-all | bytes 1310720 | tf_op jit(solution)/shard_map/all_to_all | solution.py:500
  231.5 0.9 shard_map.96
  232.5 20.2 %all_to_all.159 = bf16[8,40,1024]{2,1,0:T(8,128)(2,1)S(1)} all-to-all(bf16[8,40,1024]{2,1,0:T(8,128)(2,1)S(1)} %bitcast.119), channel_id=1, replica_groups=mesh['section'=4,'expert'=8] {'expert'}, dimensions={0} | all-to-all | bytes 1310720 | tf_op jit(solution)/shard_map/all_to_all | solution.py:500
  252.7 5.3 %shard_map.97 = bf16[320,1024]{1,0:T(8,128)(2,1)S(1)} custom-call(bf16[320,1024]{1,0:T(8,128)(2,1)S(1)} %bitcast.95, f32[320,2048]{1,0:T(8,128)S(1)} %get-tuple-element.26.slope_ref, bf16[1024,2048]{1,0:T(8,128)(2,1)S(1)} %bitcast.77, bf16[2048,1024]{1,0:T(8,128)(2,1)} %bitcast.82, bf16[1024,2048]{1,0:T(8,128)(2,1)} %collective-permute-done.1.refs_2_.sib_up.refs_3_, ...), custom_call_target="tpu_custom_call" | custom-call | flops 2684354560 | bytes 12320768 | tf_op jit(solution)/shard_map/pallas_call | solution.py:255
  258.1 20.4 %all_to_all.160 = bf16[8,40,1024]{2,1,0:T(8,128)(2,1)S(1)} all-to-all(bf16[8,40,1024]{2,1,0:T(8,128)(2,1)S(1)} %bitcast.97), channel_id=1, replica_groups=mesh['section'=4,'expert'=8] {'expert'}, dimensions={0} | all-to-all | bytes 1310720 | tf_op jit(solution)/shard_map/all_to_all | solution.py:500
  279.1 1.5 collective-permute-start.4
  280.6 5.1 %collective-permute-done.4.up_ref = bf16[128,1024]{1,0:T(8,128)(2,1)S(1)} collective-permute-done((bf16[128,1024]{1,0:T(8,128)(2,1)S(1)}, bf16[128,1024]{1,0:T(8,128)(2,1)S(1)}, u32[]{:S(2)}, u32[]{:S(2)}) %collective-permute-start.4) | collective-permute-done | bytes 262176 | tf_op jit(solution)/shard_map/ppermute | solution.py:495
  285.7 1.2 shard_map.99
  286.9 0.7 copy-done.26
  287.6 4.3 %all-to-all-start.10 = ((bf16[8,40,1024]{2,1,0:T(8,128)(2,1)}), bf16[8,40,1024]{2,1,0:T(8,128)(2,1)S(1)}, u32[]{:S(2)}, u32[]{:S(2)}) async-start(bf16[8,40,1024]{2,1,0:T(8,128)(2,1)} %bitcast.39), calls=%async_computation.10 | async-start | bytes 1310720 | tf_op jit(solution)/shard_map/all_to_all | solution.py:500
  291.9 6.2 %fusion.3.refs_0_ = bf16[320,1024]{1,0:T(8,128)(2,1)} fusion(bf16[320,2048]{1,0:T(8,128)(2,1)} %copy-done.45, bf16[2048,1024]{1,0:T(8,128)(2,1)} %collective-permute-done.2.refs_3_.sib_down.refs_4_, pred[]{:T(512)S(6)} %eq.26, bf16[1,1,2048,1024]{3,2,1,0:T(8,128)(2,1)} %param.10), kind=kOutput, calls=%fused_computation.3 | convolution fusion | flops 1344602112 | bytes 10354689 | tf_op jit(solution)/shard_map/dot_general | solution.py:557
  298.1 9.7 %all-to-all-done.10 = bf16[8,40,1024]{2,1,0:T(8,128)(2,1)S(1)} async-done(((bf16[8,40,1024]{2,1,0:T(8,128)(2,1)}), bf16[8,40,1024]{2,1,0:T(8,128)(2,1)S(1)}, u32[]{:S(2)}, u32[]{:S(2)}) %all-to-all-start.10) | async-done | bytes 655392 | tf_op jit(solution)/shard_map/all_to_all | solution.py:500
  307.8 2.2 copy-done.4
  310.0 1.7 copy-done.12
  311.8 1.1 copy-done.36
  312.8 5.3 %shard_map.100 = bf16[320,1024]{1,0:T(8,128)(2,1)S(1)} custom-call(bf16[320,1024]{1,0:T(8,128)(2,1)S(1)} %bitcast.105, f32[320,2048]{1,0:T(8,128)S(1)} %copy-done.12, bf16[320,1024]{1,0:T(8,128)(2,1)S(1)} %copy-done.36, bf16[1024,2048]{1,0:T(8,128)(2,1)S(1)} %bitcast.78, bf16[2048,1024]{1,0:T(8,128)(2,1)} %bitcast.83, ...), custom_call_target="tpu_custom_call" | custom-call | flops 2684354560 | bytes 12320768 | tf_op jit(solution)/shard_map/pallas_call | solution.py:255
  318.1 20.2 %all_to_all.161 = bf16[8,40,1024]{2,1,0:T(8,128)(2,1)S(1)} all-to-all(bf16[8,40,1024]{2,1,0:T(8,128)(2,1)S(1)} %bitcast.106), channel_id=1, replica_groups=mesh['section'=4,'expert'=8] {'expert'}, dimensions={0} | all-to-all | bytes 1310720 | tf_op jit(solution)/shard_map/all_to_all | solution.py:500
  338.4 0.9 shard_map.102
  339.3 20.3 %all_to_all.162 = bf16[8,40,1024]{2,1,0:T(8,128)(2,1)S(1)} all-to-all(bf16[8,40,1024]{2,1,0:T(8,128)(2,1)S(1)} %bitcast.116), channel_id=1, replica_groups=mesh['section'=4,'expert'=8] {'expert'}, dimensions={0} | all-to-all | bytes 1310720 | tf_op jit(solution)/shard_map/all_to_all | solution.py:500
  359.6 5.3 %shard_map.103 = bf16[320,1024]{1,0:T(8,128)(2,1)S(1)} custom-call(bf16[320,1024]{1,0:T(8,128)(2,1)S(1)} %bitcast.93, f32[320,2048]{1,0:T(8,128)S(1)} %get-tuple-element.26.slope_ref, bf16[1024,2048]{1,0:T(8,128)(2,1)S(1)} %bitcast.79, bf16[2048,1024]{1,0:T(8,128)(2,1)} %bitcast.84, bf16[1024,2048]{1,0:T(8,128)(2,1)} %collective-permute-done.1.refs_2_.sib_up.refs_3_, ...), custom_call_target="tpu_custom_call" | custom-call | flops 2684354560 | bytes 12320768 | tf_op jit(solution)/shard_map/pallas_call | solution.py:255
  364.9 0.9 copy-done.10
  365.8 3.7 all-to-all-start.13
  369.5 0.8 copy-done.20
  370.3 0.8 copy-done.38
  371.6 1.0 select_bitcast_fusion.1
  372.7 13.2 %all-to-all-done.13 = bf16[8,40,1024]{2,1,0:T(8,128)(2,1)S(1)} async-done(((bf16[8,40,1024]{2,1,0:T(8,128)(2,1)}), bf16[8,40,1024]{2,1,0:T(8,128)(2,1)S(1)}, u32[]{:S(2)}, u32[]{:S(2)}) %all-to-all-start.13) | async-done | bytes 655392 | tf_op jit(solution)/shard_map/all_to_all | solution.py:500
  386.0 0.8 copy-done.16
  386.8 0.9 copy-done.25
  387.8 0.9 copy-done.34
  389.5 0.9 maximum_select_fusion
  391.0 0.9 maximum_select_fusion.1
  (112 shorter events, 8.3 us)
Async XLA Ops:
  0.6 35.1 %collective-permute-start.1 = (bf16[1024,2048]{1,0:T(8,128)(2,1)}, bf16[1024,2048]{1,0:T(8,128)(2,1)}, u32[]{:S(2)}, u32[]{:S(2)}) collective-permute-start(bf16[1024,2048]{1,0:T(8,128)(2,1)} %bitcast.72), channel_id=1, source_target_pairs={{0,8},{8,0},{16,24},{24,16},{1,9},{9,1},{17,25},{25,17},{2,10},{10... | collective-permute-start | bytes 12582920 | tf_op jit(solution)/shard_map/ppermute | solution.py:492
  1.1 34.6 %collective-permute-start.2 = (bf16[2048,1024]{1,0:T(8,128)(2,1)}, bf16[2048,1024]{1,0:T(8,128)(2,1)}, u32[]{:S(2)}, u32[]{:S(2)}) collective-permute-start(bf16[2048,1024]{1,0:T(8,128)(2,1)} %bitcast.80), channel_id=1, source_target_pairs={{0,8},{8,0},{16,24},{24,16},{1,9},{9,1},{17,25},{25,17},{2,10},{10... | collective-permute-start | bytes 12582920 | tf_op jit(solution)/shard_map/ppermute | solution.py:492
  3.3 4.6 %collective-permute-start = (f32[12,128]{1,0:T(8,128)S(1)}, f32[12,128]{1,0:T(8,128)S(1)}, u32[]{:S(2)}, u32[]{:S(2)}) collective-permute-start(f32[12,128]{1,0:T(8,128)S(1)} %fusion.8), channel_id=1, source_target_pairs={{0,8},{8,0},{16,24},{24,16},{1,9},{9,1},{17,25},{25,17},{2,10},{10... | collective-permute-start | bytes 18440 | tf_op jit(solution)/shard_map/ppermute | solution.py:492
  5.0 30.7 %copy-start.21 = (bf16[128,1024]{1,0:T(8,128)(2,1)}, bf16[128,1024]{1,0:T(8,128)(2,1)S(1)}, u32[]{:S(2)}) copy-start(bf16[128,1024]{1,0:T(8,128)(2,1)S(1)} %get-tuple-element.48.grad_ref.up_ref) | copy-start | bytes 786436
  9.3 36.9 %copy-start.43 = (f32[2,128]{1,0:T(2,128)}, f32[2,128]{1,0:T(2,128)S(1)}, u32[]{:S(2)}) copy-start(f32[2,128]{1,0:T(2,128)S(1)} %get-tuple-element.42.ggt_ref.gt_ref) | copy-start | bytes 3076
  10.0 109.9 %copy-start.17 = (s32[2,128]{0,1:T(8,128)}, s32[2,128]{0,1:T(8,128)S(1)}, u32[]{:S(2)}) copy-start(s32[2,128]{0,1:T(8,128)S(1)} %add.13) | copy-start | bytes 3076
  10.2 56.6 %copy-start.13 = (s32[2,128]{0,1:T(8,128)}, s32[2,128]{0,1:T(8,128)S(1)}, u32[]{:S(2)}) copy-start(s32[2,128]{0,1:T(8,128)S(1)} %add.12) | copy-start | bytes 3076
  35.7 2.2 copy-start
  37.9 2.2 copy-start.5
  46.2 20.7 %all-to-all-start.1 = ((bf16[8,40,1024]{2,1,0:T(8,128)(2,1)}), bf16[8,40,1024]{2,1,0:T(8,128)(2,1)S(1)}, u32[]{:S(2)}, u32[]{:S(2)}) async-start(bf16[8,40,1024]{2,1,0:T(8,128)(2,1)} %bitcast.16), calls=%async_computation.1 | async-start | bytes 1310720 | tf_op jit(solution)/shard_map/all_to_all | solution.py:500
  49.8 49.9 %copy-start.39 = (f32[128,2]{1,0:T(8,128)}, f32[128,2]{1,0:T(8,128)S(1)}, u32[]{:S(2)}) copy-start(f32[128,2]{1,0:T(8,128)S(1)} %copy.106.g_ref) | copy-start | bytes 3076
  89.1 2.2 copy-start.1
  91.2 2.2 copy-start.6
  99.8 20.2 %all-to-all-start.3 = ((bf16[8,40,1024]{2,1,0:T(8,128)(2,1)}), bf16[8,40,1024]{2,1,0:T(8,128)(2,1)S(1)}, u32[]{:S(2)}, u32[]{:S(2)}) async-start(bf16[8,40,1024]{2,1,0:T(8,128)(2,1)} %bitcast.23), calls=%async_computation.3 | async-start | bytes 1310720 | tf_op jit(solution)/shard_map/all_to_all | solution.py:500
  103.4 45.9 %copy-start.37 = (f32[128,2]{1,0:T(8,128)}, f32[128,2]{1,0:T(8,128)S(1)}, u32[]{:S(2)}) copy-start(f32[128,2]{1,0:T(8,128)S(1)} %copy.108.g_ref) | copy-start | bytes 3076
  120.4 28.9 %copy-start.28 = (bf16[128,1024]{1,0:T(8,128)(2,1)}, bf16[128,1024]{1,0:T(8,128)(2,1)S(1)}, u32[]{:S(2)}) copy-start(bf16[128,1024]{1,0:T(8,128)(2,1)S(1)} %shard_map.90) | copy-start | bytes 786436
  120.4 6.4 %collective-permute-start.3 = (bf16[128,1024]{1,0:T(8,128)(2,1)S(1)}, bf16[128,1024]{1,0:T(8,128)(2,1)S(1)}, u32[]{:S(2)}, u32[]{:S(2)}) collective-permute-start(bf16[128,1024]{1,0:T(8,128)(2,1)S(1)} %shard_map.90), channel_id=1, source_target_pairs={{0,16},{8,24},{16,0},{24,8},{1,17},{9,25},{17,1},{25,9},{2,18},{10... | collective-permute-start | bytes 786440 | tf_op jit(solution)/shard_map/ppermute | solution.py:495
  127.3 50.7 %copy-start.23 = (bf16[128,1024]{1,0:T(8,128)(2,1)}, bf16[128,1024]{1,0:T(8,128)(2,1)S(1)}, u32[]{:S(2)}) copy-start(bf16[128,1024]{1,0:T(8,128)(2,1)S(1)} %get-tuple-element.21.state_ref) | copy-start | bytes 786436
  149.3 2.2 copy-start.2
  151.5 26.5 %copy-start.14 = (s32[2,128]{0,1:T(8,128)S(1)}, s32[2,128]{0,1:T(8,128)}, u32[]{:S(2)}) copy-start(s32[2,128]{0,1:T(8,128)} %copy-done.13) | copy-start | bytes 3076
  151.5 26.5 %copy-start.40 = (f32[128,2]{1,0:T(8,128)S(1)}, f32[128,2]{1,0:T(8,128)}, u32[]{:S(2)}) copy-start(f32[128,2]{1,0:T(8,128)} %copy-done.39) | copy-start | bytes 3076
  179.0 0.9 copy-start.35
  179.8 20.4 %all-to-all-start.6 = ((bf16[8,40,1024]{2,1,0:T(8,128)(2,1)}), bf16[8,40,1024]{2,1,0:T(8,128)(2,1)}, u32[]{:S(2)}, u32[]{:S(2)}) async-start(bf16[8,40,1024]{2,1,0:T(8,128)(2,1)} %bitcast.115), calls=%async_computation.6 | async-start | bytes 1310720 | tf_op jit(solution)/shard_map/all_to_all | solution.py:500
  184.0 2.2 copy-start.7
  189.7 1.5 copy-start.8
  200.3 1.7 copy-start.9
  202.0 29.5 %copy-start.18 = (s32[2,128]{0,1:T(8,128)S(1)}, s32[2,128]{0,1:T(8,128)}, u32[]{:S(2)}) copy-start(s32[2,128]{0,1:T(8,128)} %copy-done.17) | copy-start | bytes 3076
  202.0 29.5 %copy-start.22 = (bf16[128,1024]{1,0:T(8,128)(2,1)S(1)}, bf16[128,1024]{1,0:T(8,128)(2,1)}, u32[]{:S(2)}) copy-start(bf16[128,1024]{1,0:T(8,128)(2,1)} %copy-done.21) | copy-start | bytes 786436
  202.0 29.5 %copy-start.41 = (f32[2,128]{1,0:T(2,128)S(1)}, f32[2,128]{1,0:T(2,128)}, u32[]{:S(2)}) copy-start(f32[2,128]{1,0:T(2,128)} %get-tuple-element.54.gt_ref) | copy-start | bytes 3076
  202.0 50.7 %copy-start.3 = (bf16[1,1,1024,2048]{3,2,1,0:T(8,128)(2,1)S(1)}, bf16[1,1,1024,2048]{3,2,1,0:T(8,128)(2,1)}, u32[]{:S(2)}) copy-start(bf16[1,1,1024,2048]{3,2,1,0:T(8,128)(2,1)} %param.9) | copy-start | bytes 12582916
  209.4 1.5 copy-start.11
  210.9 47.2 %copy-start.45 = (bf16[320,2048]{1,0:T(8,128)(2,1)}, bf16[320,2048]{1,0:T(8,128)(2,1)S(1)}, u32[]{:S(2)}) copy-start(bf16[320,2048]{1,0:T(8,128)(2,1)S(1)} %get-tuple-element.29) | copy-start | bytes 3932164
  232.5 46.0 %copy-start.29 = (bf16[128,1024]{1,0:T(8,128)(2,1)}, bf16[128,1024]{1,0:T(8,128)(2,1)S(1)}, u32[]{:S(2)}) copy-start(bf16[128,1024]{1,0:T(8,128)(2,1)S(1)} %get-tuple-element.27.up_ref) | copy-start | bytes 786436
  252.7 25.8 %copy-start.15 = (s32[2,128]{0,1:T(8,128)S(1)}, s32[2,128]{0,1:T(8,128)}, u32[]{:S(2)}) copy-start(s32[2,128]{0,1:T(8,128)} %copy-done.13) | copy-start | bytes 3076
  252.7 25.8 %copy-start.24 = (bf16[128,1024]{1,0:T(8,128)(2,1)S(1)}, bf16[128,1024]{1,0:T(8,128)(2,1)}, u32[]{:S(2)}) copy-start(bf16[128,1024]{1,0:T(8,128)(2,1)} %copy-done.23) | copy-start | bytes 786436
  252.7 33.0 %copy-start.44 = (f32[2,128]{1,0:T(2,128)S(1)}, f32[2,128]{1,0:T(2,128)}, u32[]{:S(2)}) copy-start(f32[2,128]{1,0:T(2,128)} %copy-done.43) | copy-start | bytes 3076
  279.1 7.8 %copy-start.31 = (bf16[128,1024]{1,0:T(8,128)(2,1)}, bf16[128,1024]{1,0:T(8,128)(2,1)S(1)}, u32[]{:S(2)}) copy-start(bf16[128,1024]{1,0:T(8,128)(2,1)S(1)} %shard_map.98) | copy-start | bytes 786436
  279.1 6.6 %collective-permute-start.4 = (bf16[128,1024]{1,0:T(8,128)(2,1)S(1)}, bf16[128,1024]{1,0:T(8,128)(2,1)S(1)}, u32[]{:S(2)}, u32[]{:S(2)}) collective-permute-start(bf16[128,1024]{1,0:T(8,128)(2,1)S(1)} %shard_map.98), channel_id=1, source_target_pairs={{0,16},{8,24},{16,0},{24,8},{1,17},{9,25},{17,1},{25,9},{2,18},{10... | collective-permute-start | bytes 786440 | tf_op jit(solution)/shard_map/ppermute | solution.py:495
  286.9 0.7 copy-start.26
  287.6 20.2 %all-to-all-start.10 = ((bf16[8,40,1024]{2,1,0:T(8,128)(2,1)}), bf16[8,40,1024]{2,1,0:T(8,128)(2,1)S(1)}, u32[]{:S(2)}, u32[]{:S(2)}) async-start(bf16[8,40,1024]{2,1,0:T(8,128)(2,1)} %bitcast.39), calls=%async_computation.10 | async-start | bytes 1310720 | tf_op jit(solution)/shard_map/all_to_all | solution.py:500
  307.8 2.2 copy-start.4
  310.0 1.7 copy-start.12
  311.8 1.1 copy-start.36
  312.8 25.5 %copy-start.19 = (s32[2,128]{0,1:T(8,128)S(1)}, s32[2,128]{0,1:T(8,128)}, u32[]{:S(2)}) copy-start(s32[2,128]{0,1:T(8,128)} %copy-done.17) | copy-start | bytes 3076
  312.8 25.5 %copy-start.27 = (bf16[128,1024]{1,0:T(8,128)(2,1)S(1)}, bf16[128,1024]{1,0:T(8,128)(2,1)}, u32[]{:S(2)}) copy-start(bf16[128,1024]{1,0:T(8,128)(2,1)} %copy-done.26) | copy-start | bytes 786436
  312.8 25.5 %copy-start.42 = (f32[2,128]{1,0:T(2,128)S(1)}, f32[2,128]{1,0:T(2,128)}, u32[]{:S(2)}) copy-start(f32[2,128]{1,0:T(2,128)} %get-tuple-element.54.gt_ref) | copy-start | bytes 3076
  339.3 20.3 %copy-start.33 = (bf16[128,1024]{1,0:T(8,128)(2,1)}, bf16[128,1024]{1,0:T(8,128)(2,1)S(1)}, u32[]{:S(2)}) copy-start(bf16[128,1024]{1,0:T(8,128)(2,1)S(1)} %get-tuple-element.31.up_ref) | copy-start | bytes 786436
  364.9 0.9 copy-start.10
  365.8 23.6 %copy-start.30 = (bf16[128,1024]{1,0:T(8,128)(2,1)S(1)}, bf16[128,1024]{1,0:T(8,128)(2,1)}, u32[]{:S(2)}) copy-start(bf16[128,1024]{1,0:T(8,128)(2,1)} %copy-done.29) | copy-start | bytes 786436
  365.8 23.6 %copy-start.32 = (bf16[128,1024]{1,0:T(8,128)(2,1)S(1)}, bf16[128,1024]{1,0:T(8,128)(2,1)}, u32[]{:S(2)}) copy-start(bf16[128,1024]{1,0:T(8,128)(2,1)} %copy-done.31) | copy-start | bytes 786436
  365.8 20.2 %all-to-all-start.13 = ((bf16[8,40,1024]{2,1,0:T(8,128)(2,1)}), bf16[8,40,1024]{2,1,0:T(8,128)(2,1)S(1)}, u32[]{:S(2)}, u32[]{:S(2)}) async-start(bf16[8,40,1024]{2,1,0:T(8,128)(2,1)} %bitcast.92), calls=%async_computation.13 | async-start | bytes 1310720 | tf_op jit(solution)/shard_map/all_to_all | solution.py:500
  369.5 0.8 copy-start.20
  370.3 0.8 copy-start.38
  372.6 16.8 %collective-permute-start.5 = (bf16[128,1024]{1,0:T(8,128)(2,1)S(1)}, bf16[128,1024]{1,0:T(8,128)(2,1)S(1)}, u32[]{:S(2)}, u32[]{:S(2)}) collective-permute-start(bf16[128,1024]{1,0:T(8,128)(2,1)S(1)} %get-tuple-element.35), channel_id=1, source_target_pairs={{0,8},{8,0},{16,24},{24,16},{1,9},{9,1},{17,25},{25,17},{2,10},{10... | collective-permute-start | bytes 786440 | tf_op jit(solution)/shard_map/ppermute | solution.py:492
  386.0 0.8 copy-start.16
  386.8 0.9 copy-start.25
  387.8 0.9 copy-start.34
  389.4 1.6 collective-permute-start.6

commit v2 on v1

--- a/solution.py
+++ b/solution.py
@@ -1,4 +1,3 @@
-import functools
 import jax
 import jax.numpy as jnp
 from jax import lax
@@ -14,6 +13,11 @@
 bf16 = jnp.bfloat16
 vmem_spec = pl.BlockSpec(memory_space=pltpu.VMEM)
 any_spec = pl.BlockSpec(memory_space=pl.ANY)
+forward_cut = 512
+backward_cut = 1024
+feature_cut = 512
+small_limit = 12 * 1024 * 1024
+mlp_limit = 60 * 1024 * 1024
 
 
 def gelu_parts(pre):
@@ -74,7 +78,7 @@
         out_shape=out_shapes,
         in_specs=[vmem_spec] * len(args),
         out_specs=[vmem_spec] * len(out_shapes),
-        compiler_params=pltpu.CompilerParams(vmem_limit_bytes=32 * 1024 * 1024),
+        compiler_params=pltpu.CompilerParams(vmem_limit_bytes=small_limit),
     )(*args)
 
 
@@ -201,111 +205,123 @@
     return small_call(body, [shape_of(slots, upstream.shape[1])], (upstream, targets_t, gates_t))[0]
 
 
-def tile_width(hidden):
-    return 512 if hidden % 512 == 0 else hidden
-
-
-def weight_copies(parity, own_up, own_down, sib_up, sib_down, up_buf, down_buf, up_sem, down_sem):
-    tiles, _, width = up_buf.shape
+def cuts(size, width):
+    width = width if size % width == 0 else size
+    return [slice(at, at + width) for at in range(0, size, width)]
+
+
+class TileCopies:
+    def __init__(self, where, semaphores):
+        self.where = where
+        self.semaphores = semaphores
+
+    def copy(self, source, target, i):
+        at = self.where[i]
+        return pltpu.make_async_copy(source.at[at], target.at[at], self.semaphores.at[i])
+
+
+def start_from(parity, own, sibling, begin):
     own_layer = core_index() == parity
 
-    def up_copy(source, i):
-        return pltpu.make_async_copy(
-            source.at[:, pl.ds(i * width, width)], up_buf.at[i], up_sem.at[i]
-        )
-
-    def down_copy(source, i):
-        return pltpu.make_async_copy(
-            source.at[pl.ds(i * width, width), :], down_buf.at[i], down_sem.at[i]
-        )
-
-    def start_all(up_source, down_source, down_first):
-        for i in range(tiles):
-            if down_first:
-                down_copy(down_source, i).start()
-                up_copy(up_source, i).start()
-            else:
-                up_copy(up_source, i).start()
-                down_copy(down_source, i).start()
-
-    def start(down_first):
-        @pl.when(own_layer)
-        def _():
-            start_all(own_up, own_down, down_first)
-
-        @pl.when(jnp.logical_not(own_layer))
-        def _():
-            start_all(sib_up, sib_down, down_first)
-
-    return start, lambda i: up_copy(own_up, i).wait(), lambda i: down_copy(own_down, i).wait()
-
-
-def mlp_scratch(features, hidden):
-    width = tile_width(hidden)
-    tiles = hidden // width
-    return [
-        pltpu.VMEM((tiles, features, width), bf16),
-        pltpu.VMEM((tiles, width, features), bf16),
-        pltpu.SemaphoreType.DMA((tiles,)),
-        pltpu.SemaphoreType.DMA((tiles,)),
-    ]
-
-
-def mlp_call(body, out_shapes, out_specs, arrays, weights, scratch, flops, moved):
+    @pl.when(own_layer)
+    def _():
+        begin(*own)
+
+    @pl.when(jnp.logical_not(own_layer))
+    def _():
+        begin(*sibling)
+
+
+def column_tiles(size, width):
+    return [(slice(None), cut) for cut in cuts(size, width)]
+
+
+def row_tiles(size, width):
+    return [(cut, slice(None)) for cut in cuts(size, width)]
+
+
+def mlp_call(body, out_shapes, arrays, scratch, flops, moved):
     return pl.pallas_call(
         body,
         out_shape=out_shapes,
-        in_specs=[vmem_spec] * len(arrays) + [any_spec] * 4,
-        out_specs=out_specs,
+        in_specs=[any_spec] * len(arrays),
+        out_specs=[any_spec] * len(out_shapes),
         scratch_shapes=scratch,
-        compiler_params=pltpu.CompilerParams(vmem_limit_bytes=44 * 1024 * 1024),
+        compiler_params=pltpu.CompilerParams(vmem_limit_bytes=mlp_limit),
         cost_estimate=pl.CostEstimate(flops=flops, bytes_accessed=moved, transcendentals=0),
-    )(*arrays, *weights)
+    )(*arrays)
+
+
+def copy_slots(tiles):
+    return pltpu.SemaphoreType.DMA((len(tiles),))
 
 
 def expert_forward(rows, weights, parity, keep_slope):
     slots, features = rows.shape
     hidden = weights[0].shape[1]
-    width = tile_width(hidden)
-    tiles = hidden // width
-
-    def body(x_ref, *refs):
-        hbm, refs = refs[:4], refs[4:]
+    up_tiles, down_tiles = column_tiles(hidden, forward_cut), column_tiles(features, feature_cut)
+
+    def body(rows_ref, own_up, own_down, sib_up, sib_down, out_ref, *refs):
         if keep_slope:
-            out_ref, slope_ref = refs[:2]
-            up_buf, down_buf, up_sem, down_sem, acc = refs[2:]
-        else:
-            out_ref = refs[0]
-            up_buf, down_buf, up_sem, down_sem, acc = refs[1:]
-        start, wait_up, wait_down = weight_copies(
-            parity, *hbm, up_buf, down_buf, up_sem, down_sem
-        )
-        start(False)
-        for i in range(tiles):
-            wait_up(i)
-            pre = jnp.dot(x_ref[...], up_buf[i], preferred_element_type=f32)
-            active, slope = gelu_parts(pre)
+            slope_ref, refs = refs[0], refs[1:]
+            slope_buf, slope_sem = refs[-2:]
+            slope_out = TileCopies(up_tiles, slope_sem)
+        up_buf, down_buf, active, x_ref, out_buf, up_sem, down_sem, x_sem, out_sem = refs[:9]
+        rows_in = pltpu.make_async_copy(rows_ref, x_ref, x_sem)
+        rows_in.start()
+        rows_out = TileCopies(down_tiles, out_sem)
+        up_in, down_in = TileCopies(up_tiles, up_sem), TileCopies(down_tiles, down_sem)
+
+        def begin_up(up):
+            for i in range(len(up_tiles)):
+                up_in.copy(up, up_buf, i).start()
+
+        def begin_down(down):
+            for i in range(len(down_tiles)):
+                down_in.copy(down, down_buf, i).start()
+
+        start_from(parity, (own_up,), (sib_up,), begin_up)
+        for i, at in enumerate(up_tiles):
+            up_in.copy(own_up, up_buf, i).wait()
+            if i == 0:
+                rows_in.wait()
+                start_from(parity, (own_down,), (sib_down,), begin_down)
+            pre = jnp.dot(x_ref[...], up_buf[at], preferred_element_type=f32)
+            value, slope = gelu_parts(pre)
+            active[at] = value.astype(bf16)
             if keep_slope:
-                slope_ref[:, i * width : (i + 1) * width] = slope
-            wait_down(i)
-            part = jnp.dot(active.astype(bf16), down_buf[i], preferred_element_type=f32)
-            if i == 0:
-                acc[...] = part
-            elif i < tiles - 1:
-                acc[...] += part
-            else:
-                out_ref[...] = (acc[...] + part).astype(bf16)
+                slope_buf[at] = slope
+                slope_out.copy(slope_buf, slope_ref, i).start()
+        for i, at in enumerate(down_tiles):
+            down_in.copy(own_down, down_buf, i).wait()
+            out_buf[at] = jnp.dot(active[...], down_buf[at], preferred_element_type=f32).astype(bf16)
+            rows_out.copy(out_buf, out_ref, i).start()
+        for i in range(len(down_tiles)):
+            rows_out.copy(out_buf, out_ref, i).wait()
+        if keep_slope:
+            for i in range(len(up_tiles)):
+                slope_out.copy(slope_buf, slope_ref, i).wait()
 
     out_shapes = [shape_of(slots, features)]
+    scratch = [
+        pltpu.VMEM((features, hidden), bf16),
+        pltpu.VMEM((hidden, features), bf16),
+        pltpu.VMEM((slots, hidden), bf16),
+        pltpu.VMEM((slots, features), bf16),
+        pltpu.VMEM((slots, features), bf16),
+        copy_slots(up_tiles),
+        copy_slots(down_tiles),
+        pltpu.SemaphoreType.DMA,
+        copy_slots(down_tiles),
+    ]
     if keep_slope:
         out_shapes.append(shape_of(slots, hidden, f32))
+        scratch += [pltpu.VMEM((slots, hidden), f32), copy_slots(up_tiles)]
     return mlp_call(
         body,
         out_shapes,
-        [vmem_spec] * len(out_shapes),
-        (rows,),
-        weights,
-        mlp_scratch(features, hidden) + [pltpu.VMEM((slots, features), f32)],
+        (rows, *weights),
+        scratch,
         4 * slots * features * hidden,
         4 * features * hidden + 4 * slots * features + 4 * slots * hidden * int(keep_slope),
     )
@@ -314,47 +330,89 @@
 def expert_backward(grads, slope, weights, parity, other=None, other_chip=None):
     slots, features = grads.shape
     hidden = weights[0].shape[1]
-    width = tile_width(hidden)
-    tiles = hidden // width
-    arrays = (grads, slope) if other is None else (grads, slope, other)
-
-    def body(g_ref, slope_ref, *refs):
+    down_tiles, up_tiles = row_tiles(hidden, backward_cut), row_tiles(features, feature_cut)
+    slope_tiles = column_tiles(hidden, backward_cut)
+    out_tiles = column_tiles(features, feature_cut)
+    arrays = (grads,) if other is None else (grads, other)
+
+    def body(grads_ref, *refs):
         if other is not None:
             other_ref, refs = refs[0], refs[1:]
-        hbm, refs = refs[:4], refs[4:]
-        out_ref, up_buf, down_buf, up_sem, down_sem, acc = refs
-        start, wait_up, wait_down = weight_copies(
-            parity, *hbm, up_buf, down_buf, up_sem, down_sem
-        )
-        start(True)
-        for i in range(tiles):
-            wait_down(i)
+        own_up, own_down, sib_up, sib_down, slope_ref, out_ref = refs[:6]
+        up_buf, down_buf, slope_buf, pre_grad, g_ref, out_buf = refs[6:12]
+        up_sem, down_sem, slope_sem, g_sem, out_sem = refs[12:17]
+        if other is not None:
+            other_buf = refs[17]
+        grads_in = pltpu.make_async_copy(grads_ref, g_ref, g_sem)
+        grads_in.start()
+        rows_out = TileCopies(out_tiles, out_sem)
+        up_in, down_in = TileCopies(up_tiles, up_sem), TileCopies(down_tiles, down_sem)
+        slope_in = TileCopies(slope_tiles, slope_sem)
+
+        def begin_down(down):
+            for i in range(len(down_tiles)):
+                down_in.copy(down, down_buf, i).start()
+                slope_in.copy(slope_ref, slope_buf, i).start()
+
+        def begin_up(up):
+            for i in range(len(up_tiles)):
+                up_in.copy(up, up_buf, i).start()
+
+        start_from(parity, (own_down,), (sib_down,), begin_down)
+        for i, at in enumerate(down_tiles):
+            down_in.copy(own_down, down_buf, i).wait()
+            if i == 0:
+                grads_in.wait()
+                start_from(parity, (own_up,), (sib_up,), begin_up)
+                if other is not None:
+                    pltpu.make_async_copy(other_ref, other_buf, g_sem).start()
             act_grad = lax.dot_general(
-                g_ref[...], down_buf[i], contract_last, preferred_element_type=f32
+                g_ref[...], down_buf[at], contract_last, preferred_element_type=f32
             )
-            pre_grad = (act_grad * slope_ref[:, i * width : (i + 1) * width]).astype(bf16)
-            wait_up(i)
-            part = lax.dot_general(
-                pre_grad, up_buf[i], contract_last, preferred_element_type=f32
-            )
-            if i == 0:
-                acc[...] = part
-            elif i < tiles - 1:
-                acc[...] += part
-            else:
-                out_ref[...] = (acc[...] + part).astype(bf16)
-        if other is not None:
+            slope_in.copy(slope_ref, slope_buf, i).wait()
+            pre_grad[slope_tiles[i]] = (act_grad * slope_buf[slope_tiles[i]]).astype(bf16)
+        for i, at in enumerate(up_tiles):
+            up_in.copy(own_up, up_buf, i).wait()
+            out_buf[out_tiles[i]] = lax.dot_general(
+                pre_grad[...], up_buf[at], contract_last, preferred_element_type=f32
+            ).astype(bf16)
+            if other is None:
+                rows_out.copy(out_buf, out_ref, i).start()
+        if other is None:
+            for i in range(len(out_tiles)):
+                rows_out.copy(out_buf, out_ref, i).wait()
+        else:
+            whole = out_sem.at[0]
+            pltpu.make_async_copy(other_ref, other_buf, g_sem).wait()
+
             @pl.when(chip_index() == other_chip)
             def _():
-                out_ref[...] = other_ref[...]
+                pltpu.make_async_copy(other_buf, out_ref, whole).start()
+
+            @pl.when(chip_index() != other_chip)
+            def _():
+                pltpu.make_async_copy(out_buf, out_ref, whole).start()
+
+            pltpu.make_async_copy(out_buf, out_ref, whole).wait()
 
     return mlp_call(
         body,
         [shape_of(slots, features)],
-        [vmem_spec],
-        arrays,
-        weights,
-        mlp_scratch(features, hidden) + [pltpu.VMEM((slots, features), f32)],
+        (*arrays, *weights, slope),
+        [
+            pltpu.VMEM((features, hidden), bf16),
+            pltpu.VMEM((hidden, features), bf16),
+            pltpu.VMEM((slots, hidden), f32),
+            pltpu.VMEM((slots, hidden), bf16),
+            pltpu.VMEM((slots, features), bf16),
+            pltpu.VMEM((slots, features), bf16),
+            copy_slots(up_tiles),
+            copy_slots(down_tiles),
+            copy_slots(slope_tiles),
+            pltpu.SemaphoreType.DMA,
+            copy_slots(out_tiles),
+        ]
+        + ([] if other is None else [pltpu.VMEM((slots, features), bf16)]),
         4 * slots * features * hidden,
         4 * features * hidden + 4 * slots * features + 4 * slots * hidden,
     )[0]
@@ -363,108 +421,110 @@
 def act_gradient(grads, weights, parity):
     slots, features = grads.shape
     hidden = weights[0].shape[1]
-    width = tile_width(hidden)
-    tiles = hidden // width
-
-    def body(g_ref, own_down, sib_down, out_ref, buf, sem):
-        own_layer = core_index() == parity
-
-        def copy(source, i):
-            return pltpu.make_async_copy(
-                source.at[pl.ds(i * width, width), :], buf.at[i], sem.at[i]
+    down_tiles, out_tiles = row_tiles(hidden, backward_cut), column_tiles(hidden, backward_cut)
+
+    def body(grads_ref, own_down, sib_down, out_ref, down_buf, g_ref, out_buf, down_sem, g_sem, out_sem):
+        grads_in = pltpu.make_async_copy(grads_ref, g_ref, g_sem)
+        grads_in.start()
+        down_in, grads_out = TileCopies(down_tiles, down_sem), TileCopies(out_tiles, out_sem)
+
+        def begin(down):
+            for i in range(len(down_tiles)):
+                down_in.copy(down, down_buf, i).start()
+
+        start_from(parity, (own_down,), (sib_down,), begin)
+        for i, at in enumerate(down_tiles):
+            down_in.copy(own_down, down_buf, i).wait()
+            if i == 0:
+                grads_in.wait()
+            out_buf[out_tiles[i]] = lax.dot_general(
+                g_ref[...], down_buf[at], contract_last, preferred_element_type=f32
             )
-
-        @pl.when(own_layer)
-        def _():
-            for i in range(tiles):
-                copy(own_down, i).start()
-
-        @pl.when(jnp.logical_not(own_layer))
-        def _():
-            for i in range(tiles):
-                copy(sib_down, i).start()
-
-        for i in range(tiles):
-            copy(own_down, i).wait()
-            out_ref[:, i * width : (i + 1) * width] = lax.dot_general(
-                g_ref[...], buf[i], contract_last, preferred_element_type=f32
-            )
-
-    return pl.pallas_call(
-        body,
-        out_shape=shape_of(slots, hidden, f32),
-        in_specs=[vmem_spec, any_spec, any_spec],
-        out_specs=vmem_spec,
-        scratch_shapes=[
-            pltpu.VMEM((tiles, width, features), bf16),
-            pltpu.SemaphoreType.DMA((tiles,)),
+            grads_out.copy(out_buf, out_ref, i).start()
+        for i in range(len(out_tiles)):
+            grads_out.copy(out_buf, out_ref, i).wait()
+
+    return mlp_call(
+        body,
+        [shape_of(slots, hidden, f32)],
+        (grads, weights[1], weights[3]),
+        [
+            pltpu.VMEM((hidden, features), bf16),
+            pltpu.VMEM((slots, features), bf16),
+            pltpu.VMEM((slots, hidden), f32),
+            copy_slots(down_tiles),
+            pltpu.SemaphoreType.DMA,
+            copy_slots(out_tiles),
         ],
-        compiler_params=pltpu.CompilerParams(vmem_limit_bytes=32 * 1024 * 1024),
-        cost_estimate=pl.CostEstimate(
-            flops=2 * slots * features * hidden,
-            bytes_accessed=2 * features * hidden + 4 * slots * hidden,
-            transcendentals=0,
-        ),
-    )(grads, weights[1], weights[3])
+        2 * slots * features * hidden,
+        2 * features * hidden + 4 * slots * hidden,
+    )[0]
 
 
 def turn_around(rows, act_grad, weights, parity):
     slots, features = rows.shape
     hidden = weights[0].shape[1]
-    width = tile_width(hidden)
-    tiles = hidden // width
-
-    def body(x_ref, ag_ref, own_up, sib_up, out_ref, slope_ref, active_ref, buf, sem, acc):
-        own_layer = core_index() == parity
-
-        def copy(source, i):
-            return pltpu.make_async_copy(
-                source.at[:, pl.ds(i * width, width)], buf.at[i], sem.at[i]
-            )
-
-        @pl.when(own_layer)
-        def _():
-            for i in range(tiles):
-                copy(own_up, i).start()
-
-        @pl.when(jnp.logical_not(own_layer))
-        def _():
-            for i in range(tiles):
-                copy(sib_up, i).start()
-
-        for i in range(tiles):
-            copy(own_up, i).wait()
-            columns = slice(i * width, (i + 1) * width)
-            pre = jnp.dot(x_ref[...], buf[i], preferred_element_type=f32)
-            active, slope = gelu_parts(pre)
-            slope_ref[:, columns] = slope
-            active_ref[:, columns] = active.astype(bf16)
-            pre_grad = (ag_ref[:, columns] * slope).astype(bf16)
-            part = lax.dot_general(pre_grad, buf[i], contract_last, preferred_element_type=f32)
+    tiles, out_tiles = column_tiles(hidden, backward_cut), column_tiles(features, feature_cut)
+    up_rows = row_tiles(features, feature_cut)
+
+    def body(rows_ref, own_up, sib_up, ag_ref, out_ref, slope_ref, active_ref, *refs):
+        up_buf, ag_buf, slope_buf, active_buf, pre_grad, x_ref, out_buf = refs[:7]
+        up_in, grad_in, slope_out, active_out = [TileCopies(tiles, sem) for sem in refs[7:11]]
+        rows_out = TileCopies(out_tiles, refs[11])
+        rows_in = pltpu.make_async_copy(rows_ref, x_ref, refs[12])
+        rows_in.start()
+
+        def begin(up):
+            for i in range(len(tiles)):
+                up_in.copy(up, up_buf, i).start()
+                grad_in.copy(ag_ref, ag_buf, i).start()
+
+        start_from(parity, (own_up,), (sib_up,), begin)
+        for i, at in enumerate(tiles):
+            up_in.copy(own_up, up_buf, i).wait()
             if i == 0:
-                acc[...] = part
-            elif i < tiles - 1:
-                acc[...] += part
-            else:
-                out_ref[...] = (acc[...] + part).astype(bf16)
-
-    return pl.pallas_call(
-        body,
-        out_shape=[shape_of(slots, features), shape_of(slots, hidden, f32), shape_of(slots, hidden)],
-        in_specs=[vmem_spec, vmem_spec, any_spec, any_spec],
-        out_specs=[vmem_spec] * 3,
-        scratch_shapes=[
-            pltpu.VMEM((tiles, features, width), bf16),
-            pltpu.SemaphoreType.DMA((tiles,)),
-            pltpu.VMEM((slots, features), f32),
+                rows_in.wait()
+            pre = jnp.dot(x_ref[...], up_buf[at], preferred_element_type=f32)
+            value, slope = gelu_parts(pre)
+            slope_buf[at] = slope
+            active_buf[at] = value.astype(bf16)
+            slope_out.copy(slope_buf, slope_ref, i).start()
+            active_out.copy(active_buf, active_ref, i).start()
+            grad_in.copy(ag_ref, ag_buf, i).wait()
+            pre_grad[at] = (ag_buf[at] * slope).astype(bf16)
+        for i, (at, rows_at) in enumerate(zip(out_tiles, up_rows)):
+            out_buf[at] = lax.dot_general(
+                pre_grad[...], up_buf[rows_at], contract_last, preferred_element_type=f32
+            ).astype(bf16)
+            rows_out.copy(out_buf, out_ref, i).start()
+        for i in range(len(out_tiles)):
+            rows_out.copy(out_buf, out_ref, i).wait()
+        for i in range(len(tiles)):
+            slope_out.copy(slope_buf, slope_ref, i).wait()
+            active_out.copy(active_buf, active_ref, i).wait()
+
+    return mlp_call(
+        body,
+        [shape_of(slots, features), shape_of(slots, hidden, f32), shape_of(slots, hidden)],
+        (rows, weights[0], weights[2], act_grad),
+        [
+            pltpu.VMEM((features, hidden), bf16),
+            pltpu.VMEM((slots, hidden), f32),
+            pltpu.VMEM((slots, hidden), f32),
+            pltpu.VMEM((slots, hidden), bf16),
+            pltpu.VMEM((slots, hidden), bf16),
+            pltpu.VMEM((slots, features), bf16),
+            pltpu.VMEM((slots, features), bf16),
+            copy_slots(tiles),
+            copy_slots(tiles),
+            copy_slots(tiles),
+            copy_slots(tiles),
+            copy_slots(out_tiles),
+            pltpu.SemaphoreType.DMA,
         ],
-        compiler_params=pltpu.CompilerParams(vmem_limit_bytes=44 * 1024 * 1024),
-        cost_estimate=pl.CostEstimate(
-            flops=4 * slots * features * hidden,
-            bytes_accessed=2 * features * hidden + 10 * slots * hidden,
-            transcendentals=0,
-        ),
-    )(rows, act_grad, weights[0], weights[2])
+        4 * slots * features * hidden,
+        2 * features * hidden + 10 * slots * hidden,
+    )
 
 
 def slot_targets(picks_t, experts, capacity):

time: 393 us -> 378 us (0.962)
  local copies, waits for them, and re-layouts: 31.3 us -> 3.26 us
  Pallas kernels: 52.8 us -> 61.2 us
  waiting for transfers between devices: 79.3 us -> 84.3 us
    unnamed x92 -> x4, local copies, waits for them, and re-layouts: 29.7 us -> 1.75 us
    pallas_call x8, Pallas kernels: 44.8 us -> 52.2 us  [mlp_call(): pl.pallas_call(body, out_shape=out_shapes, in_specs=[any_spec] * len(arra...]
    all_to_all x5, waiting for transfers between devices: 65.6 us -> 70.8 us  [to_experts(): return lax.all_to_all(x, 'expert', split_axis=0, concat_axis=0, tiled=True)]
  transfers between devices with their start and end apart: 12 -> 12, of which waited for: 9 -> 9; matrix products, arithmetic and copies ran while one was open for 4% -> 3% of each run, Pallas kernels for 1% -> 2%
where the time goes in v2:
time: 378 us; the launch traced here: 377 us
  blocking collectives  193 us (51%)
  waiting for transfers between devices  84.3 us (22%)
  Pallas kernels  61.2 us (16%)
  starting transfers between devices  22.7 us (6%)
  matrix products  6.47 us (2%)
  other arithmetic  5.31 us (1%)
    all_to_all x9, blocking collectives, to_experts(): return lax.all_to_all(x, 'expert', split_axis=0, concat_axis=0, tiled=True)  193 us
    all_to_all x5, waiting for transfers between devices, to_experts(): return lax.all_to_all(x, 'expert', split_axis=0, concat_axis=0, tiled=True)  70.8 us
    pallas_call x8, Pallas kernels, mlp_call(): pl.pallas_call(body, out_shape=out_shapes, in_specs=[any_spec] * len(arra...  52.2 us
    all_to_all x5, starting transfers between devices, to_experts(): return lax.all_to_all(x, 'expert', split_axis=0, concat_axis=0, tiled=True)  18.6 us
    ppermute x2, waiting for transfers between devices, shift_chips(): lax.ppermute(x, 'section', [(s, (s + 2 * by) % sections) for s in range(s...  9.94 us
    pallas_call x11, Pallas kernels, small_call(): pl.pallas_call(body, out_shape=out_shapes, in_specs=[vmem_spec] * len(arg...  8.95 us
  transfers between devices with their start and end apart: 12, of which 9 were waited for; matrix products, arithmetic and copies ran while one was open for 3% of the time, Pallas kernels for 2%

profile of v2, /device:TPU:0, one launch (start us, length us, event | category | flops | bytes accessed | tf_op | source)
XLA Modules:
  0.0 376.8 jit_solution(3493028832396353945)
XLA Ops:
  0.6 0.5 collective-permute-start.1
  1.2 0.7 convert_bitcast_fusion
  1.9 0.7 slice_bitcast_fusion
  2.6 0.7 fusion.8
  3.3 0.4 collective-permute-start
  3.8 1.2 select_bitcast_fusion.2
  5.0 3.0 collective-permute-done
  8.0 0.7 broadcast_select_fusion.5
  8.7 0.1 fusion.6
  8.9 0.1 fusion.7
  9.1 0.1 copy.100
  9.2 0.1 copy.103
  9.3 0.1 copy.102
  9.5 0.1 copy.99
  9.7 0.5 shard_map.86
  10.2 25.1 %all_to_all.154 = bf16[8,40,1024]{2,1,0:T(8,128)(2,1)} all-to-all(bf16[8,40,1024]{2,1,0:T(8,128)(2,1)S(1)} %bitcast.80), channel_id=1, replica_groups=mesh['section'=4,'expert'=8] {'expert'}, dimensions={0} | all-to-all | bytes 1310720 | tf_op jit(solution)/shard_map/all_to_all | solution.py:560
  35.2 6.5 %shard_map.87 = bf16[320,1024]{1,0:T(8,128)(2,1)} custom-call(bf16[320,1024]{1,0:T(8,128)(2,1)} %bitcast.117, bf16[1024,2048]{1,0:T(8,128)(2,1)} %bitcast.102, bf16[2048,1024]{1,0:T(8,128)(2,1)} %bitcast.110, bf16[1024,2048]{1,0:T(8,128)(2,1)} %collective-permute-done.1.sib_up.refs_2_.refs_3_, bf16[2048,1024]{1,0:T(8,128)(2,1)} %collective-permute-done.2.sib_down.refs_3_.refs_4_), custom_call_target="tpu_custom_call" | custom-call | flops 2684354560 | bytes 9699328 | tf_op jit(solution)/shard_map/pallas_call | solution.py:244
  41.7 3.6 all-to-all-start.1
  45.3 0.1 copy.106.g_ref
  45.4 16.7 %all-to-all-done.1 = bf16[8,40,1024]{2,1,0:T(8,128)(2,1)S(1)} async-done(((bf16[8,40,1024]{2,1,0:T(8,128)(2,1)}), bf16[8,40,1024]{2,1,0:T(8,128)(2,1)S(1)}, u32[]{:S(2)}, u32[]{:S(2)}) %all-to-all-start.1) | async-done | bytes 655392 | tf_op jit(solution)/shard_map/all_to_all | solution.py:560
  62.1 0.9 shard_map.88
  63.1 21.4 %all_to_all.155 = bf16[8,40,1024]{2,1,0:T(8,128)(2,1)} all-to-all(bf16[8,40,1024]{2,1,0:T(8,128)(2,1)S(1)} %bitcast.92), channel_id=1, replica_groups=mesh['section'=4,'expert'=8] {'expert'}, dimensions={0} | all-to-all | bytes 1310720 | tf_op jit(solution)/shard_map/all_to_all | solution.py:560
  84.4 6.4 %shard_map.89 = bf16[320,1024]{1,0:T(8,128)(2,1)} custom-call(bf16[320,1024]{1,0:T(8,128)(2,1)} %bitcast.126, bf16[1024,2048]{1,0:T(8,128)(2,1)} %bitcast.103, bf16[2048,1024]{1,0:T(8,128)(2,1)} %bitcast.111, bf16[1024,2048]{1,0:T(8,128)(2,1)} %collective-permute-done.1.sib_up.refs_2_.refs_3_, bf16[2048,1024]{1,0:T(8,128)(2,1)} %collective-permute-done.2.sib_down.refs_3_.refs_4_), custom_call_target="tpu_custom_call" | custom-call | flops 2684354560 | bytes 9699328 | tf_op jit(solution)/shard_map/pallas_call | solution.py:244
  90.9 3.6 all-to-all-start.3
  94.4 0.1 copy.108.g_ref
  94.5 16.8 %all-to-all-done.3 = bf16[8,40,1024]{2,1,0:T(8,128)(2,1)S(1)} async-done(((bf16[8,40,1024]{2,1,0:T(8,128)(2,1)}), bf16[8,40,1024]{2,1,0:T(8,128)(2,1)S(1)}, u32[]{:S(2)}, u32[]{:S(2)}) %all-to-all-start.3) | async-done | bytes 655392 | tf_op jit(solution)/shard_map/all_to_all | solution.py:560
  111.3 0.5 shard_map.90
  111.8 1.5 collective-permute-start.3
  113.3 5.0 %collective-permute-done.3.arrived_ref = bf16[128,1024]{1,0:T(8,128)(2,1)S(1)} collective-permute-done((bf16[128,1024]{1,0:T(8,128)(2,1)S(1)}, bf16[128,1024]{1,0:T(8,128)(2,1)S(1)}, u32[]{:S(2)}, u32[]{:S(2)}) %collective-permute-start.3) | collective-permute-done | bytes 262176 | tf_op jit(solution)/shard_map/ppermute | solution.py:555
  118.2 0.5 shard_map.91
  118.7 22.4 %all_to_all.156 = bf16[8,40,1024]{2,1,0:T(8,128)(2,1)} all-to-all(bf16[8,40,1024]{2,1,0:T(8,128)(2,1)S(1)} %bitcast.90), channel_id=1, replica_groups=mesh['section'=4,'expert'=8] {'expert'}, dimensions={0} | all-to-all | bytes 1310720 | tf_op jit(solution)/shard_map/all_to_all | solution.py:560
  141.1 7.3 %shard_map.92 = (bf16[320,1024]{1,0:T(8,128)(2,1)}, f32[320,2048]{1,0:T(8,128)}) custom-call(bf16[320,1024]{1,0:T(8,128)(2,1)} %bitcast.124, bf16[1024,2048]{1,0:T(8,128)(2,1)} %bitcast.104, bf16[2048,1024]{1,0:T(8,128)(2,1)} %bitcast.112, bf16[1024,2048]{1,0:T(8,128)(2,1)} %collective-permute-done.1.sib_up.refs_2_.refs_3_, ...), custom_call_target="tpu_custom_call" | custom-call | flops 2684354560 | bytes 12320768 | tf_op jit(solution)/shard_map/pallas_call | solution.py:244
  148.4 20.5 %all_to_all.157 = bf16[8,40,1024]{2,1,0:T(8,128)(2,1)S(1)} all-to-all(bf16[8,40,1024]{2,1,0:T(8,128)(2,1)} %bitcast.131), channel_id=1, replica_groups=mesh['section'=4,'expert'=8] {'expert'}, dimensions={0} | all-to-all | bytes 1310720 | tf_op jit(solution)/shard_map/all_to_all | solution.py:560
  168.8 1.8 shard_map.93
  170.6 3.5 all-to-all-start.6
  174.2 4.8 %shard_map.94.ag_ref = f32[320,2048]{1,0:T(8,128)} custom-call(bf16[320,1024]{1,0:T(8,128)(2,1)} %bitcast.118, bf16[2048,1024]{1,0:T(8,128)(2,1)} %bitcast.113, bf16[2048,1024]{1,0:T(8,128)(2,1)} %collective-permute-done.2.sib_down.refs_3_.refs_4_), custom_call_target="tpu_custom_call" | custom-call | flops 1342177280 | bytes 6815744 | tf_op jit(solution)/shard_map/pallas_call | solution.py:244
  179.0 11.7 %all-to-all-done.6 = bf16[8,40,1024]{2,1,0:T(8,128)(2,1)S(1)} async-done(((bf16[8,40,1024]{2,1,0:T(8,128)(2,1)}), bf16[8,40,1024]{2,1,0:T(8,128)(2,1)S(1)}, u32[]{:S(2)}, u32[]{:S(2)}) %all-to-all-start.6) | async-done | bytes 655392 | tf_op jit(solution)/shard_map/all_to_all | solution.py:560
  190.7 0.9 copy-done
  191.6 7.3 %shard_map.95 = (bf16[320,1024]{1,0:T(8,128)(2,1)}, f32[320,2048]{1,0:T(8,128)}, bf16[320,2048]{1,0:T(8,128)(2,1)}) custom-call(bf16[320,1024]{1,0:T(8,128)(2,1)} %bitcast.120, bf16[1024,2048]{1,0:T(8,128)(2,1)} %bitcast.105, bf16[1024,2048]{1,0:T(8,128)(2,1)} %collective-permute-done.1.sib_up.refs_2_.refs_3_, f32[320,2048]{1,0:T(8,128)} %shard_map.94.ag_ref), custom_call_target="tpu_custom_call" | custom-call | flops 2684354560 | bytes 10747904 | tf_op jit(solution)/shard_map/pallas_call | solution.py:244
  199.0 21.3 %all_to_all.158 = bf16[8,40,1024]{2,1,0:T(8,128)(2,1)S(1)} all-to-all(bf16[8,40,1024]{2,1,0:T(8,128)(2,1)} %bitcast.130), channel_id=1, replica_groups=mesh['section'=4,'expert'=8] {'expert'}, dimensions={0} | all-to-all | bytes 1310720 | tf_op jit(solution)/shard_map/all_to_all | solution.py:560
  220.2 0.9 shard_map.96
  221.2 20.6 %all_to_all.159 = bf16[8,40,1024]{2,1,0:T(8,128)(2,1)} all-to-all(bf16[8,40,1024]{2,1,0:T(8,128)(2,1)S(1)} %bitcast.91), channel_id=1, replica_groups=mesh['section'=4,'expert'=8] {'expert'}, dimensions={0} | all-to-all | bytes 1310720 | tf_op jit(solution)/shard_map/all_to_all | solution.py:560
  241.8 6.6 %shard_map.97 = bf16[320,1024]{1,0:T(8,128)(2,1)} custom-call(bf16[320,1024]{1,0:T(8,128)(2,1)} %bitcast.125, bf16[1024,2048]{1,0:T(8,128)(2,1)} %bitcast.106, bf16[2048,1024]{1,0:T(8,128)(2,1)} %bitcast.114, bf16[1024,2048]{1,0:T(8,128)(2,1)} %collective-permute-done.1.sib_up.refs_2_.refs_3_, ...), custom_call_target="tpu_custom_call" | custom-call | flops 2684354560 | bytes 12320768 | tf_op jit(solution)/shard_map/pallas_call | solution.py:244
  248.5 20.6 %all_to_all.160 = bf16[8,40,1024]{2,1,0:T(8,128)(2,1)S(1)} all-to-all(bf16[8,40,1024]{2,1,0:T(8,128)(2,1)} %bitcast.127), channel_id=1, replica_groups=mesh['section'=4,'expert'=8] {'expert'}, dimensions={0} | all-to-all | bytes 1310720 | tf_op jit(solution)/shard_map/all_to_all | solution.py:560
  269.0 0.6 shard_map.98
  269.7 1.5 collective-permute-start.4
  271.1 5.0 %collective-permute-done.4.up_ref = bf16[128,1024]{1,0:T(8,128)(2,1)S(1)} collective-permute-done((bf16[128,1024]{1,0:T(8,128)(2,1)S(1)}, bf16[128,1024]{1,0:T(8,128)(2,1)S(1)}, u32[]{:S(2)}, u32[]{:S(2)}) %collective-permute-start.4) | collective-permute-done | bytes 262176 | tf_op jit(solution)/shard_map/ppermute | solution.py:555
  276.1 1.2 shard_map.99
  277.3 4.4 %all-to-all-start.10 = ((bf16[8,40,1024]{2,1,0:T(8,128)(2,1)}), bf16[8,40,1024]{2,1,0:T(8,128)(2,1)S(1)}, u32[]{:S(2)}, u32[]{:S(2)}) async-start(bf16[8,40,1024]{2,1,0:T(8,128)(2,1)} %bitcast.39), calls=%async_computation.10 | async-start | bytes 1310720 | tf_op jit(solution)/shard_map/all_to_all | solution.py:560
  281.7 6.2 %fusion.3.refs_0_ = bf16[320,1024]{1,0:T(8,128)(2,1)} fusion(bf16[320,2048]{1,0:T(8,128)(2,1)} %get-tuple-element.28, bf16[2048,1024]{1,0:T(8,128)(2,1)} %collective-permute-done.2.sib_down.refs_3_.refs_4_, pred[]{:T(512)S(6)} %eq.26, bf16[1,1,2048,1024]{3,2,1,0:T(8,128)(2,1)} %param.10), kind=kOutput, calls=%fused_computation.3 | convolution fusion | flops 1344602112 | bytes 10354689 | tf_op jit(solution)/shard_map/dot_general | solution.py:617
  287.9 9.7 %all-to-all-done.10 = bf16[8,40,1024]{2,1,0:T(8,128)(2,1)S(1)} async-done(((bf16[8,40,1024]{2,1,0:T(8,128)(2,1)}), bf16[8,40,1024]{2,1,0:T(8,128)(2,1)S(1)}, u32[]{:S(2)}, u32[]{:S(2)}) %all-to-all-start.10) | async-done | bytes 655392 | tf_op jit(solution)/shard_map/all_to_all | solution.py:560
  297.6 0.9 copy-done.1
  298.4 6.7 %shard_map.100 = bf16[320,1024]{1,0:T(8,128)(2,1)} custom-call(bf16[320,1024]{1,0:T(8,128)(2,1)} %bitcast.128, bf16[320,1024]{1,0:T(8,128)(2,1)} %fusion.3.refs_0_, bf16[1024,2048]{1,0:T(8,128)(2,1)} %bitcast.107, bf16[2048,1024]{1,0:T(8,128)(2,1)} %bitcast.115, bf16[1024,2048]{1,0:T(8,128)(2,1)} %collective-permute-done.1.sib_up.refs_2_.refs_3_, ...), custom_call_target="tpu_custom_call" | custom-call | flops 2684354560 | bytes 12320768 | tf_op jit(solution)/shard_map/pallas_call | solution.py:244
  305.2 20.4 %all_to_all.161 = bf16[8,40,1024]{2,1,0:T(8,128)(2,1)S(1)} all-to-all(bf16[8,40,1024]{2,1,0:T(8,128)(2,1)} %bitcast.129), channel_id=1, replica_groups=mesh['section'=4,'expert'=8] {'expert'}, dimensions={0} | all-to-all | bytes 1310720 | tf_op jit(solution)/shard_map/all_to_all | solution.py:560
  325.6 0.9 shard_map.102
  326.6 20.4 %all_to_all.162 = bf16[8,40,1024]{2,1,0:T(8,128)(2,1)} all-to-all(bf16[8,40,1024]{2,1,0:T(8,128)(2,1)S(1)} %bitcast.89), channel_id=1, replica_groups=mesh['section'=4,'expert'=8] {'expert'}, dimensions={0} | all-to-all | bytes 1310720 | tf_op jit(solution)/shard_map/all_to_all | solution.py:560
  346.9 6.6 %shard_map.103 = bf16[320,1024]{1,0:T(8,128)(2,1)} custom-call(bf16[320,1024]{1,0:T(8,128)(2,1)} %bitcast.123, bf16[1024,2048]{1,0:T(8,128)(2,1)} %bitcast.108, bf16[2048,1024]{1,0:T(8,128)(2,1)} %bitcast.116, bf16[1024,2048]{1,0:T(8,128)(2,1)} %collective-permute-done.1.sib_up.refs_2_.refs_3_, ...), custom_call_target="tpu_custom_call" | custom-call | flops 2684354560 | bytes 12320768 | tf_op jit(solution)/shard_map/pallas_call | solution.py:244
  353.5 3.6 all-to-all-start.13
  357.1 0.5 shard_map.101
  357.8 15.9 %all-to-all-done.13 = bf16[8,40,1024]{2,1,0:T(8,128)(2,1)S(1)} async-done(((bf16[8,40,1024]{2,1,0:T(8,128)(2,1)}), bf16[8,40,1024]{2,1,0:T(8,128)(2,1)S(1)}, u32[]{:S(2)}, u32[]{:S(2)}) %all-to-all-start.13) | async-done | bytes 655392 | tf_op jit(solution)/shard_map/all_to_all | solution.py:560
  373.6 0.6 shard_map.104
  374.4 0.9 maximum_select_fusion
  375.3 0.6 collective-permute-done.6
  375.9 0.9 maximum_select_fusion.1
  (24 shorter events, 0.6 us)
Async XLA Ops:
  0.6 34.6 %collective-permute-start.1 = (bf16[1024,2048]{1,0:T(8,128)(2,1)}, bf16[1024,2048]{1,0:T(8,128)(2,1)}, u32[]{:S(2)}, u32[]{:S(2)}) collective-permute-start(bf16[1024,2048]{1,0:T(8,128)(2,1)} %bitcast.101), channel_id=1, source_target_pairs={{0,8},{8,0},{16,24},{24,16},{1,9},{9,1},{17,25},{25,17},{2,10},{10... | collective-permute-start | bytes 12582920 | tf_op jit(solution)/shard_map/ppermute | solution.py:552
  1.1 34.1 %collective-permute-start.2 = (bf16[2048,1024]{1,0:T(8,128)(2,1)}, bf16[2048,1024]{1,0:T(8,128)(2,1)}, u32[]{:S(2)}, u32[]{:S(2)}) collective-permute-start(bf16[2048,1024]{1,0:T(8,128)(2,1)} %bitcast.109), channel_id=1, source_target_pairs={{0,8},{8,0},{16,24},{24,16},{1,9},{9,1},{17,25},{25,17},{2,10},{10... | collective-permute-start | bytes 12582920 | tf_op jit(solution)/shard_map/ppermute | solution.py:552
  3.3 4.6 %collective-permute-start = (f32[12,128]{1,0:T(8,128)S(1)}, f32[12,128]{1,0:T(8,128)S(1)}, u32[]{:S(2)}, u32[]{:S(2)}) collective-permute-start(f32[12,128]{1,0:T(8,128)S(1)} %fusion.8), channel_id=1, source_target_pairs={{0,8},{8,0},{16,24},{24,16},{1,9},{9,1},{17,25},{25,17},{2,10},{10... | collective-permute-start | bytes 18440 | tf_op jit(solution)/shard_map/ppermute | solution.py:552
  41.7 20.4 %all-to-all-start.1 = ((bf16[8,40,1024]{2,1,0:T(8,128)(2,1)}), bf16[8,40,1024]{2,1,0:T(8,128)(2,1)S(1)}, u32[]{:S(2)}, u32[]{:S(2)}) async-start(bf16[8,40,1024]{2,1,0:T(8,128)(2,1)} %bitcast.121), calls=%async_computation.1 | async-start | bytes 1310720 | tf_op jit(solution)/shard_map/all_to_all | solution.py:560
  90.9 20.4 %all-to-all-start.3 = ((bf16[8,40,1024]{2,1,0:T(8,128)(2,1)}), bf16[8,40,1024]{2,1,0:T(8,128)(2,1)S(1)}, u32[]{:S(2)}, u32[]{:S(2)}) async-start(bf16[8,40,1024]{2,1,0:T(8,128)(2,1)} %bitcast.122), calls=%async_computation.3 | async-start | bytes 1310720 | tf_op jit(solution)/shard_map/all_to_all | solution.py:560
  111.8 6.4 %collective-permute-start.3 = (bf16[128,1024]{1,0:T(8,128)(2,1)S(1)}, bf16[128,1024]{1,0:T(8,128)(2,1)S(1)}, u32[]{:S(2)}, u32[]{:S(2)}) collective-permute-start(bf16[128,1024]{1,0:T(8,128)(2,1)S(1)} %shard_map.90), channel_id=1, source_target_pairs={{0,16},{8,24},{16,0},{24,8},{1,17},{9,25},{17,1},{25,9},{2,18},{10... | collective-permute-start | bytes 786440 | tf_op jit(solution)/shard_map/ppermute | solution.py:555
  170.6 20.1 %all-to-all-start.6 = ((bf16[8,40,1024]{2,1,0:T(8,128)(2,1)}), bf16[8,40,1024]{2,1,0:T(8,128)(2,1)S(1)}, u32[]{:S(2)}, u32[]{:S(2)}) async-start(bf16[8,40,1024]{2,1,0:T(8,128)(2,1)} %bitcast.31), calls=%async_computation.6 | async-start | bytes 1310720 | tf_op jit(solution)/shard_map/all_to_all | solution.py:560
  190.7 0.9 copy-start
  269.7 6.5 %collective-permute-start.4 = (bf16[128,1024]{1,0:T(8,128)(2,1)S(1)}, bf16[128,1024]{1,0:T(8,128)(2,1)S(1)}, u32[]{:S(2)}, u32[]{:S(2)}) collective-permute-start(bf16[128,1024]{1,0:T(8,128)(2,1)S(1)} %shard_map.98), channel_id=1, source_target_pairs={{0,16},{8,24},{16,0},{24,8},{1,17},{9,25},{17,1},{25,9},{2,18},{10... | collective-permute-start | bytes 786440 | tf_op jit(solution)/shard_map/ppermute | solution.py:555
  277.3 20.2 %all-to-all-start.10 = ((bf16[8,40,1024]{2,1,0:T(8,128)(2,1)}), bf16[8,40,1024]{2,1,0:T(8,128)(2,1)S(1)}, u32[]{:S(2)}, u32[]{:S(2)}) async-start(bf16[8,40,1024]{2,1,0:T(8,128)(2,1)} %bitcast.39), calls=%async_computation.10 | async-start | bytes 1310720 | tf_op jit(solution)/shard_map/all_to_all | solution.py:560
  297.6 0.9 copy-start.1
  353.5 20.1 %all-to-all-start.13 = ((bf16[8,40,1024]{2,1,0:T(8,128)(2,1)}), bf16[8,40,1024]{2,1,0:T(8,128)(2,1)S(1)}, u32[]{:S(2)}, u32[]{:S(2)}) async-start(bf16[8,40,1024]{2,1,0:T(8,128)(2,1)} %bitcast.119), calls=%async_computation.13 | async-start | bytes 1310720 | tf_op jit(solution)/shard_map/all_to_all | solution.py:560
  357.7 16.7 %collective-permute-start.5 = (bf16[128,1024]{1,0:T(8,128)(2,1)S(1)}, bf16[128,1024]{1,0:T(8,128)(2,1)S(1)}, u32[]{:S(2)}, u32[]{:S(2)}) collective-permute-start(bf16[128,1024]{1,0:T(8,128)(2,1)S(1)} %get-tuple-element.35), channel_id=1, source_target_pairs={{0,8},{8,0},{16,24},{24,16},{1,9},{9,1},{17,25},{25,17},{2,10},{10... | collective-permute-start | bytes 786440 | tf_op jit(solution)/shard_map/ppermute | solution.py:552
  374.3 1.6 collective-permute-start.6

commit v3 on v2

--- a/solution.py
+++ b/solution.py
@@ -86,27 +86,114 @@
     return jax.ShapeDtypeStruct((rows, columns), kind)
 
 
-def first_pack(state, gain, targets_t, grad, grad_targets_t, grad_gates_t, slots, last_chip):
-    def body(state_ref, gain_ref, tt_ref, grad_ref, gtt_ref, ggt_ref, out_ref):
+def gather_params(ids_t, gates_t, gain):
+    def body(ids_hbm, gates_hbm, gain_hbm, own_ref, send_ref, ids_ref, gates_ref, gain_ref, sem):
+        copies = [
+            pltpu.make_async_copy(source, target, sem.at[i])
+            for i, (source, target) in enumerate(
+                ((ids_hbm, ids_ref), (gates_hbm, gates_ref), (gain_hbm, gain_ref))
+            )
+        ]
+        for copy in copies:
+            copy.start()
+        for copy in copies:
+            copy.wait()
+        for out_ref, batch in ((own_ref, core_index()), (send_ref, 1 - core_index())):
+            out_ref[0:2] = ids_ref[batch].astype(f32)
+            out_ref[2:4] = gates_ref[batch]
+            out_ref[4:] = gain_ref[...]
+
+    rows = 4 + gain.shape[0]
+    return pl.pallas_call(
+        body,
+        out_shape=[shape_of(rows, gain.shape[1], f32)] * 2,
+        in_specs=[any_spec] * 3,
+        out_specs=[vmem_spec] * 2,
+        scratch_shapes=[
+            pltpu.VMEM(ids_t.shape, jnp.int32),
+            pltpu.VMEM(gates_t.shape, f32),
+            pltpu.VMEM(gain.shape, f32),
+            pltpu.SemaphoreType.DMA((3,)),
+        ],
+        compiler_params=pltpu.CompilerParams(vmem_limit_bytes=mlp_limit),
+    )(ids_t, gates_t, gain)
+
+
+def as_column(row):
+    size = row.shape[1]
+    down = lax.broadcasted_iota(jnp.int32, (size, size), 0)
+    across = lax.broadcasted_iota(jnp.int32, (size, size), 1)
+    return jnp.sum(jnp.where(down == across, row, 0.0), axis=1, keepdims=True)
+
+
+def slot_rows(ids_t, experts, capacity):
+    rows = ids_t.shape[1]
+    expert = lax.broadcasted_iota(jnp.int32, (experts, rows), 0).astype(f32)
+    hits = [(ids_t[k : k + 1, :] == expert).astype(f32) for k in range(2)]
+    before = lax.broadcasted_iota(jnp.int32, (rows, rows), 0)
+    after = lax.broadcasted_iota(jnp.int32, (rows, rows), 1)
+    earlier = (before < after).astype(f32)
+    rank = jnp.dot(hits[0] + hits[1], earlier, preferred_element_type=f32)
+    return [
+        ids_t[k : k + 1, :] * float(capacity) + jnp.sum(hits[k] * rank, axis=0, keepdims=True)
+        for k in range(2)
+    ]
+
+
+def prepare_pack(own_small, sib_small, inputs, out_grad, experts, capacity, last_chip):
+    rows, features = inputs.shape[1:]
+    slots = experts * capacity
+    params = [
+        jax.ShapeDtypeStruct((2, rows), jnp.int32),
+        jax.ShapeDtypeStruct((rows, 2), jnp.int32),
+        shape_of(2, rows, f32),
+        shape_of(rows, 2, f32),
+        shape_of(1, features, f32),
+    ]
+
+    def body(own_ref, sib_ref, inputs_ref, out_grad_ref, *refs):
+        even, odd = refs[:5], refs[5:10]
+        state_ref, grad_ref, out_ref, sem = refs[10:]
+        state_in = pltpu.make_async_copy(inputs_ref.at[core_index()], state_ref, sem.at[0])
+        grad_in = pltpu.make_async_copy(out_grad_ref.at[core_index()], grad_ref, sem.at[1])
+        state_in.start()
+        grad_in.start()
+        for parity, (tt_ref, t_ref, gt_ref, g_ref, gain_ref) in ((0, even), (1, odd)):
+            chosen = jnp.where(core_index() == parity, own_ref[...], sib_ref[...])
+            gt_ref[...] = chosen[2:4]
+            at = slot_rows(chosen[0:2], experts, capacity)
+            for k in range(2):
+                tt_ref[k : k + 1, :] = at[k].astype(jnp.int32)
+                t_ref[:, k : k + 1] = as_column(at[k]).astype(jnp.int32)
+                g_ref[:, k : k + 1] = as_column(chosen[2 + k : 3 + k])
+            for i in range(features // rows):
+                gain_ref[:, i * rows : (i + 1) * rows] = chosen[4 + i : 5 + i]
+        state_in.wait()
+        grad_in.wait()
         is_last = chip_index() == last_chip
 
         @pl.when(is_last)
         def _():
-            hits = slot_hits(gtt_ref[...], slots)
+            hits = slot_hits(odd[0][...], slots)
             out_ref[...] = (
-                pack_rows(grad_ref[...], hits) * slot_gates(hits, ggt_ref[...])
+                pack_rows(grad_ref[...], hits) * slot_gates(hits, odd[2][...])
             ).astype(bf16)
 
         @pl.when(jnp.logical_not(is_last))
         def _():
-            normed = normalize(state_ref[...].astype(f32), gain_ref[...])
-            out_ref[...] = pack_rows(normed, slot_hits(tt_ref[...], slots)).astype(bf16)
-
-    return small_call(
-        body,
-        [shape_of(slots, state.shape[1])],
-        (state, gain, targets_t, grad, grad_targets_t, grad_gates_t),
-    )[0]
+            normed = normalize(state_ref[...].astype(f32), even[4][...])
+            out_ref[...] = pack_rows(normed, slot_hits(even[0][...], slots)).astype(bf16)
+
+    out_shapes = params + params + [shape_of(rows, features)] * 2 + [shape_of(slots, features)]
+    made = pl.pallas_call(
+        body,
+        out_shape=out_shapes,
+        in_specs=[vmem_spec, vmem_spec, any_spec, any_spec],
+        out_specs=[vmem_spec] * len(out_shapes),
+        scratch_shapes=[pltpu.SemaphoreType.DMA((2,))],
+        compiler_params=pltpu.CompilerParams(vmem_limit_bytes=small_limit),
+    )(own_small, sib_small, inputs, out_grad)
+    return made[:5], made[5:10], made[10], made[11], made[12]
 
 
 def select_pack(arrived, state, gain, targets_t, slots, chip):
@@ -290,7 +377,7 @@
             value, slope = gelu_parts(pre)
             active[at] = value.astype(bf16)
             if keep_slope:
-                slope_buf[at] = slope
+                slope_buf[at] = slope.astype(bf16)
                 slope_out.copy(slope_buf, slope_ref, i).start()
         for i, at in enumerate(down_tiles):
             down_in.copy(own_down, down_buf, i).wait()
@@ -315,8 +402,8 @@
         copy_slots(down_tiles),
     ]
     if keep_slope:
-        out_shapes.append(shape_of(slots, hidden, f32))
-        scratch += [pltpu.VMEM((slots, hidden), f32), copy_slots(up_tiles)]
+        out_shapes.append(shape_of(slots, hidden))
+        scratch += [pltpu.VMEM((slots, hidden), bf16), copy_slots(up_tiles)]
     return mlp_call(
         body,
         out_shapes,
@@ -370,7 +457,7 @@
                 g_ref[...], down_buf[at], contract_last, preferred_element_type=f32
             )
             slope_in.copy(slope_ref, slope_buf, i).wait()
-            pre_grad[slope_tiles[i]] = (act_grad * slope_buf[slope_tiles[i]]).astype(bf16)
+            pre_grad[slope_tiles[i]] = (act_grad * slope_buf[slope_tiles[i]].astype(f32)).astype(bf16)
         for i, at in enumerate(up_tiles):
             up_in.copy(own_up, up_buf, i).wait()
             out_buf[out_tiles[i]] = lax.dot_general(
@@ -402,7 +489,7 @@
         [
             pltpu.VMEM((features, hidden), bf16),
             pltpu.VMEM((hidden, features), bf16),
-            pltpu.VMEM((slots, hidden), f32),
+            pltpu.VMEM((slots, hidden), bf16),
             pltpu.VMEM((slots, hidden), bf16),
             pltpu.VMEM((slots, features), bf16),
             pltpu.VMEM((slots, features), bf16),
@@ -486,7 +573,7 @@
                 rows_in.wait()
             pre = jnp.dot(x_ref[...], up_buf[at], preferred_element_type=f32)
             value, slope = gelu_parts(pre)
-            slope_buf[at] = slope
+            slope_buf[at] = slope.astype(bf16)
             active_buf[at] = value.astype(bf16)
             slope_out.copy(slope_buf, slope_ref, i).start()
             active_out.copy(active_buf, active_ref, i).start()
@@ -505,12 +592,12 @@
 
     return mlp_call(
         body,
-        [shape_of(slots, features), shape_of(slots, hidden, f32), shape_of(slots, hidden)],
+        [shape_of(slots, features), shape_of(slots, hidden), shape_of(slots, hidden)],
         (rows, weights[0], weights[2], act_grad),
         [
             pltpu.VMEM((features, hidden), bf16),
             pltpu.VMEM((slots, hidden), f32),
-            pltpu.VMEM((slots, hidden), f32),
+            pltpu.VMEM((slots, hidden), bf16),
             pltpu.VMEM((slots, hidden), bf16),
             pltpu.VMEM((slots, hidden), bf16),
             pltpu.VMEM((slots, features), bf16),
@@ -527,17 +614,6 @@
     )
 
 
-def slot_targets(picks_t, experts, capacity):
-    rows = picks_t.shape[1]
-    onehot = (picks_t[:, :, None] == jnp.arange(experts, dtype=jnp.int32)[None, None, :])
-    named = jnp.sum(onehot.astype(f32), axis=0).astype(bf16)
-    at = jnp.arange(rows, dtype=jnp.int32)
-    earlier = (at[None, :] < at[:, None]).astype(bf16)
-    rank = jnp.dot(earlier, named, preferred_element_type=f32)
-    rank_of_pick = jnp.sum(jnp.where(onehot, rank[None], 0.0), axis=2).astype(jnp.int32)
-    return picks_t * capacity + rank_of_pick
-
-
 def local(inputs, norm_gain, w_up, w_down, expert_ids, gates, out_grad):
     sections = lax.axis_size("section")
     experts = lax.axis_size("expert")
@@ -559,35 +635,21 @@
     def to_experts(x):
         return lax.all_to_all(x, "expert", split_axis=0, concat_axis=0, tiled=True)
 
-    folds = features // rows_dev
-    small = [
-        jnp.concatenate(
-            [
-                expert_ids[0, m].T.astype(f32),
-                gates[0, m].T,
-                norm_gain[0].reshape(folds, rows_dev),
-            ]
-        )
-        for m in range(2)
-    ]
-    own_small = jnp.where(core == 0, small[0], small[1])
-    sib_small = swap_cores(jnp.where(core == 0, small[1], small[0]))
-    params = []
-    for parity in range(2):
-        chosen = jnp.where(core == parity, own_small, sib_small)
-        targets_t = slot_targets(chosen[:2].astype(jnp.int32), experts, capacity)
-        gates_t = chosen[2:4]
-        gain = chosen[4:].reshape(1, features)
-        params.append((targets_t, targets_t.T, gates_t, gates_t.T, gain))
-    (even_tt, even_t, even_gt, even_g, even_gain) = params[0]
-    (odd_tt, odd_t, odd_gt, odd_g, odd_gain) = params[1]
-
-    state = jnp.where(core == 0, inputs[0], inputs[1])
-    last_grad = jnp.where(core == 0, out_grad[0], out_grad[1])
+    own_small, to_send = gather_params(
+        jnp.swapaxes(expert_ids[0], 1, 2),
+        jnp.swapaxes(gates[0], 1, 2),
+        norm_gain[0].reshape(features // rows_dev, rows_dev),
+    )
+    sib_small = swap_cores(to_send)
     own_up, own_down = w_up[0, 0], w_down[0, 0]
-    weights = (own_up, own_down, swap_cores(own_up), swap_cores(own_down))
-
-    send = first_pack(state, even_gain, even_tt, last_grad, odd_tt, odd_gt, slots, last)
+    sib_small, up_to_send, down_to_send = lax.optimization_barrier((sib_small, own_up, own_down))
+    weights = (own_up, own_down, swap_cores(up_to_send), swap_cores(down_to_send))
+
+    even, odd, state, last_grad, send = prepare_pack(
+        own_small, sib_small, inputs, out_grad, experts, capacity, last
+    )
+    (even_tt, even_t, even_gt, even_g, even_gain) = even
+    (odd_tt, odd_t, odd_gt, odd_g, odd_gain) = odd
     odd_out = None
     act_grad = None
     for turn in range(chips):

time: 378 us -> 373 us (0.987)
  blocking collectives: 193 us -> 231 us
  waiting for transfers between devices: 84.3 us -> 48.9 us
  starting transfers between devices: 22.7 us -> 15.5 us
    all_to_all x9 -> x11, blocking collectives: 193 us -> 231 us  [to_experts(): return lax.all_to_all(x, 'expert', split_axis=0, concat_axis=0, tiled=True)]
    all_to_all x5 -> x3, waiting for transfers between devices: 70.8 us -> 37.2 us  [to_experts(): return lax.all_to_all(x, 'expert', split_axis=0, concat_axis=0, tiled=True)]
    all_to_all x5 -> x3, starting transfers between devices: 18.6 us -> 11.4 us  [to_experts(): return lax.all_to_all(x, 'expert', split_axis=0, concat_axis=0, tiled=True)]
    pallas_call x11 -> x10, Pallas kernels: 8.95 us -> 8.43 us  [small_call(): pl.pallas_call(body, out_shape=out_shapes, in_specs=[vmem_spec] * len(arg...]
  transfers between devices with their start and end apart: 12 -> 10, of which waited for: 9 -> 7; matrix products, arithmetic and copies ran while one was open for 3% -> 2% of each run, Pallas kernels for 2% -> 2%
where the time goes in v3:
time: 373 us; the launch traced here: 372 us
  blocking collectives  231 us (62%)
  Pallas kernels  62.7 us (17%)
  waiting for transfers between devices  48.9 us (13%)
  starting transfers between devices  15.5 us (4%)
  matrix products  6.29 us (2%)
  local copies, waits for them, and re-layouts  4.48 us (1%)
    all_to_all x11, blocking collectives, to_experts(): return lax.all_to_all(x, 'expert', split_axis=0, concat_axis=0, tiled=True)  231 us
    pallas_call x8, Pallas kernels, mlp_call(): pl.pallas_call(body, out_shape=out_shapes, in_specs=[any_spec] * len(arra...  52.1 us
    all_to_all x3, waiting for transfers between devices, to_experts(): return lax.all_to_all(x, 'expert', split_axis=0, concat_axis=0, tiled=True)  37.2 us
    all_to_all x3, starting transfers between devices, to_experts(): return lax.all_to_all(x, 'expert', split_axis=0, concat_axis=0, tiled=True)  11.4 us
    ppermute x2, waiting for transfers between devices, shift_chips(): lax.ppermute(x, 'section', [(s, (s + 2 * by) % sections) for s in range(s...  10 us
    pallas_call x10, Pallas kernels, small_call(): pl.pallas_call(body, out_shape=out_shapes, in_specs=[vmem_spec] * len(arg...  8.43 us
  transfers between devices with their start and end apart: 10, of which 7 were waited for; matrix products, arithmetic and copies ran while one was open for 2% of the time, Pallas kernels for 2%

profile of v3, /device:TPU:0, one launch (start us, length us, event | category | flops | bytes accessed | tf_op | source)
XLA Modules:
  0.0 371.7 jit_solution(1441357419783092495)
XLA Ops:
  0.6 1.3 shard_map.86
  2.0 0.5 collective-permute-start
  2.5 1.0 collective-permute-done.sib_ref
  3.5 0.3 collective-permute-start.2
  3.9 0.2 collective-permute-start.1
  4.1 0.0 copy-start
  4.1 1.0 copy-done
  5.1 0.0 copy-start.1
  5.1 1.0 copy-done.1
  6.1 0.0 copy-start.2
  6.1 0.7 copy-done.2
  6.8 0.8 shard_map.87
  7.6 25.1 %all_to_all.154 = bf16[8,40,1024]{2,1,0:T(8,128)(2,1)} all-to-all(bf16[8,40,1024]{2,1,0:T(8,128)(2,1)S(1)} %bitcast.56), channel_id=1, replica_groups=mesh['section'=4,'expert'=8] {'expert'}, dimensions={0} | all-to-all | bytes 1310720 | tf_op jit(solution)/shard_map/all_to_all | solution.py:636
  32.7 0.0 collective-permute-done.2.sib_down.refs_3_.refs_4_
  32.7 0.0 collective-permute-done.1.sib_up.refs_2_.refs_3_
  32.7 6.5 %shard_map.88 = bf16[320,1024]{1,0:T(8,128)(2,1)} custom-call(bf16[320,1024]{1,0:T(8,128)(2,1)} %bitcast.77, bf16[1024,2048]{1,0:T(8,128)(2,1)} %bitcast.62, bf16[2048,1024]{1,0:T(8,128)(2,1)} %bitcast.70, bf16[1024,2048]{1,0:T(8,128)(2,1)} %collective-permute-done.1.sib_up.refs_2_.refs_3_, bf16[2048,1024]{1,0:T(8,128)(2,1)} %collective-permute-done.2.sib_down.refs_3_.refs_4_), custom_call_target="tpu_custom_call" | custom-call | flops 2684354560 | bytes 9699328 | tf_op jit(solution)/shard_map/pallas_call | solution.py:331
  39.2 20.8 %all_to_all.155 = bf16[8,40,1024]{2,1,0:T(8,128)(2,1)S(1)} all-to-all(bf16[8,40,1024]{2,1,0:T(8,128)(2,1)} %bitcast.89), channel_id=1, replica_groups=mesh['section'=4,'expert'=8] {'expert'}, dimensions={0} | all-to-all | bytes 1310720 | tf_op jit(solution)/shard_map/all_to_all | solution.py:636
  60.0 0.9 shard_map.89
  60.9 20.4 %all_to_all.156 = bf16[8,40,1024]{2,1,0:T(8,128)(2,1)} all-to-all(bf16[8,40,1024]{2,1,0:T(8,128)(2,1)S(1)} %bitcast.60), channel_id=1, replica_groups=mesh['section'=4,'expert'=8] {'expert'}, dimensions={0} | all-to-all | bytes 1310720 | tf_op jit(solution)/shard_map/all_to_all | solution.py:636
  81.3 6.5 %shard_map.90 = bf16[320,1024]{1,0:T(8,128)(2,1)} custom-call(bf16[320,1024]{1,0:T(8,128)(2,1)} %bitcast.86, bf16[1024,2048]{1,0:T(8,128)(2,1)} %bitcast.63, bf16[2048,1024]{1,0:T(8,128)(2,1)} %bitcast.71, bf16[1024,2048]{1,0:T(8,128)(2,1)} %collective-permute-done.1.sib_up.refs_2_.refs_3_, bf16[2048,1024]{1,0:T(8,128)(2,1)} %collective-permute-done.2.sib_down.refs_3_.refs_4_), custom_call_target="tpu_custom_call" | custom-call | flops 2684354560 | bytes 9699328 | tf_op jit(solution)/shard_map/pallas_call | solution.py:331
  87.7 20.5 %all_to_all.157 = bf16[8,40,1024]{2,1,0:T(8,128)(2,1)S(1)} all-to-all(bf16[8,40,1024]{2,1,0:T(8,128)(2,1)} %bitcast.87), channel_id=1, replica_groups=mesh['section'=4,'expert'=8] {'expert'}, dimensions={0} | all-to-all | bytes 1310720 | tf_op jit(solution)/shard_map/all_to_all | solution.py:636
  108.2 0.5 shard_map.91
  108.7 1.5 collective-permute-start.3
  110.1 5.0 %collective-permute-done.3.arrived_ref = bf16[128,1024]{1,0:T(8,128)(2,1)S(1)} collective-permute-done((bf16[128,1024]{1,0:T(8,128)(2,1)S(1)}, bf16[128,1024]{1,0:T(8,128)(2,1)S(1)}, u32[]{:S(2)}, u32[]{:S(2)}) %collective-permute-start.3) | collective-permute-done | bytes 262176 | tf_op jit(solution)/shard_map/ppermute | solution.py:631
  115.1 0.5 shard_map.92
  115.6 20.6 %all_to_all.158 = bf16[8,40,1024]{2,1,0:T(8,128)(2,1)} all-to-all(bf16[8,40,1024]{2,1,0:T(8,128)(2,1)S(1)} %bitcast.58), channel_id=1, replica_groups=mesh['section'=4,'expert'=8] {'expert'}, dimensions={0} | all-to-all | bytes 1310720 | tf_op jit(solution)/shard_map/all_to_all | solution.py:636
  136.2 7.3 %shard_map.93 = (bf16[320,1024]{1,0:T(8,128)(2,1)}, bf16[320,2048]{1,0:T(8,128)(2,1)}) custom-call(bf16[320,1024]{1,0:T(8,128)(2,1)} %bitcast.83, bf16[1024,2048]{1,0:T(8,128)(2,1)} %bitcast.64, bf16[2048,1024]{1,0:T(8,128)(2,1)} %bitcast.72, bf16[1024,2048]{1,0:T(8,128)(2,1)} %collective-permute-done.1.sib_up.refs_2_.refs_3_, ...), custom_call_target="tpu_custom_call" | custom-call | flops 2684354560 | bytes 12320768 | tf_op jit(solution)/shard_map/pallas_call | solution.py:331
  143.5 20.5 %all_to_all.159 = bf16[8,40,1024]{2,1,0:T(8,128)(2,1)S(1)} all-to-all(bf16[8,40,1024]{2,1,0:T(8,128)(2,1)} %bitcast.91), channel_id=1, replica_groups=mesh['section'=4,'expert'=8] {'expert'}, dimensions={0} | all-to-all | bytes 1310720 | tf_op jit(solution)/shard_map/all_to_all | solution.py:636
  164.0 1.8 shard_map.94
  165.7 3.5 all-to-all-start.6
  169.3 4.7 %shard_map.95.ag_ref = f32[320,2048]{1,0:T(8,128)} custom-call(bf16[320,1024]{1,0:T(8,128)(2,1)} %bitcast.78, bf16[2048,1024]{1,0:T(8,128)(2,1)} %bitcast.73, bf16[2048,1024]{1,0:T(8,128)(2,1)} %collective-permute-done.2.sib_down.refs_3_.refs_4_), custom_call_target="tpu_custom_call" | custom-call | flops 1342177280 | bytes 6815744 | tf_op jit(solution)/shard_map/pallas_call | solution.py:331
  174.0 11.8 %all-to-all-done.6 = bf16[8,40,1024]{2,1,0:T(8,128)(2,1)S(1)} async-done(((bf16[8,40,1024]{2,1,0:T(8,128)(2,1)}), bf16[8,40,1024]{2,1,0:T(8,128)(2,1)S(1)}, u32[]{:S(2)}, u32[]{:S(2)}) %all-to-all-start.6) | async-done | bytes 655392 | tf_op jit(solution)/shard_map/all_to_all | solution.py:636
  185.8 0.0 copy-start.4
  185.8 0.9 copy-done.4
  186.7 7.4 %shard_map.96 = (bf16[320,1024]{1,0:T(8,128)(2,1)}, bf16[320,2048]{1,0:T(8,128)(2,1)}, bf16[320,2048]{1,0:T(8,128)(2,1)}) custom-call(bf16[320,1024]{1,0:T(8,128)(2,1)} %bitcast.81, bf16[1024,2048]{1,0:T(8,128)(2,1)} %bitcast.65, bf16[1024,2048]{1,0:T(8,128)(2,1)} %collective-permute-done.1.sib_up.refs_2_.refs_3_, f32[320,2048]{1,0:T(8,128)} %shard_map.95.ag_ref), custom_call_target="tpu_custom_call" | custom-call | flops 2684354560 | bytes 10747904 | tf_op jit(solution)/shard_map/pallas_call | solution.py:331
  194.0 21.3 %all_to_all.160 = bf16[8,40,1024]{2,1,0:T(8,128)(2,1)S(1)} all-to-all(bf16[8,40,1024]{2,1,0:T(8,128)(2,1)} %bitcast.90), channel_id=1, replica_groups=mesh['section'=4,'expert'=8] {'expert'}, dimensions={0} | all-to-all | bytes 1310720 | tf_op jit(solution)/shard_map/all_to_all | solution.py:636
  215.3 0.9 shard_map.97
  216.3 20.6 %all_to_all.161 = bf16[8,40,1024]{2,1,0:T(8,128)(2,1)} all-to-all(bf16[8,40,1024]{2,1,0:T(8,128)(2,1)S(1)} %bitcast.59), channel_id=1, replica_groups=mesh['section'=4,'expert'=8] {'expert'}, dimensions={0} | all-to-all | bytes 1310720 | tf_op jit(solution)/shard_map/all_to_all | solution.py:636
  236.9 6.6 %shard_map.98 = bf16[320,1024]{1,0:T(8,128)(2,1)} custom-call(bf16[320,1024]{1,0:T(8,128)(2,1)} %bitcast.85, bf16[1024,2048]{1,0:T(8,128)(2,1)} %bitcast.66, bf16[2048,1024]{1,0:T(8,128)(2,1)} %bitcast.74, bf16[1024,2048]{1,0:T(8,128)(2,1)} %collective-permute-done.1.sib_up.refs_2_.refs_3_, ...), custom_call_target="tpu_custom_call" | custom-call | flops 2684354560 | bytes 12320768 | tf_op jit(solution)/shard_map/pallas_call | solution.py:331
  243.5 20.6 %all_to_all.162 = bf16[8,40,1024]{2,1,0:T(8,128)(2,1)S(1)} all-to-all(bf16[8,40,1024]{2,1,0:T(8,128)(2,1)} %bitcast.88), channel_id=1, replica_groups=mesh['section'=4,'expert'=8] {'expert'}, dimensions={0} | all-to-all | bytes 1310720 | tf_op jit(solution)/shard_map/all_to_all | solution.py:636
  264.1 0.6 shard_map.99
  264.7 1.5 collective-permute-start.4
  266.1 5.0 %collective-permute-done.4.up_ref = bf16[128,1024]{1,0:T(8,128)(2,1)S(1)} collective-permute-done((bf16[128,1024]{1,0:T(8,128)(2,1)S(1)}, bf16[128,1024]{1,0:T(8,128)(2,1)S(1)}, u32[]{:S(2)}, u32[]{:S(2)}) %collective-permute-start.4) | collective-permute-done | bytes 262176 | tf_op jit(solution)/shard_map/ppermute | solution.py:631
  271.2 1.2 shard_map.100
  272.4 4.3 %all-to-all-start.10 = ((bf16[8,40,1024]{2,1,0:T(8,128)(2,1)}), bf16[8,40,1024]{2,1,0:T(8,128)(2,1)S(1)}, u32[]{:S(2)}, u32[]{:S(2)}) async-start(bf16[8,40,1024]{2,1,0:T(8,128)(2,1)} %bitcast.27), calls=%async_computation.10 | async-start | bytes 1310720 | tf_op jit(solution)/shard_map/all_to_all | solution.py:636
  276.7 6.3 %fusion.3.refs_0_ = bf16[320,1024]{1,0:T(8,128)(2,1)} fusion(bf16[320,2048]{1,0:T(8,128)(2,1)} %get-tuple-element.64, bf16[2048,1024]{1,0:T(8,128)(2,1)} %collective-permute-done.2.sib_down.refs_3_.refs_4_, pred[]{:T(512)S(6)} %eq.22, bf16[1,1,2048,1024]{3,2,1,0:T(8,128)(2,1)} %param.10), kind=kOutput, calls=%fused_computation.3 | convolution fusion | flops 1344602112 | bytes 10354689 | tf_op jit(solution)/shard_map/dot_general | solution.py:679
  283.0 9.6 %all-to-all-done.10 = bf16[8,40,1024]{2,1,0:T(8,128)(2,1)S(1)} async-done(((bf16[8,40,1024]{2,1,0:T(8,128)(2,1)}), bf16[8,40,1024]{2,1,0:T(8,128)(2,1)S(1)}, u32[]{:S(2)}, u32[]{:S(2)}) %all-to-all-start.10) | async-done | bytes 655392 | tf_op jit(solution)/shard_map/all_to_all | solution.py:636
  292.6 0.8 copy-done.3
  293.5 6.7 %shard_map.101 = bf16[320,1024]{1,0:T(8,128)(2,1)} custom-call(bf16[320,1024]{1,0:T(8,128)(2,1)} %bitcast.80, bf16[320,1024]{1,0:T(8,128)(2,1)} %fusion.3.refs_0_, bf16[1024,2048]{1,0:T(8,128)(2,1)} %bitcast.67, bf16[2048,1024]{1,0:T(8,128)(2,1)} %bitcast.75, bf16[1024,2048]{1,0:T(8,128)(2,1)} %collective-permute-done.1.sib_up.refs_2_.refs_3_, ...), custom_call_target="tpu_custom_call" | custom-call | flops 2684354560 | bytes 12320768 | tf_op jit(solution)/shard_map/pallas_call | solution.py:331
  300.1 20.4 %all_to_all.163 = bf16[8,40,1024]{2,1,0:T(8,128)(2,1)S(1)} all-to-all(bf16[8,40,1024]{2,1,0:T(8,128)(2,1)} %bitcast.84), channel_id=1, replica_groups=mesh['section'=4,'expert'=8] {'expert'}, dimensions={0} | all-to-all | bytes 1310720 | tf_op jit(solution)/shard_map/all_to_all | solution.py:636
  320.6 0.9 shard_map.103
  321.5 20.4 %all_to_all.164 = bf16[8,40,1024]{2,1,0:T(8,128)(2,1)} all-to-all(bf16[8,40,1024]{2,1,0:T(8,128)(2,1)S(1)} %bitcast.57), channel_id=1, replica_groups=mesh['section'=4,'expert'=8] {'expert'}, dimensions={0} | all-to-all | bytes 1310720 | tf_op jit(solution)/shard_map/all_to_all | solution.py:636
  341.9 6.6 %shard_map.104 = bf16[320,1024]{1,0:T(8,128)(2,1)} custom-call(bf16[320,1024]{1,0:T(8,128)(2,1)} %bitcast.82, bf16[1024,2048]{1,0:T(8,128)(2,1)} %bitcast.68, bf16[2048,1024]{1,0:T(8,128)(2,1)} %bitcast.76, bf16[1024,2048]{1,0:T(8,128)(2,1)} %collective-permute-done.1.sib_up.refs_2_.refs_3_, ...), custom_call_target="tpu_custom_call" | custom-call | flops 2684354560 | bytes 12320768 | tf_op jit(solution)/shard_map/pallas_call | solution.py:331
  348.5 3.6 all-to-all-start.13
  352.0 0.5 shard_map.102
  352.6 0.1 collective-permute-start.5
  352.7 15.9 %all-to-all-done.13 = bf16[8,40,1024]{2,1,0:T(8,128)(2,1)S(1)} async-done(((bf16[8,40,1024]{2,1,0:T(8,128)(2,1)}), bf16[8,40,1024]{2,1,0:T(8,128)(2,1)S(1)}, u32[]{:S(2)}, u32[]{:S(2)}) %all-to-all-start.13) | async-done | bytes 655392 | tf_op jit(solution)/shard_map/all_to_all | solution.py:636
  368.6 0.6 shard_map.105
  369.2 0.1 select_bitcast_fusion
  369.3 0.1 collective-permute-start.6
  369.3 0.0 collective-permute-done.5
  369.3 0.9 maximum_select_fusion
  370.2 0.6 collective-permute-done.6
  370.9 0.9 maximum_select_fusion.1
  (2 shorter events, 0.1 us)
Async XLA Ops:
  2.0 1.6 collective-permute-start
  3.5 29.2 %collective-permute-start.2 = (bf16[2048,1024]{1,0:T(8,128)(2,1)}, bf16[2048,1024]{1,0:T(8,128)(2,1)}, u32[]{:S(2)}, u32[]{:S(2)}) collective-permute-start(bf16[2048,1024]{1,0:T(8,128)(2,1)} %bitcast.69), channel_id=1, source_target_pairs={{0,8},{8,0},{16,24},{24,16},{1,9},{9,1},{17,25},{25,17},{2,10},{10... | collective-permute-start | bytes 12582920 | tf_op jit(solution)/shard_map/ppermute | solution.py:628
  3.9 28.8 %collective-permute-start.1 = (bf16[1024,2048]{1,0:T(8,128)(2,1)}, bf16[1024,2048]{1,0:T(8,128)(2,1)}, u32[]{:S(2)}, u32[]{:S(2)}) collective-permute-start(bf16[1024,2048]{1,0:T(8,128)(2,1)} %bitcast.61), channel_id=1, source_target_pairs={{0,8},{8,0},{16,24},{24,16},{1,9},{9,1},{17,25},{25,17},{2,10},{10... | collective-permute-start | bytes 12582920 | tf_op jit(solution)/shard_map/ppermute | solution.py:628
  4.1 1.0 copy-start
  5.1 1.0 copy-start.1
  6.1 0.7 copy-start.2
  108.7 6.4 %collective-permute-start.3 = (bf16[128,1024]{1,0:T(8,128)(2,1)S(1)}, bf16[128,1024]{1,0:T(8,128)(2,1)S(1)}, u32[]{:S(2)}, u32[]{:S(2)}) collective-permute-start(bf16[128,1024]{1,0:T(8,128)(2,1)S(1)} %shard_map.91), channel_id=1, source_target_pairs={{0,16},{8,24},{16,0},{24,8},{1,17},{9,25},{17,1},{25,9},{2,18},{10... | collective-permute-start | bytes 786440 | tf_op jit(solution)/shard_map/ppermute | solution.py:631
  165.7 20.1 %all-to-all-start.6 = ((bf16[8,40,1024]{2,1,0:T(8,128)(2,1)}), bf16[8,40,1024]{2,1,0:T(8,128)(2,1)S(1)}, u32[]{:S(2)}, u32[]{:S(2)}) async-start(bf16[8,40,1024]{2,1,0:T(8,128)(2,1)} %bitcast.19), calls=%async_computation.6 | async-start | bytes 1310720 | tf_op jit(solution)/shard_map/all_to_all | solution.py:636
  185.8 0.9 copy-start.4
  264.7 6.5 %collective-permute-start.4 = (bf16[128,1024]{1,0:T(8,128)(2,1)S(1)}, bf16[128,1024]{1,0:T(8,128)(2,1)S(1)}, u32[]{:S(2)}, u32[]{:S(2)}) collective-permute-start(bf16[128,1024]{1,0:T(8,128)(2,1)S(1)} %shard_map.99), channel_id=1, source_target_pairs={{0,16},{8,24},{16,0},{24,8},{1,17},{9,25},{17,1},{25,9},{2,18},{10... | collective-permute-start | bytes 786440 | tf_op jit(solution)/shard_map/ppermute | solution.py:631
  272.4 20.2 %all-to-all-start.10 = ((bf16[8,40,1024]{2,1,0:T(8,128)(2,1)}), bf16[8,40,1024]{2,1,0:T(8,128)(2,1)S(1)}, u32[]{:S(2)}, u32[]{:S(2)}) async-start(bf16[8,40,1024]{2,1,0:T(8,128)(2,1)} %bitcast.27), calls=%async_computation.10 | async-start | bytes 1310720 | tf_op jit(solution)/shard_map/all_to_all | solution.py:636
  292.6 0.9 copy-start.3
  348.5 20.1 %all-to-all-start.13 = ((bf16[8,40,1024]{2,1,0:T(8,128)(2,1)}), bf16[8,40,1024]{2,1,0:T(8,128)(2,1)S(1)}, u32[]{:S(2)}, u32[]{:S(2)}) async-start(bf16[8,40,1024]{2,1,0:T(8,128)(2,1)} %bitcast.79), calls=%async_computation.13 | async-start | bytes 1310720 | tf_op jit(solution)/shard_map/all_to_all | solution.py:636
  352.6 16.7 %collective-permute-start.5 = (bf16[128,1024]{1,0:T(8,128)(2,1)S(1)}, bf16[128,1024]{1,0:T(8,128)(2,1)S(1)}, u32[]{:S(2)}, u32[]{:S(2)}) collective-permute-start(bf16[128,1024]{1,0:T(8,128)(2,1)S(1)} %get-tuple-element.71), channel_id=1, source_target_pairs={{0,8},{8,0},{16,24},{24,16},{1,9},{9,1},{17,25},{25,17},{2,10},{10... | collective-permute-start | bytes 786440 | tf_op jit(solution)/shard_map/ppermute | solution.py:628
  369.3 1.6 collective-permute-start.6

commit v4 on v3

--- a/solution.py
+++ b/solution.py
@@ -72,14 +72,17 @@
     return jnp.sum(total, axis=1, keepdims=True)
 
 
-def small_call(body, out_shapes, args):
+def small_call(body, out_shapes, args, earlier=()):
+    def with_earlier(*refs):
+        body(*refs[: len(args)], *refs[len(args) + len(earlier) :])
+
     return pl.pallas_call(
-        body,
+        with_earlier,
         out_shape=out_shapes,
-        in_specs=[vmem_spec] * len(args),
+        in_specs=[vmem_spec] * len(args) + [any_spec] * len(earlier),
         out_specs=[vmem_spec] * len(out_shapes),
         compiler_params=pltpu.CompilerParams(vmem_limit_bytes=small_limit),
-    )(*args)
+    )(*args, *earlier)
 
 
 def shape_of(rows, columns, kind=bf16):
@@ -140,8 +143,8 @@
     ]
 
 
-def prepare_pack(own_small, sib_small, inputs, out_grad, experts, capacity, last_chip):
-    rows, features = inputs.shape[1:]
+def prepare_pack(own_small, sib_small, state, out_grad, experts, capacity, last_chip):
+    rows, features = state.shape
     slots = experts * capacity
     params = [
         jax.ShapeDtypeStruct((2, rows), jnp.int32),
@@ -151,13 +154,8 @@
         shape_of(1, features, f32),
     ]
 
-    def body(own_ref, sib_ref, inputs_ref, out_grad_ref, *refs):
-        even, odd = refs[:5], refs[5:10]
-        state_ref, grad_ref, out_ref, sem = refs[10:]
-        state_in = pltpu.make_async_copy(inputs_ref.at[core_index()], state_ref, sem.at[0])
-        grad_in = pltpu.make_async_copy(out_grad_ref.at[core_index()], grad_ref, sem.at[1])
-        state_in.start()
-        grad_in.start()
+    def body(own_ref, sib_ref, state_ref, grad_ref, *refs):
+        even, odd, out_ref = refs[:5], refs[5:10], refs[10]
         for parity, (tt_ref, t_ref, gt_ref, g_ref, gain_ref) in ((0, even), (1, odd)):
             chosen = jnp.where(core_index() == parity, own_ref[...], sib_ref[...])
             gt_ref[...] = chosen[2:4]
@@ -168,8 +166,6 @@
                 g_ref[:, k : k + 1] = as_column(chosen[2 + k : 3 + k])
             for i in range(features // rows):
                 gain_ref[:, i * rows : (i + 1) * rows] = chosen[4 + i : 5 + i]
-        state_in.wait()
-        grad_in.wait()
         is_last = chip_index() == last_chip
 
         @pl.when(is_last)
@@ -184,16 +180,9 @@
             normed = normalize(state_ref[...].astype(f32), even[4][...])
             out_ref[...] = pack_rows(normed, slot_hits(even[0][...], slots)).astype(bf16)
 
-    out_shapes = params + params + [shape_of(rows, features)] * 2 + [shape_of(slots, features)]
-    made = pl.pallas_call(
-        body,
-        out_shape=out_shapes,
-        in_specs=[vmem_spec, vmem_spec, any_spec, any_spec],
-        out_specs=[vmem_spec] * len(out_shapes),
-        scratch_shapes=[pltpu.SemaphoreType.DMA((2,))],
-        compiler_params=pltpu.CompilerParams(vmem_limit_bytes=small_limit),
-    )(own_small, sib_small, inputs, out_grad)
-    return made[:5], made[5:10], made[10], made[11], made[12]
+    out_shapes = params + params + [shape_of(slots, features)]
+    made = small_call(body, out_shapes, (own_small, sib_small, state, out_grad))
+    return made[:5], made[5:10], made[10]
 
 
 def select_pack(arrived, state, gain, targets_t, slots, chip):
@@ -230,7 +219,7 @@
     return small_call(body, [shape_of(*state.shape)], (returned, state, targets, gates))[0]
 
 
-def combine_pack(returned, state, targets, gates, gain, targets_t):
+def combine_pack(returned, state, targets, gates, gain, targets_t, earlier=()):
     slots = returned.shape[0]
 
     def body(ret_ref, state_ref, t_ref, g_ref, gain_ref, tt_ref, state_out, out_ref):
@@ -243,6 +232,7 @@
         body,
         [shape_of(*state.shape), shape_of(slots, state.shape[1])],
         (returned, state, targets, gates, gain, targets_t),
+        earlier,
     )
 
 
@@ -268,7 +258,9 @@
     )[0]
 
 
-def grad_combine_pack(returned, upstream, state, targets, gain, targets_t, gates_t):
+def grad_combine_pack(
+    returned, upstream, state, targets, gain, targets_t, gates_t, earlier=()
+):
     slots = returned.shape[0]
 
     def body(ret_ref, up_ref, state_ref, t_ref, gain_ref, tt_ref, gt_ref, grad_out, out_ref):
@@ -281,6 +273,7 @@
         body,
         [shape_of(*state.shape), shape_of(slots, state.shape[1])],
         (returned, upstream, state, targets, gain, targets_t, gates_t),
+        earlier,
     )
 
 
@@ -641,12 +634,16 @@
         norm_gain[0].reshape(features // rows_dev, rows_dev),
     )
     sib_small = swap_cores(to_send)
+    state = jnp.where(core == 0, inputs[0], inputs[1])
+    last_grad = jnp.where(core == 0, out_grad[0], out_grad[1])
     own_up, own_down = w_up[0, 0], w_down[0, 0]
-    sib_small, up_to_send, down_to_send = lax.optimization_barrier((sib_small, own_up, own_down))
+    sib_small, state, last_grad, up_to_send, down_to_send = lax.optimization_barrier(
+        (sib_small, state, last_grad, own_up, own_down)
+    )
     weights = (own_up, own_down, swap_cores(up_to_send), swap_cores(down_to_send))
 
-    even, odd, state, last_grad, send = prepare_pack(
-        own_small, sib_small, inputs, out_grad, experts, capacity, last
+    even, odd, send = prepare_pack(
+        own_small, sib_small, state, last_grad, experts, capacity, last
     )
     (even_tt, even_t, even_gt, even_g, even_gain) = even
     (odd_tt, odd_t, odd_gt, odd_g, odd_gain) = odd
@@ -664,7 +661,9 @@
         returned = to_experts(outputs)
         if turn == 0:
             act_grad = act_gradient(received, weights, 1)
-        middle, send = combine_pack(returned, state, even_t, even_g, odd_gain, odd_tt)
+        middle, send = combine_pack(
+            returned, state, even_t, even_g, odd_gain, odd_tt, (act_grad[:8, :128],) if turn == last else ()
+        )
         received = to_experts(send)
         if turn < last:
             (outputs,) = expert_forward(received, weights, 1, False)
@@ -697,7 +696,8 @@
                 final_out = combine(returned, middle, odd_t, odd_g)
                 odd_out = jnp.where(chip == last, final_out, odd_out)
         odd_now, send = grad_combine_pack(
-            returned, upstream, middle, odd_t, odd_gain, even_tt, even_gt
+            returned, upstream, middle, odd_t, odd_gain, even_tt, even_gt,
+            (odd_down,) if turn == last else (),
         )
         odd_grad = odd_now if odd_grad is None else jnp.where(chip == turn, odd_now, odd_grad)
         received = to_experts(send)

time: 373 us -> 369 us (0.989)
    unnamed x10 -> x4, local copies, waits for them, and re-layouts: 4.48 us -> 0.7 us
  transfers between devices with their start and end apart: 10 -> 10, of which waited for: 7 -> 6; matrix products, arithmetic and copies ran while one was open for 2% -> 2% of each run, Pallas kernels for 2% -> 2%
where the time goes in v4:
time: 369 us; the launch traced here: 368 us
  blocking collectives  233 us (63%)
  Pallas kernels  60.9 us (17%)
  waiting for transfers between devices  48.9 us (13%)
  starting transfers between devices  15.1 us (4%)
  matrix products  5.36 us (1%)
    all_to_all x11, blocking collectives, to_experts(): return lax.all_to_all(x, 'expert', split_axis=0, concat_axis=0, tiled=True)  233 us
    pallas_call x8, Pallas kernels, mlp_call(): pl.pallas_call(body, out_shape=out_shapes, in_specs=[any_spec] * len(arra...  52.1 us
    all_to_all x3, waiting for transfers between devices, to_experts(): return lax.all_to_all(x, 'expert', split_axis=0, concat_axis=0, tiled=True)  38.1 us
    all_to_all x3, starting transfers between devices, to_experts(): return lax.all_to_all(x, 'expert', split_axis=0, concat_axis=0, tiled=True)  10.9 us
    ppermute x2, waiting for transfers between devices, shift_chips(): lax.ppermute(x, 'section', [(s, (s + 2 * by) % sections) for s in range(s...  10.1 us
    pallas_call x11, Pallas kernels, small_call(): pl.pallas_call(with_earlier, out_shape=out_shapes, in_specs=[vmem_spec] *...  7.46 us
  transfers between devices with their start and end apart: 10, of which 6 were waited for; matrix products, arithmetic and copies ran while one was open for 2% of the time, Pallas kernels for 2%

profile of v4, /device:TPU:0, one launch (start us, length us, event | category | flops | bytes accessed | tf_op | source)
XLA Modules:
  0.0 368.3 jit_solution(12025573721949343634)
XLA Ops:
  0.6 1.3 shard_map.86
  2.0 0.5 collective-permute-start
  2.5 1.2 select_bitcast_fusion.2
  3.8 0.0 collective-permute-done.refs_1_
  3.8 0.1 collective-permute-start.1
  3.9 0.4 collective-permute-start.2
  4.3 0.0 copy-start.1
  4.3 0.7 copy-done.1
  5.0 0.7 shard_map.87
  5.8 25.1 %all_to_all.154 = bf16[8,40,1024]{2,1,0:T(8,128)(2,1)} all-to-all(bf16[8,40,1024]{2,1,0:T(8,128)(2,1)S(1)} %bitcast.61), channel_id=1, replica_groups=mesh['section'=4,'expert'=8] {'expert'}, dimensions={0} | all-to-all | bytes 1310720 | tf_op jit(solution)/shard_map/all_to_all | solution.py:629
  30.9 0.0 collective-permute-done.1.sib_up.refs_2_.refs_3_
  30.9 0.0 collective-permute-done.2.sib_down.refs_3_.refs_4_
  30.9 6.5 %shard_map.88 = bf16[320,1024]{1,0:T(8,128)(2,1)} custom-call(bf16[320,1024]{1,0:T(8,128)(2,1)} %bitcast.83, bf16[1024,2048]{1,0:T(8,128)(2,1)} %bitcast.68, bf16[2048,1024]{1,0:T(8,128)(2,1)} %bitcast.76, bf16[1024,2048]{1,0:T(8,128)(2,1)} %collective-permute-done.1.sib_up.refs_2_.refs_3_, bf16[2048,1024]{1,0:T(8,128)(2,1)} %collective-permute-done.2.sib_down.refs_3_.refs_4_), custom_call_target="tpu_custom_call" | custom-call | flops 2684354560 | bytes 9699328 | tf_op jit(solution)/shard_map/pallas_call | solution.py:324
  37.3 21.2 %all_to_all.155 = bf16[8,40,1024]{2,1,0:T(8,128)(2,1)S(1)} all-to-all(bf16[8,40,1024]{2,1,0:T(8,128)(2,1)} %bitcast.95), channel_id=1, replica_groups=mesh['section'=4,'expert'=8] {'expert'}, dimensions={0} | all-to-all | bytes 1310720 | tf_op jit(solution)/shard_map/all_to_all | solution.py:629
  58.5 0.9 shard_map.89
  59.4 20.7 %all_to_all.156 = bf16[8,40,1024]{2,1,0:T(8,128)(2,1)} all-to-all(bf16[8,40,1024]{2,1,0:T(8,128)(2,1)S(1)} %bitcast.66), channel_id=1, replica_groups=mesh['section'=4,'expert'=8] {'expert'}, dimensions={0} | all-to-all | bytes 1310720 | tf_op jit(solution)/shard_map/all_to_all | solution.py:629
  80.1 6.4 %shard_map.90 = bf16[320,1024]{1,0:T(8,128)(2,1)} custom-call(bf16[320,1024]{1,0:T(8,128)(2,1)} %bitcast.92, bf16[1024,2048]{1,0:T(8,128)(2,1)} %bitcast.69, bf16[2048,1024]{1,0:T(8,128)(2,1)} %bitcast.77, bf16[1024,2048]{1,0:T(8,128)(2,1)} %collective-permute-done.1.sib_up.refs_2_.refs_3_, bf16[2048,1024]{1,0:T(8,128)(2,1)} %collective-permute-done.2.sib_down.refs_3_.refs_4_), custom_call_target="tpu_custom_call" | custom-call | flops 2684354560 | bytes 9699328 | tf_op jit(solution)/shard_map/pallas_call | solution.py:324
  86.5 20.6 %all_to_all.157 = bf16[8,40,1024]{2,1,0:T(8,128)(2,1)S(1)} all-to-all(bf16[8,40,1024]{2,1,0:T(8,128)(2,1)} %bitcast.93), channel_id=1, replica_groups=mesh['section'=4,'expert'=8] {'expert'}, dimensions={0} | all-to-all | bytes 1310720 | tf_op jit(solution)/shard_map/all_to_all | solution.py:629
  107.1 0.5 shard_map.91
  107.6 1.5 collective-permute-start.3
  109.1 5.1 %collective-permute-done.3.refs_0_ = bf16[128,1024]{1,0:T(8,128)(2,1)S(1)} collective-permute-done((bf16[128,1024]{1,0:T(8,128)(2,1)S(1)}, bf16[128,1024]{1,0:T(8,128)(2,1)S(1)}, u32[]{:S(2)}, u32[]{:S(2)}) %collective-permute-start.3) | collective-permute-done | bytes 262176 | tf_op jit(solution)/shard_map/ppermute | solution.py:624
  114.2 0.5 shard_map.92
  114.6 20.5 %all_to_all.158 = bf16[8,40,1024]{2,1,0:T(8,128)(2,1)} all-to-all(bf16[8,40,1024]{2,1,0:T(8,128)(2,1)S(1)} %bitcast.64), channel_id=1, replica_groups=mesh['section'=4,'expert'=8] {'expert'}, dimensions={0} | all-to-all | bytes 1310720 | tf_op jit(solution)/shard_map/all_to_all | solution.py:629
  135.1 7.3 %shard_map.93 = (bf16[320,1024]{1,0:T(8,128)(2,1)}, bf16[320,2048]{1,0:T(8,128)(2,1)}) custom-call(bf16[320,1024]{1,0:T(8,128)(2,1)} %bitcast.89, bf16[1024,2048]{1,0:T(8,128)(2,1)} %bitcast.70, bf16[2048,1024]{1,0:T(8,128)(2,1)} %bitcast.78, bf16[1024,2048]{1,0:T(8,128)(2,1)} %collective-permute-done.1.sib_up.refs_2_.refs_3_, ...), custom_call_target="tpu_custom_call" | custom-call | flops 2684354560 | bytes 12320768 | tf_op jit(solution)/shard_map/pallas_call | solution.py:324
  142.4 3.6 all-to-all-start.5
  146.0 4.8 %shard_map.94.ag_ref = f32[320,2048]{1,0:T(8,128)} custom-call(bf16[320,1024]{1,0:T(8,128)(2,1)} %bitcast.84, bf16[2048,1024]{1,0:T(8,128)(2,1)} %bitcast.79, bf16[2048,1024]{1,0:T(8,128)(2,1)} %collective-permute-done.2.sib_down.refs_3_.refs_4_), custom_call_target="tpu_custom_call" | custom-call | flops 1342177280 | bytes 6815744 | tf_op jit(solution)/shard_map/pallas_call | solution.py:324
  150.8 0.7 slice.20.refs_6_
  151.5 11.1 %all-to-all-done.5 = bf16[8,40,1024]{2,1,0:T(8,128)(2,1)S(1)} async-done(((bf16[8,40,1024]{2,1,0:T(8,128)(2,1)}), bf16[8,40,1024]{2,1,0:T(8,128)(2,1)S(1)}, u32[]{:S(2)}, u32[]{:S(2)}) %all-to-all-start.5) | async-done | bytes 655392 | tf_op jit(solution)/shard_map/all_to_all | solution.py:629
  162.5 0.9 shard_map.95
  163.5 21.2 %all_to_all.159 = bf16[8,40,1024]{2,1,0:T(8,128)(2,1)} all-to-all(bf16[8,40,1024]{2,1,0:T(8,128)(2,1)S(1)} %bitcast.63), channel_id=1, replica_groups=mesh['section'=4,'expert'=8] {'expert'}, dimensions={0} | all-to-all | bytes 1310720 | tf_op jit(solution)/shard_map/all_to_all | solution.py:629
  184.7 7.4 %shard_map.96 = (bf16[320,1024]{1,0:T(8,128)(2,1)}, bf16[320,2048]{1,0:T(8,128)(2,1)}, bf16[320,2048]{1,0:T(8,128)(2,1)}) custom-call(bf16[320,1024]{1,0:T(8,128)(2,1)} %bitcast.86, bf16[1024,2048]{1,0:T(8,128)(2,1)} %bitcast.71, bf16[1024,2048]{1,0:T(8,128)(2,1)} %collective-permute-done.1.sib_up.refs_2_.refs_3_, f32[320,2048]{1,0:T(8,128)} %shard_map.94.ag_ref), custom_call_target="tpu_custom_call" | custom-call | flops 2684354560 | bytes 10747904 | tf_op jit(solution)/shard_map/pallas_call | solution.py:324
  192.1 3.8 %all-to-all-start.7 = ((bf16[8,40,1024]{2,1,0:T(8,128)(2,1)}), bf16[8,40,1024]{2,1,0:T(8,128)(2,1)S(1)}, u32[]{:S(2)}, u32[]{:S(2)}) async-start(bf16[8,40,1024]{2,1,0:T(8,128)(2,1)} %bitcast.96), calls=%async_computation.7 | async-start | bytes 1310720 | tf_op jit(solution)/shard_map/all_to_all | solution.py:629
  195.8 5.4 %fusion.3.refs_7_.refs_0_ = bf16[320,1024]{1,0:T(8,128)(2,1)S(1)} fusion(bf16[320,2048]{1,0:T(8,128)(2,1)} %get-tuple-element.60, bf16[2048,1024]{1,0:T(8,128)(2,1)} %collective-permute-done.2.sib_down.refs_3_.refs_4_, pred[]{:T(512)S(6)} %eq.12, bf16[1,1,2048,1024]{3,2,1,0:T(8,128)(2,1)} %param.10), kind=kOutput, calls=%fused_computation.3 | convolution fusion | flops 1344602112 | bytes 10354689 | tf_op jit(solution)/shard_map/dot_general | solution.py:678
  201.2 0.0 copy-start
  201.2 11.2 %all-to-all-done.7 = bf16[8,40,1024]{2,1,0:T(8,128)(2,1)S(1)} async-done(((bf16[8,40,1024]{2,1,0:T(8,128)(2,1)}), bf16[8,40,1024]{2,1,0:T(8,128)(2,1)S(1)}, u32[]{:S(2)}, u32[]{:S(2)}) %all-to-all-start.7) | async-done | bytes 655392 | tf_op jit(solution)/shard_map/all_to_all | solution.py:629
  212.4 0.9 shard_map.97
  213.4 21.3 %all_to_all.160 = bf16[8,40,1024]{2,1,0:T(8,128)(2,1)} all-to-all(bf16[8,40,1024]{2,1,0:T(8,128)(2,1)S(1)} %bitcast.65), channel_id=1, replica_groups=mesh['section'=4,'expert'=8] {'expert'}, dimensions={0} | all-to-all | bytes 1310720 | tf_op jit(solution)/shard_map/all_to_all | solution.py:629
  234.7 6.6 %shard_map.98 = bf16[320,1024]{1,0:T(8,128)(2,1)} custom-call(bf16[320,1024]{1,0:T(8,128)(2,1)} %bitcast.91, bf16[1024,2048]{1,0:T(8,128)(2,1)} %bitcast.72, bf16[2048,1024]{1,0:T(8,128)(2,1)} %bitcast.80, bf16[1024,2048]{1,0:T(8,128)(2,1)} %collective-permute-done.1.sib_up.refs_2_.refs_3_, ...), custom_call_target="tpu_custom_call" | custom-call | flops 2684354560 | bytes 12320768 | tf_op jit(solution)/shard_map/pallas_call | solution.py:324
  241.3 0.0 copy-done
  241.3 20.8 %all_to_all.161 = bf16[8,40,1024]{2,1,0:T(8,128)(2,1)S(1)} all-to-all(bf16[8,40,1024]{2,1,0:T(8,128)(2,1)} %bitcast.94), channel_id=1, replica_groups=mesh['section'=4,'expert'=8] {'expert'}, dimensions={0} | all-to-all | bytes 1310720 | tf_op jit(solution)/shard_map/all_to_all | solution.py:629
  262.1 0.6 shard_map.99
  262.7 1.5 collective-permute-start.4
  264.2 5.1 %collective-permute-done.4.refs_0_.refs_1_ = bf16[128,1024]{1,0:T(8,128)(2,1)S(1)} collective-permute-done((bf16[128,1024]{1,0:T(8,128)(2,1)S(1)}, bf16[128,1024]{1,0:T(8,128)(2,1)S(1)}, u32[]{:S(2)}, u32[]{:S(2)}) %collective-permute-start.4) | collective-permute-done | bytes 262176 | tf_op jit(solution)/shard_map/ppermute | solution.py:624
  269.3 0.3 shard_map.100
  269.6 20.4 %all_to_all.162 = bf16[8,40,1024]{2,1,0:T(8,128)(2,1)} all-to-all(bf16[8,40,1024]{2,1,0:T(8,128)(2,1)S(1)} %bitcast.60), channel_id=1, replica_groups=mesh['section'=4,'expert'=8] {'expert'}, dimensions={0} | all-to-all | bytes 1310720 | tf_op jit(solution)/shard_map/all_to_all | solution.py:629
  290.1 6.7 %shard_map.101 = bf16[320,1024]{1,0:T(8,128)(2,1)} custom-call(bf16[320,1024]{1,0:T(8,128)(2,1)} %bitcast.87, bf16[320,1024]{1,0:T(8,128)(2,1)} %copy-done, bf16[1024,2048]{1,0:T(8,128)(2,1)} %bitcast.73, bf16[2048,1024]{1,0:T(8,128)(2,1)} %bitcast.81, bf16[1024,2048]{1,0:T(8,128)(2,1)} %collective-permute-done.1.sib_up.refs_2_.refs_3_, ...), custom_call_target="tpu_custom_call" | custom-call | flops 2684354560 | bytes 12320768 | tf_op jit(solution)/shard_map/pallas_call | solution.py:324
  296.7 20.5 %all_to_all.163 = bf16[8,40,1024]{2,1,0:T(8,128)(2,1)S(1)} all-to-all(bf16[8,40,1024]{2,1,0:T(8,128)(2,1)} %bitcast.90), channel_id=1, replica_groups=mesh['section'=4,'expert'=8] {'expert'}, dimensions={0} | all-to-all | bytes 1310720 | tf_op jit(solution)/shard_map/all_to_all | solution.py:629
  317.2 0.9 shard_map.103
  318.1 20.3 %all_to_all.164 = bf16[8,40,1024]{2,1,0:T(8,128)(2,1)} all-to-all(bf16[8,40,1024]{2,1,0:T(8,128)(2,1)S(1)} %bitcast.62), channel_id=1, replica_groups=mesh['section'=4,'expert'=8] {'expert'}, dimensions={0} | all-to-all | bytes 1310720 | tf_op jit(solution)/shard_map/all_to_all | solution.py:629
  338.5 6.6 %shard_map.104 = bf16[320,1024]{1,0:T(8,128)(2,1)} custom-call(bf16[320,1024]{1,0:T(8,128)(2,1)} %bitcast.88, bf16[1024,2048]{1,0:T(8,128)(2,1)} %bitcast.74, bf16[2048,1024]{1,0:T(8,128)(2,1)} %bitcast.82, bf16[1024,2048]{1,0:T(8,128)(2,1)} %collective-permute-done.1.sib_up.refs_2_.refs_3_, ...), custom_call_target="tpu_custom_call" | custom-call | flops 2684354560 | bytes 12320768 | tf_op jit(solution)/shard_map/pallas_call | solution.py:324
  345.0 3.6 all-to-all-start.13
  348.6 0.5 shard_map.102
  349.1 0.1 select_bitcast_fusion.1
  349.2 0.1 collective-permute-start.5
  349.3 15.9 %all-to-all-done.13 = bf16[8,40,1024]{2,1,0:T(8,128)(2,1)S(1)} async-done(((bf16[8,40,1024]{2,1,0:T(8,128)(2,1)}), bf16[8,40,1024]{2,1,0:T(8,128)(2,1)S(1)}, u32[]{:S(2)}, u32[]{:S(2)}) %all-to-all-start.13) | async-done | bytes 655392 | tf_op jit(solution)/shard_map/all_to_all | solution.py:629
  365.1 0.6 shard_map.105
  365.7 0.1 select_bitcast_fusion
  365.8 0.1 collective-permute-start.6
  365.9 0.0 collective-permute-done.5
  365.9 0.9 maximum_select_fusion
  366.8 0.6 collective-permute-done.6
  367.4 0.9 maximum_select_fusion.1
Async XLA Ops:
  2.0 1.8 collective-permute-start
  3.8 27.1 %collective-permute-start.1 = (bf16[1024,2048]{1,0:T(8,128)(2,1)}, bf16[1024,2048]{1,0:T(8,128)(2,1)}, u32[]{:S(2)}, u32[]{:S(2)}) collective-permute-start(bf16[1024,2048]{1,0:T(8,128)(2,1)} %bitcast.67), channel_id=1, source_target_pairs={{0,8},{8,0},{16,24},{24,16},{1,9},{9,1},{17,25},{25,17},{2,10},{10... | collective-permute-start | bytes 12582920 | tf_op jit(solution)/shard_map/ppermute | solution.py:621
  3.9 27.0 %collective-permute-start.2 = (bf16[2048,1024]{1,0:T(8,128)(2,1)}, bf16[2048,1024]{1,0:T(8,128)(2,1)}, u32[]{:S(2)}, u32[]{:S(2)}) collective-permute-start(bf16[2048,1024]{1,0:T(8,128)(2,1)} %bitcast.75), channel_id=1, source_target_pairs={{0,8},{8,0},{16,24},{24,16},{1,9},{9,1},{17,25},{25,17},{2,10},{10... | collective-permute-start | bytes 12582920 | tf_op jit(solution)/shard_map/ppermute | solution.py:621
  4.3 0.7 copy-start.1
  107.6 6.5 %collective-permute-start.3 = (bf16[128,1024]{1,0:T(8,128)(2,1)S(1)}, bf16[128,1024]{1,0:T(8,128)(2,1)S(1)}, u32[]{:S(2)}, u32[]{:S(2)}) collective-permute-start(bf16[128,1024]{1,0:T(8,128)(2,1)S(1)} %shard_map.91), channel_id=1, source_target_pairs={{0,16},{8,24},{16,0},{24,8},{1,17},{9,25},{17,1},{25,9},{2,18},{10... | collective-permute-start | bytes 786440 | tf_op jit(solution)/shard_map/ppermute | solution.py:624
  142.4 20.1 %all-to-all-start.5 = ((bf16[8,40,1024]{2,1,0:T(8,128)(2,1)}), bf16[8,40,1024]{2,1,0:T(8,128)(2,1)S(1)}, u32[]{:S(2)}, u32[]{:S(2)}) async-start(bf16[8,40,1024]{2,1,0:T(8,128)(2,1)} %bitcast.97), calls=%async_computation.5 | async-start | bytes 1310720 | tf_op jit(solution)/shard_map/all_to_all | solution.py:629
  192.1 20.4 %all-to-all-start.7 = ((bf16[8,40,1024]{2,1,0:T(8,128)(2,1)}), bf16[8,40,1024]{2,1,0:T(8,128)(2,1)S(1)}, u32[]{:S(2)}, u32[]{:S(2)}) async-start(bf16[8,40,1024]{2,1,0:T(8,128)(2,1)} %bitcast.96), calls=%async_computation.7 | async-start | bytes 1310720 | tf_op jit(solution)/shard_map/all_to_all | solution.py:629
  201.2 40.1 %copy-start = (bf16[320,1024]{1,0:T(8,128)(2,1)}, bf16[320,1024]{1,0:T(8,128)(2,1)S(1)}, u32[]{:S(2)}) copy-start(bf16[320,1024]{1,0:T(8,128)(2,1)S(1)} %fusion.3.refs_7_.refs_0_) | copy-start | bytes 1966084
  262.7 6.6 %collective-permute-start.4 = (bf16[128,1024]{1,0:T(8,128)(2,1)S(1)}, bf16[128,1024]{1,0:T(8,128)(2,1)S(1)}, u32[]{:S(2)}, u32[]{:S(2)}) collective-permute-start(bf16[128,1024]{1,0:T(8,128)(2,1)S(1)} %shard_map.99), channel_id=1, source_target_pairs={{0,16},{8,24},{16,0},{24,8},{1,17},{9,25},{17,1},{25,9},{2,18},{10... | collective-permute-start | bytes 786440 | tf_op jit(solution)/shard_map/ppermute | solution.py:624
  345.0 20.1 %all-to-all-start.13 = ((bf16[8,40,1024]{2,1,0:T(8,128)(2,1)}), bf16[8,40,1024]{2,1,0:T(8,128)(2,1)S(1)}, u32[]{:S(2)}, u32[]{:S(2)}) async-start(bf16[8,40,1024]{2,1,0:T(8,128)(2,1)} %bitcast.85), calls=%async_computation.13 | async-start | bytes 1310720 | tf_op jit(solution)/shard_map/all_to_all | solution.py:629
  349.2 16.7 %collective-permute-start.5 = (bf16[128,1024]{1,0:T(8,128)(2,1)S(1)}, bf16[128,1024]{1,0:T(8,128)(2,1)S(1)}, u32[]{:S(2)}, u32[]{:S(2)}) collective-permute-start(bf16[128,1024]{1,0:T(8,128)(2,1)S(1)} %get-tuple-element.71), channel_id=1, source_target_pairs={{0,8},{8,0},{16,24},{24,16},{1,9},{9,1},{17,25},{25,17},{2,10},{10... | collective-permute-start | bytes 786440 | tf_op jit(solution)/shard_map/ppermute | solution.py:621
  365.8 1.6 collective-permute-start.6

commit v5 on v4

--- a/solution.py
+++ b/solution.py
@@ -18,15 +18,15 @@
 feature_cut = 512
 small_limit = 12 * 1024 * 1024
 mlp_limit = 60 * 1024 * 1024
+rows_limit = 52 * 1024 * 1024
 
 
 def gelu_parts(pre):
     square = pre * pre
-    tangent = jnp.tanh(gelu_coef * pre * (1.0 + cubic_coef * square))
-    half = 0.5 * (1.0 + tangent)
-    slope = half + 0.5 * pre * (1.0 - tangent * tangent) * gelu_coef * (
-        1.0 + 3.0 * cubic_coef * square
-    )
+    tangent = jnp.tanh(pre * (gelu_coef + (gelu_coef * cubic_coef) * square))
+    half = 0.5 + 0.5 * tangent
+    bend = (0.5 * gelu_coef) + (1.5 * gelu_coef * cubic_coef) * square
+    slope = half + pre * (1.0 - tangent * tangent) * bend
     return pre * half, slope
 
 
@@ -320,14 +320,15 @@
     return [(cut, slice(None)) for cut in cuts(size, width)]
 
 
-def mlp_call(body, out_shapes, arrays, scratch, flops, moved):
+def mlp_call(body, out_shapes, arrays, scratch, flops, moved, at_hand=False):
+    first = vmem_spec if at_hand else any_spec
     return pl.pallas_call(
         body,
         out_shape=out_shapes,
-        in_specs=[any_spec] * len(arrays),
-        out_specs=[any_spec] * len(out_shapes),
+        in_specs=[first] + [any_spec] * (len(arrays) - 1),
+        out_specs=[first] + [any_spec] * (len(out_shapes) - 1),
         scratch_shapes=scratch,
-        compiler_params=pltpu.CompilerParams(vmem_limit_bytes=mlp_limit),
+        compiler_params=pltpu.CompilerParams(vmem_limit_bytes=rows_limit if at_hand else mlp_limit),
         cost_estimate=pl.CostEstimate(flops=flops, bytes_accessed=moved, transcendentals=0),
     )(*arrays)
 
@@ -341,15 +342,12 @@
     hidden = weights[0].shape[1]
     up_tiles, down_tiles = column_tiles(hidden, forward_cut), column_tiles(features, feature_cut)
 
-    def body(rows_ref, own_up, own_down, sib_up, sib_down, out_ref, *refs):
+    def body(x_ref, own_up, own_down, sib_up, sib_down, out_ref, *refs):
         if keep_slope:
             slope_ref, refs = refs[0], refs[1:]
             slope_buf, slope_sem = refs[-2:]
             slope_out = TileCopies(up_tiles, slope_sem)
-        up_buf, down_buf, active, x_ref, out_buf, up_sem, down_sem, x_sem, out_sem = refs[:9]
-        rows_in = pltpu.make_async_copy(rows_ref, x_ref, x_sem)
-        rows_in.start()
-        rows_out = TileCopies(down_tiles, out_sem)
+        up_buf, down_buf, active, up_sem, down_sem = refs[:5]
         up_in, down_in = TileCopies(up_tiles, up_sem), TileCopies(down_tiles, down_sem)
 
         def begin_up(up):
@@ -364,7 +362,6 @@
         for i, at in enumerate(up_tiles):
             up_in.copy(own_up, up_buf, i).wait()
             if i == 0:
-                rows_in.wait()
                 start_from(parity, (own_down,), (sib_down,), begin_down)
             pre = jnp.dot(x_ref[...], up_buf[at], preferred_element_type=f32)
             value, slope = gelu_parts(pre)
@@ -374,10 +371,7 @@
                 slope_out.copy(slope_buf, slope_ref, i).start()
         for i, at in enumerate(down_tiles):
             down_in.copy(own_down, down_buf, i).wait()
-            out_buf[at] = jnp.dot(active[...], down_buf[at], preferred_element_type=f32).astype(bf16)
-            rows_out.copy(out_buf, out_ref, i).start()
-        for i in range(len(down_tiles)):
-            rows_out.copy(out_buf, out_ref, i).wait()
+            out_ref[at] = jnp.dot(active[...], down_buf[at], preferred_element_type=f32).astype(bf16)
         if keep_slope:
             for i in range(len(up_tiles)):
                 slope_out.copy(slope_buf, slope_ref, i).wait()
@@ -387,11 +381,7 @@
         pltpu.VMEM((features, hidden), bf16),
         pltpu.VMEM((hidden, features), bf16),
         pltpu.VMEM((slots, hidden), bf16),
-        pltpu.VMEM((slots, features), bf16),
-        pltpu.VMEM((slots, features), bf16),
         copy_slots(up_tiles),
-        copy_slots(down_tiles),
-        pltpu.SemaphoreType.DMA,
         copy_slots(down_tiles),
     ]
     if keep_slope:
@@ -404,6 +394,7 @@
         scratch,
         4 * slots * features * hidden,
         4 * features * hidden + 4 * slots * features + 4 * slots * hidden * int(keep_slope),
+        True,
     )
 
 
@@ -415,17 +406,14 @@
     out_tiles = column_tiles(features, feature_cut)
     arrays = (grads,) if other is None else (grads, other)
 
-    def body(grads_ref, *refs):
+    def body(g_ref, *refs):
         if other is not None:
             other_ref, refs = refs[0], refs[1:]
         own_up, own_down, sib_up, sib_down, slope_ref, out_ref = refs[:6]
-        up_buf, down_buf, slope_buf, pre_grad, g_ref, out_buf = refs[6:12]
-        up_sem, down_sem, slope_sem, g_sem, out_sem = refs[12:17]
+        up_buf, down_buf, slope_buf, pre_grad, up_sem, down_sem, slope_sem = refs[6:13]
         if other is not None:
-            other_buf = refs[17]
-        grads_in = pltpu.make_async_copy(grads_ref, g_ref, g_sem)
-        grads_in.start()
-        rows_out = TileCopies(out_tiles, out_sem)
+            other_buf, other_sem = refs[13:]
+            other_in = pltpu.make_async_copy(other_ref, other_buf, other_sem)
         up_in, down_in = TileCopies(up_tiles, up_sem), TileCopies(down_tiles, down_sem)
         slope_in = TileCopies(slope_tiles, slope_sem)
 
@@ -442,10 +430,9 @@
         for i, at in enumerate(down_tiles):
             down_in.copy(own_down, down_buf, i).wait()
             if i == 0:
-                grads_in.wait()
                 start_from(parity, (own_up,), (sib_up,), begin_up)
                 if other is not None:
-                    pltpu.make_async_copy(other_ref, other_buf, g_sem).start()
+                    other_in.start()
             act_grad = lax.dot_general(
                 g_ref[...], down_buf[at], contract_last, preferred_element_type=f32
             )
@@ -453,27 +440,15 @@
             pre_grad[slope_tiles[i]] = (act_grad * slope_buf[slope_tiles[i]].astype(f32)).astype(bf16)
         for i, at in enumerate(up_tiles):
             up_in.copy(own_up, up_buf, i).wait()
-            out_buf[out_tiles[i]] = lax.dot_general(
+            out_ref[out_tiles[i]] = lax.dot_general(
                 pre_grad[...], up_buf[at], contract_last, preferred_element_type=f32
             ).astype(bf16)
-            if other is None:
-                rows_out.copy(out_buf, out_ref, i).start()
-        if other is None:
-            for i in range(len(out_tiles)):
-                rows_out.copy(out_buf, out_ref, i).wait()
-        else:
-            whole = out_sem.at[0]
-            pltpu.make_async_copy(other_ref, other_buf, g_sem).wait()
+        if other is not None:
+            other_in.wait()
 
             @pl.when(chip_index() == other_chip)
             def _():
-                pltpu.make_async_copy(other_buf, out_ref, whole).start()
-
-            @pl.when(chip_index() != other_chip)
-            def _():
-                pltpu.make_async_copy(out_buf, out_ref, whole).start()
-
-            pltpu.make_async_copy(out_buf, out_ref, whole).wait()
+                out_ref[...] = other_buf[...]
 
     return mlp_call(
         body,
@@ -484,17 +459,14 @@
             pltpu.VMEM((hidden, features), bf16),
             pltpu.VMEM((slots, hidden), bf16),
             pltpu.VMEM((slots, hidden), bf16),
-            pltpu.VMEM((slots, features), bf16),
-            pltpu.VMEM((slots, features), bf16),
             copy_slots(up_tiles),
             copy_slots(down_tiles),
             copy_slots(slope_tiles),
-            pltpu.SemaphoreType.DMA,
-            copy_slots(out_tiles),
         ]
-        + ([] if other is None else [pltpu.VMEM((slots, features), bf16)]),
+        + ([] if other is None else [pltpu.VMEM((slots, features), bf16), pltpu.SemaphoreType.DMA]),
         4 * slots * features * hidden,
         4 * features * hidden + 4 * slots * features + 4 * slots * hidden,
+        True,
     )[0]
 
 

time: 369 us -> 367 us (level)
  Pallas kernels: 60.9 us -> 56.1 us
    pallas_call x8, Pallas kernels: 52.1 us -> 47.3 us  [mlp_call(): pl.pallas_call(body, out_shape=out_shapes, in_specs=[first] + [any_spec]...]
where the time goes in v5:
time: 367 us; the launch traced here: 366 us
  blocking collectives  231 us (63%)
  Pallas kernels  56.1 us (15%)
  waiting for transfers between devices  49.4 us (13%)
  starting transfers between devices  14.8 us (4%)
  matrix products  5.36 us (1%)
  local copies, waits for them, and re-layouts  4.67 us (1%)
    all_to_all x11, blocking collectives, to_experts(): return lax.all_to_all(x, 'expert', split_axis=0, concat_axis=0, tiled=True)  231 us
    pallas_call x8, Pallas kernels, mlp_call(): pl.pallas_call(body, out_shape=out_shapes, in_specs=[first] + [any_spec]...  47.3 us
    all_to_all x3, waiting for transfers between devices, to_experts(): return lax.all_to_all(x, 'expert', split_axis=0, concat_axis=0, tiled=True)  38.4 us
    all_to_all x3, starting transfers between devices, to_experts(): return lax.all_to_all(x, 'expert', split_axis=0, concat_axis=0, tiled=True)  10.7 us
    ppermute x2, waiting for transfers between devices, shift_chips(): lax.ppermute(x, 'section', [(s, (s + 2 * by) % sections) for s in range(s...  10.3 us
    pallas_call x11, Pallas kernels, small_call(): pl.pallas_call(with_earlier, out_shape=out_shapes, in_specs=[vmem_spec] *...  7.45 us
  transfers between devices with their start and end apart: 10, of which 6 were waited for; matrix products, arithmetic and copies ran while one was open for 2% of the time, Pallas kernels for 2%

profile of v5, /device:TPU:0, one launch (start us, length us, event | category | flops | bytes accessed | tf_op | source)
XLA Modules:
  0.0 365.7 jit_solution(9538190981237253753)
XLA Ops:
  0.6 1.3 shard_map.86
  2.0 0.5 collective-permute-start
  2.5 1.2 select_bitcast_fusion.2
  3.8 0.0 collective-permute-done.refs_1_
  3.8 0.1 collective-permute-start.1
  3.9 0.4 collective-permute-start.2
  4.3 0.0 copy-start.1
  4.3 0.7 copy-done.1
  5.0 0.7 shard_map.87
  5.8 25.0 %all_to_all.154 = bf16[8,40,1024]{2,1,0:T(8,128)(2,1)S(1)} all-to-all(bf16[8,40,1024]{2,1,0:T(8,128)(2,1)S(1)} %bitcast.72), channel_id=1, replica_groups=mesh['section'=4,'expert'=8] {'expert'}, dimensions={0} | all-to-all | bytes 1310720 | tf_op jit(solution)/shard_map/all_to_all | solution.py:601
  30.8 0.0 collective-permute-done.1.sib_up.refs_2_.refs_3_
  30.8 0.0 collective-permute-done.2.sib_down.refs_3_.refs_4_
  30.8 0.0 copy-start.3
  30.8 2.0 copy-done.3
  32.8 1.2 copy-done.2
  34.1 5.4 %shard_map.88 = bf16[320,1024]{1,0:T(8,128)(2,1)S(1)} custom-call(bf16[320,1024]{1,0:T(8,128)(2,1)S(1)} %bitcast.52, bf16[1024,2048]{1,0:T(8,128)(2,1)} %bitcast.79, bf16[2048,1024]{1,0:T(8,128)(2,1)} %bitcast.87, bf16[1024,2048]{1,0:T(8,128)(2,1)} %copy-done.2, bf16[2048,1024]{1,0:T(8,128)(2,1)} %copy-done.3), custom_call_target="tpu_custom_call" | custom-call | flops 2684354560 | bytes 9699328 | tf_op jit(solution)/shard_map/pallas_call | solution.py:325
  39.5 0.0 copy-done
  39.5 20.9 %all_to_all.155 = bf16[8,40,1024]{2,1,0:T(8,128)(2,1)S(1)} all-to-all(bf16[8,40,1024]{2,1,0:T(8,128)(2,1)S(1)} %bitcast.64), channel_id=1, replica_groups=mesh['section'=4,'expert'=8] {'expert'}, dimensions={0} | all-to-all | bytes 1310720 | tf_op jit(solution)/shard_map/all_to_all | solution.py:601
  60.4 0.9 shard_map.89
  61.3 20.6 %all_to_all.156 = bf16[8,40,1024]{2,1,0:T(8,128)(2,1)S(1)} all-to-all(bf16[8,40,1024]{2,1,0:T(8,128)(2,1)S(1)} %bitcast.77), channel_id=1, replica_groups=mesh['section'=4,'expert'=8] {'expert'}, dimensions={0} | all-to-all | bytes 1310720 | tf_op jit(solution)/shard_map/all_to_all | solution.py:601
  81.9 5.4 %shard_map.90 = bf16[320,1024]{1,0:T(8,128)(2,1)S(1)} custom-call(bf16[320,1024]{1,0:T(8,128)(2,1)S(1)} %bitcast.61, bf16[1024,2048]{1,0:T(8,128)(2,1)} %bitcast.80, bf16[2048,1024]{1,0:T(8,128)(2,1)} %bitcast.88, bf16[1024,2048]{1,0:T(8,128)(2,1)} %copy-done.2, bf16[2048,1024]{1,0:T(8,128)(2,1)} %copy-done.3), custom_call_target="tpu_custom_call" | custom-call | flops 2684354560 | bytes 9699328 | tf_op jit(solution)/shard_map/pallas_call | solution.py:325
  87.3 20.4 %all_to_all.157 = bf16[8,40,1024]{2,1,0:T(8,128)(2,1)S(1)} all-to-all(bf16[8,40,1024]{2,1,0:T(8,128)(2,1)S(1)} %bitcast.62), channel_id=1, replica_groups=mesh['section'=4,'expert'=8] {'expert'}, dimensions={0} | all-to-all | bytes 1310720 | tf_op jit(solution)/shard_map/all_to_all | solution.py:601
  107.7 0.5 shard_map.91
  108.2 1.5 collective-permute-start.3
  109.7 5.1 %collective-permute-done.3.refs_0_ = bf16[128,1024]{1,0:T(8,128)(2,1)S(1)} collective-permute-done((bf16[128,1024]{1,0:T(8,128)(2,1)S(1)}, bf16[128,1024]{1,0:T(8,128)(2,1)S(1)}, u32[]{:S(2)}, u32[]{:S(2)}) %collective-permute-start.3) | collective-permute-done | bytes 262176 | tf_op jit(solution)/shard_map/ppermute | solution.py:596
  114.8 0.5 shard_map.92
  115.3 20.3 %all_to_all.158 = bf16[8,40,1024]{2,1,0:T(8,128)(2,1)S(1)} all-to-all(bf16[8,40,1024]{2,1,0:T(8,128)(2,1)S(1)} %bitcast.75), channel_id=1, replica_groups=mesh['section'=4,'expert'=8] {'expert'}, dimensions={0} | all-to-all | bytes 1310720 | tf_op jit(solution)/shard_map/all_to_all | solution.py:601
  135.6 6.9 %shard_map.93 = (bf16[320,1024]{1,0:T(8,128)(2,1)}, bf16[320,2048]{1,0:T(8,128)(2,1)}) custom-call(bf16[320,1024]{1,0:T(8,128)(2,1)S(1)} %bitcast.58, bf16[1024,2048]{1,0:T(8,128)(2,1)} %bitcast.81, bf16[2048,1024]{1,0:T(8,128)(2,1)} %bitcast.89, bf16[1024,2048]{1,0:T(8,128)(2,1)} %copy-done.2, bf16[2048,1024]{1,0:T(8,128)(2,1)} %copy-done.3), custom_call_target="tpu_custom_call" | custom-call | flops 2684354560 | bytes 12320768 | tf_op jit(solution)/shard_map/pallas_call | solution.py:325
  142.5 3.6 all-to-all-start.5
  146.0 4.7 %shard_map.94.ag_ref = f32[320,2048]{1,0:T(8,128)} custom-call(bf16[320,1024]{1,0:T(8,128)(2,1)} %bitcast.53, bf16[2048,1024]{1,0:T(8,128)(2,1)} %bitcast.90, bf16[2048,1024]{1,0:T(8,128)(2,1)} %copy-done.3), custom_call_target="tpu_custom_call" | custom-call | flops 1342177280 | bytes 6815744 | tf_op jit(solution)/shard_map/pallas_call | solution.py:325
  150.8 0.7 slice.20.refs_6_
  151.5 11.1 %all-to-all-done.5 = bf16[8,40,1024]{2,1,0:T(8,128)(2,1)S(1)} async-done(((bf16[8,40,1024]{2,1,0:T(8,128)(2,1)}), bf16[8,40,1024]{2,1,0:T(8,128)(2,1)S(1)}, u32[]{:S(2)}, u32[]{:S(2)}) %all-to-all-start.5) | async-done | bytes 655392 | tf_op jit(solution)/shard_map/all_to_all | solution.py:601
  162.6 0.9 shard_map.95
  163.5 21.2 %all_to_all.159 = bf16[8,40,1024]{2,1,0:T(8,128)(2,1)} all-to-all(bf16[8,40,1024]{2,1,0:T(8,128)(2,1)S(1)} %bitcast.74), channel_id=1, replica_groups=mesh['section'=4,'expert'=8] {'expert'}, dimensions={0} | all-to-all | bytes 1310720 | tf_op jit(solution)/shard_map/all_to_all | solution.py:601
  184.7 7.1 %shard_map.96 = (bf16[320,1024]{1,0:T(8,128)(2,1)}, bf16[320,2048]{1,0:T(8,128)(2,1)}, bf16[320,2048]{1,0:T(8,128)(2,1)}) custom-call(bf16[320,1024]{1,0:T(8,128)(2,1)} %bitcast.94, bf16[1024,2048]{1,0:T(8,128)(2,1)} %bitcast.82, bf16[1024,2048]{1,0:T(8,128)(2,1)} %copy-done.2, f32[320,2048]{1,0:T(8,128)} %shard_map.94.ag_ref), custom_call_target="tpu_custom_call" | custom-call | flops 2684354560 | bytes 10747904 | tf_op jit(solution)/shard_map/pallas_call | solution.py:325
  191.8 3.6 all-to-all-start.7
  195.4 5.4 %fusion.3.refs_7_.refs_0_ = bf16[320,1024]{1,0:T(8,128)(2,1)S(1)} fusion(bf16[320,2048]{1,0:T(8,128)(2,1)} %get-tuple-element.60, bf16[2048,1024]{1,0:T(8,128)(2,1)} %copy-done.3, pred[]{:T(512)S(6)} %eq.12, bf16[1,1,2048,1024]{3,2,1,0:T(8,128)(2,1)} %param.10), kind=kOutput, calls=%fused_computation.3 | convolution fusion | flops 1344602112 | bytes 10354689 | tf_op jit(solution)/shard_map/dot_general | solution.py:650
  200.8 11.4 %all-to-all-done.7 = bf16[8,40,1024]{2,1,0:T(8,128)(2,1)S(1)} async-done(((bf16[8,40,1024]{2,1,0:T(8,128)(2,1)}), bf16[8,40,1024]{2,1,0:T(8,128)(2,1)S(1)}, u32[]{:S(2)}, u32[]{:S(2)}) %all-to-all-start.7) | async-done | bytes 655392 | tf_op jit(solution)/shard_map/all_to_all | solution.py:601
  212.2 0.9 shard_map.97
  213.2 21.2 %all_to_all.160 = bf16[8,40,1024]{2,1,0:T(8,128)(2,1)S(1)} all-to-all(bf16[8,40,1024]{2,1,0:T(8,128)(2,1)S(1)} %bitcast.76), channel_id=1, replica_groups=mesh['section'=4,'expert'=8] {'expert'}, dimensions={0} | all-to-all | bytes 1310720 | tf_op jit(solution)/shard_map/all_to_all | solution.py:601
  234.4 5.6 %shard_map.98 = bf16[320,1024]{1,0:T(8,128)(2,1)S(1)} custom-call(bf16[320,1024]{1,0:T(8,128)(2,1)S(1)} %bitcast.60, bf16[1024,2048]{1,0:T(8,128)(2,1)} %bitcast.83, bf16[2048,1024]{1,0:T(8,128)(2,1)} %bitcast.91, bf16[1024,2048]{1,0:T(8,128)(2,1)} %copy-done.2, bf16[2048,1024]{1,0:T(8,128)(2,1)} %copy-done.3, bf16[320,2048]{1,0:T(8,128)(2,1)} %get-tuple-element.62.refs_4_), custom_call_target="tpu_custom_call" | custom-call | flops 2684354560 | bytes 12320768 | tf_op jit(solution)/shard_map/pallas_call | solution.py:325
  240.0 20.6 %all_to_all.161 = bf16[8,40,1024]{2,1,0:T(8,128)(2,1)S(1)} all-to-all(bf16[8,40,1024]{2,1,0:T(8,128)(2,1)S(1)} %bitcast.63), channel_id=1, replica_groups=mesh['section'=4,'expert'=8] {'expert'}, dimensions={0} | all-to-all | bytes 1310720 | tf_op jit(solution)/shard_map/all_to_all | solution.py:601
  260.6 0.6 shard_map.99
  261.2 1.5 collective-permute-start.4
  262.6 5.1 %collective-permute-done.4.refs_0_.refs_1_ = bf16[128,1024]{1,0:T(8,128)(2,1)S(1)} collective-permute-done((bf16[128,1024]{1,0:T(8,128)(2,1)S(1)}, bf16[128,1024]{1,0:T(8,128)(2,1)S(1)}, u32[]{:S(2)}, u32[]{:S(2)}) %collective-permute-start.4) | collective-permute-done | bytes 262176 | tf_op jit(solution)/shard_map/ppermute | solution.py:596
  267.8 0.3 shard_map.100
  268.1 20.6 %all_to_all.162 = bf16[8,40,1024]{2,1,0:T(8,128)(2,1)S(1)} all-to-all(bf16[8,40,1024]{2,1,0:T(8,128)(2,1)S(1)} %bitcast.71), channel_id=1, replica_groups=mesh['section'=4,'expert'=8] {'expert'}, dimensions={0} | all-to-all | bytes 1310720 | tf_op jit(solution)/shard_map/all_to_all | solution.py:601
  288.7 5.8 %shard_map.101 = bf16[320,1024]{1,0:T(8,128)(2,1)S(1)} custom-call(bf16[320,1024]{1,0:T(8,128)(2,1)S(1)} %bitcast.56, bf16[320,1024]{1,0:T(8,128)(2,1)S(1)} %fusion.3.refs_7_.refs_0_, bf16[1024,2048]{1,0:T(8,128)(2,1)} %bitcast.84, bf16[2048,1024]{1,0:T(8,128)(2,1)} %bitcast.92, bf16[1024,2048]{1,0:T(8,128)(2,1)} %copy-done.2, bf16[2048,1024]{1,0:T(8,128)(2,1)} %copy-done.3, ...), custom_call_target="tpu_custom_call" | custom-call | flops 2684354560 | bytes 12320768 | tf_op jit(solution)/shard_map/pallas_call | solution.py:325
  294.5 20.3 %all_to_all.163 = bf16[8,40,1024]{2,1,0:T(8,128)(2,1)S(1)} all-to-all(bf16[8,40,1024]{2,1,0:T(8,128)(2,1)S(1)} %bitcast.59), channel_id=1, replica_groups=mesh['section'=4,'expert'=8] {'expert'}, dimensions={0} | all-to-all | bytes 1310720 | tf_op jit(solution)/shard_map/all_to_all | solution.py:601
  314.8 0.9 shard_map.103
  315.7 20.2 %all_to_all.164 = bf16[8,40,1024]{2,1,0:T(8,128)(2,1)S(1)} all-to-all(bf16[8,40,1024]{2,1,0:T(8,128)(2,1)S(1)} %bitcast.73), channel_id=1, replica_groups=mesh['section'=4,'expert'=8] {'expert'}, dimensions={0} | all-to-all | bytes 1310720 | tf_op jit(solution)/shard_map/all_to_all | solution.py:601
  336.0 6.5 %shard_map.104 = bf16[320,1024]{1,0:T(8,128)(2,1)} custom-call(bf16[320,1024]{1,0:T(8,128)(2,1)S(1)} %bitcast.57, bf16[1024,2048]{1,0:T(8,128)(2,1)} %bitcast.85, bf16[2048,1024]{1,0:T(8,128)(2,1)} %bitcast.93, bf16[1024,2048]{1,0:T(8,128)(2,1)} %copy-done.2, bf16[2048,1024]{1,0:T(8,128)(2,1)} %copy-done.3, bf16[320,2048]{1,0:T(8,128)(2,1)} %get-tuple-element.62.refs_4_), custom_call_target="tpu_custom_call" | custom-call | flops 2684354560 | bytes 12320768 | tf_op jit(solution)/shard_map/pallas_call | solution.py:325
  342.5 3.6 all-to-all-start.13
  346.0 0.5 shard_map.102
  346.5 0.1 select_bitcast_fusion.1
  346.6 0.1 collective-permute-start.5
  346.7 15.9 %all-to-all-done.13 = bf16[8,40,1024]{2,1,0:T(8,128)(2,1)S(1)} async-done(((bf16[8,40,1024]{2,1,0:T(8,128)(2,1)}), bf16[8,40,1024]{2,1,0:T(8,128)(2,1)S(1)}, u32[]{:S(2)}, u32[]{:S(2)}) %all-to-all-start.13) | async-done | bytes 655392 | tf_op jit(solution)/shard_map/all_to_all | solution.py:601
  362.6 0.6 shard_map.105
  363.2 0.1 select_bitcast_fusion
  363.2 0.1 collective-permute-start.6
  363.3 0.0 collective-permute-done.5
  363.3 0.9 maximum_select_fusion
  364.2 0.6 collective-permute-done.6
  364.8 0.9 maximum_select_fusion.1
  (2 shorter events, 0.0 us)
Async XLA Ops:
  2.0 1.8 collective-permute-start
  3.8 27.0 %collective-permute-start.1 = (bf16[1024,2048]{1,0:T(8,128)(2,1)}, bf16[1024,2048]{1,0:T(8,128)(2,1)S(1)}, u32[]{:S(2)}, u32[]{:S(2)}) collective-permute-start(bf16[1024,2048]{1,0:T(8,128)(2,1)} %bitcast.78), channel_id=1, source_target_pairs={{0,8},{8,0},{16,24},{24,16},{1,9},{9,1},{17,25},{25,17},{2,10},{10... | collective-permute-start | bytes 12582920 | tf_op jit(solution)/shard_map/ppermute | solution.py:593
  3.9 26.9 %collective-permute-start.2 = (bf16[2048,1024]{1,0:T(8,128)(2,1)}, bf16[2048,1024]{1,0:T(8,128)(2,1)S(1)}, u32[]{:S(2)}, u32[]{:S(2)}) collective-permute-start(bf16[2048,1024]{1,0:T(8,128)(2,1)} %bitcast.86), channel_id=1, source_target_pairs={{0,8},{8,0},{16,24},{24,16},{1,9},{9,1},{17,25},{25,17},{2,10},{10... | collective-permute-start | bytes 12582920 | tf_op jit(solution)/shard_map/ppermute | solution.py:593
  4.3 0.7 copy-start.1
  30.8 8.7 %copy-start = (bf16[8,40,1024]{2,1,0:T(8,128)(2,1)}, bf16[8,40,1024]{2,1,0:T(8,128)(2,1)S(1)}, u32[]{:S(2)}) copy-start(bf16[8,40,1024]{2,1,0:T(8,128)(2,1)S(1)} %all_to_all.154) | copy-start | bytes 1966084
  30.8 3.3 copy-start.2
  30.8 2.1 copy-start.3
  108.2 6.6 %collective-permute-start.3 = (bf16[128,1024]{1,0:T(8,128)(2,1)S(1)}, bf16[128,1024]{1,0:T(8,128)(2,1)S(1)}, u32[]{:S(2)}, u32[]{:S(2)}) collective-permute-start(bf16[128,1024]{1,0:T(8,128)(2,1)S(1)} %shard_map.91), channel_id=1, source_target_pairs={{0,16},{8,24},{16,0},{24,8},{1,17},{9,25},{17,1},{25,9},{2,18},{10... | collective-permute-start | bytes 786440 | tf_op jit(solution)/shard_map/ppermute | solution.py:596
  142.5 20.1 %all-to-all-start.5 = ((bf16[8,40,1024]{2,1,0:T(8,128)(2,1)}), bf16[8,40,1024]{2,1,0:T(8,128)(2,1)S(1)}, u32[]{:S(2)}, u32[]{:S(2)}) async-start(bf16[8,40,1024]{2,1,0:T(8,128)(2,1)} %bitcast.19), calls=%async_computation.5 | async-start | bytes 1310720 | tf_op jit(solution)/shard_map/all_to_all | solution.py:601
  191.8 20.4 %all-to-all-start.7 = ((bf16[8,40,1024]{2,1,0:T(8,128)(2,1)}), bf16[8,40,1024]{2,1,0:T(8,128)(2,1)S(1)}, u32[]{:S(2)}, u32[]{:S(2)}) async-start(bf16[8,40,1024]{2,1,0:T(8,128)(2,1)} %bitcast.95), calls=%async_computation.7 | async-start | bytes 1310720 | tf_op jit(solution)/shard_map/all_to_all | solution.py:601
  261.2 6.6 %collective-permute-start.4 = (bf16[128,1024]{1,0:T(8,128)(2,1)S(1)}, bf16[128,1024]{1,0:T(8,128)(2,1)S(1)}, u32[]{:S(2)}, u32[]{:S(2)}) collective-permute-start(bf16[128,1024]{1,0:T(8,128)(2,1)S(1)} %shard_map.99), channel_id=1, source_target_pairs={{0,16},{8,24},{16,0},{24,8},{1,17},{9,25},{17,1},{25,9},{2,18},{10... | collective-permute-start | bytes 786440 | tf_op jit(solution)/shard_map/ppermute | solution.py:596
  342.5 20.1 %all-to-all-start.13 = ((bf16[8,40,1024]{2,1,0:T(8,128)(2,1)}), bf16[8,40,1024]{2,1,0:T(8,128)(2,1)S(1)}, u32[]{:S(2)}, u32[]{:S(2)}) async-start(bf16[8,40,1024]{2,1,0:T(8,128)(2,1)} %bitcast.37), calls=%async_computation.13 | async-start | bytes 1310720 | tf_op jit(solution)/shard_map/all_to_all | solution.py:601
  346.6 16.7 %collective-permute-start.5 = (bf16[128,1024]{1,0:T(8,128)(2,1)S(1)}, bf16[128,1024]{1,0:T(8,128)(2,1)S(1)}, u32[]{:S(2)}, u32[]{:S(2)}) collective-permute-start(bf16[128,1024]{1,0:T(8,128)(2,1)S(1)} %get-tuple-element.71), channel_id=1, source_target_pairs={{0,8},{8,0},{16,24},{24,16},{1,9},{9,1},{17,25},{25,17},{2,10},{10... | collective-permute-start | bytes 786440 | tf_op jit(solution)/shard_map/ppermute | solution.py:593
  363.2 1.6 collective-permute-start.6

commit v6 on v5

--- a/solution.py
+++ b/solution.py
@@ -320,7 +320,7 @@
     return [(cut, slice(None)) for cut in cuts(size, width)]
 
 
-def mlp_call(body, out_shapes, arrays, scratch, flops, moved, at_hand=False):
+def mlp_call(body, out_shapes, arrays, scratch, flops, moved, at_hand=False, limit=None):
     first = vmem_spec if at_hand else any_spec
     return pl.pallas_call(
         body,
@@ -328,7 +328,9 @@
         in_specs=[first] + [any_spec] * (len(arrays) - 1),
         out_specs=[first] + [any_spec] * (len(out_shapes) - 1),
         scratch_shapes=scratch,
-        compiler_params=pltpu.CompilerParams(vmem_limit_bytes=rows_limit if at_hand else mlp_limit),
+        compiler_params=pltpu.CompilerParams(
+            vmem_limit_bytes=limit or (rows_limit if at_hand else mlp_limit)
+        ),
         cost_estimate=pl.CostEstimate(flops=flops, bytes_accessed=moved, transcendentals=0),
     )(*arrays)
 
@@ -337,7 +339,7 @@
     return pltpu.SemaphoreType.DMA((len(tiles),))
 
 
-def expert_forward(rows, weights, parity, keep_slope):
+def expert_forward(rows, weights, parity, keep_slope, limit=None):
     slots, features = rows.shape
     hidden = weights[0].shape[1]
     up_tiles, down_tiles = column_tiles(hidden, forward_cut), column_tiles(features, feature_cut)
@@ -395,6 +397,7 @@
         4 * slots * features * hidden,
         4 * features * hidden + 4 * slots * features + 4 * slots * hidden * int(keep_slope),
         True,
+        limit,
     )
 
 
@@ -627,7 +630,8 @@
             state, send = select_pack(arrived, state, even_gain, even_tt, slots, turn)
         received = to_experts(send)
         if turn < last:
-            (outputs,) = expert_forward(received, weights, 0, False)
+            limit = mlp_limit if turn == 0 else None
+            (outputs,) = expert_forward(received, weights, 0, False, limit)
         else:
             outputs, even_slope = expert_forward(received, weights, 0, True)
         returned = to_experts(outputs)

time: 367 us -> 366 us (level)
  no operation moved by 1% of the time
where the time goes in v6:
time: 366 us; the launch traced here: 365 us
  blocking collectives  232 us (63%)
  Pallas kernels  58.1 us (16%)
  waiting for transfers between devices  49.4 us (13%)
  starting transfers between devices  14.9 us (4%)
  matrix products  5.36 us (1%)
    all_to_all x11, blocking collectives, to_experts(): return lax.all_to_all(x, 'expert', split_axis=0, concat_axis=0, tiled=True)  232 us
    pallas_call x8, Pallas kernels, mlp_call(): pl.pallas_call(body, out_shape=out_shapes, in_specs=[first] + [any_spec]...  49.3 us
    all_to_all x3, waiting for transfers between devices, to_experts(): return lax.all_to_all(x, 'expert', split_axis=0, concat_axis=0, tiled=True)  38.5 us
    all_to_all x3, starting transfers between devices, to_experts(): return lax.all_to_all(x, 'expert', split_axis=0, concat_axis=0, tiled=True)  10.7 us
    ppermute x2, waiting for transfers between devices, shift_chips(): lax.ppermute(x, 'section', [(s, (s + 2 * by) % sections) for s in range(s...  10.2 us
    pallas_call x11, Pallas kernels, small_call(): pl.pallas_call(with_earlier, out_shape=out_shapes, in_specs=[vmem_spec] *...  7.46 us
  transfers between devices with their start and end apart: 10, of which 6 were waited for; matrix products, arithmetic and copies ran while one was open for 2% of the time, Pallas kernels for 2%

profile of v6, /device:TPU:0, one launch (start us, length us, event | category | flops | bytes accessed | tf_op | source)
XLA Modules:
  0.0 364.8 jit_solution(8539013612674148636)
XLA Ops:
  0.6 1.3 shard_map.86
  2.0 0.5 collective-permute-start
  2.5 1.2 select_bitcast_fusion.2
  3.8 0.0 collective-permute-done.refs_1_
  3.8 0.1 collective-permute-start.1
  3.9 0.4 collective-permute-start.2
  4.3 0.0 copy-start
  4.3 0.7 copy-done
  5.0 0.7 shard_map.87
  5.8 25.1 %all_to_all.154 = bf16[8,40,1024]{2,1,0:T(8,128)(2,1)} all-to-all(bf16[8,40,1024]{2,1,0:T(8,128)(2,1)S(1)} %bitcast.69), channel_id=1, replica_groups=mesh['section'=4,'expert'=8] {'expert'}, dimensions={0} | all-to-all | bytes 1310720 | tf_op jit(solution)/shard_map/all_to_all | solution.py:604
  30.9 0.0 collective-permute-done.1.sib_up.refs_2_.refs_3_
  30.9 0.0 collective-permute-done.2.sib_down.refs_3_.refs_4_
  30.9 7.4 %shard_map.88 = bf16[320,1024]{1,0:T(8,128)(2,1)} custom-call(bf16[320,1024]{1,0:T(8,128)(2,1)} %bitcast.91, bf16[1024,2048]{1,0:T(8,128)(2,1)} %bitcast.76, bf16[2048,1024]{1,0:T(8,128)(2,1)} %bitcast.84, bf16[1024,2048]{1,0:T(8,128)(2,1)} %collective-permute-done.1.sib_up.refs_2_.refs_3_, bf16[2048,1024]{1,0:T(8,128)(2,1)} %collective-permute-done.2.sib_down.refs_3_.refs_4_), custom_call_target="tpu_custom_call" | custom-call | flops 2684354560 | bytes 9699328 | tf_op jit(solution)/shard_map/pallas_call | solution.py:325
  38.3 21.2 %all_to_all.155 = bf16[8,40,1024]{2,1,0:T(8,128)(2,1)S(1)} all-to-all(bf16[8,40,1024]{2,1,0:T(8,128)(2,1)} %bitcast.94), channel_id=1, replica_groups=mesh['section'=4,'expert'=8] {'expert'}, dimensions={0} | all-to-all | bytes 1310720 | tf_op jit(solution)/shard_map/all_to_all | solution.py:604
  59.4 0.9 shard_map.89
  60.3 20.6 %all_to_all.156 = bf16[8,40,1024]{2,1,0:T(8,128)(2,1)S(1)} all-to-all(bf16[8,40,1024]{2,1,0:T(8,128)(2,1)S(1)} %bitcast.74), channel_id=1, replica_groups=mesh['section'=4,'expert'=8] {'expert'}, dimensions={0} | all-to-all | bytes 1310720 | tf_op jit(solution)/shard_map/all_to_all | solution.py:604
  80.9 5.4 %shard_map.90 = bf16[320,1024]{1,0:T(8,128)(2,1)S(1)} custom-call(bf16[320,1024]{1,0:T(8,128)(2,1)S(1)} %bitcast.59, bf16[1024,2048]{1,0:T(8,128)(2,1)} %bitcast.77, bf16[2048,1024]{1,0:T(8,128)(2,1)} %bitcast.85, bf16[1024,2048]{1,0:T(8,128)(2,1)} %collective-permute-done.1.sib_up.refs_2_.refs_3_, ...), custom_call_target="tpu_custom_call" | custom-call | flops 2684354560 | bytes 9699328 | tf_op jit(solution)/shard_map/pallas_call | solution.py:325
  86.3 20.4 %all_to_all.157 = bf16[8,40,1024]{2,1,0:T(8,128)(2,1)S(1)} all-to-all(bf16[8,40,1024]{2,1,0:T(8,128)(2,1)S(1)} %bitcast.60), channel_id=1, replica_groups=mesh['section'=4,'expert'=8] {'expert'}, dimensions={0} | all-to-all | bytes 1310720 | tf_op jit(solution)/shard_map/all_to_all | solution.py:604
  106.7 0.5 shard_map.91
  107.2 1.5 collective-permute-start.3
  108.7 5.1 %collective-permute-done.3.refs_0_ = bf16[128,1024]{1,0:T(8,128)(2,1)S(1)} collective-permute-done((bf16[128,1024]{1,0:T(8,128)(2,1)S(1)}, bf16[128,1024]{1,0:T(8,128)(2,1)S(1)}, u32[]{:S(2)}, u32[]{:S(2)}) %collective-permute-start.3) | collective-permute-done | bytes 262176 | tf_op jit(solution)/shard_map/ppermute | solution.py:599
  113.8 0.5 shard_map.92
  114.3 20.3 %all_to_all.158 = bf16[8,40,1024]{2,1,0:T(8,128)(2,1)S(1)} all-to-all(bf16[8,40,1024]{2,1,0:T(8,128)(2,1)S(1)} %bitcast.72), channel_id=1, replica_groups=mesh['section'=4,'expert'=8] {'expert'}, dimensions={0} | all-to-all | bytes 1310720 | tf_op jit(solution)/shard_map/all_to_all | solution.py:604
  134.6 6.9 %shard_map.93 = (bf16[320,1024]{1,0:T(8,128)(2,1)}, bf16[320,2048]{1,0:T(8,128)(2,1)}) custom-call(bf16[320,1024]{1,0:T(8,128)(2,1)S(1)} %bitcast.56, bf16[1024,2048]{1,0:T(8,128)(2,1)} %bitcast.78, bf16[2048,1024]{1,0:T(8,128)(2,1)} %bitcast.86, bf16[1024,2048]{1,0:T(8,128)(2,1)} %collective-permute-done.1.sib_up.refs_2_.refs_3_, ...), custom_call_target="tpu_custom_call" | custom-call | flops 2684354560 | bytes 12320768 | tf_op jit(solution)/shard_map/pallas_call | solution.py:325
  141.5 3.6 all-to-all-start.5
  145.0 4.7 %shard_map.94.ag_ref = f32[320,2048]{1,0:T(8,128)} custom-call(bf16[320,1024]{1,0:T(8,128)(2,1)} %bitcast.92, bf16[2048,1024]{1,0:T(8,128)(2,1)} %bitcast.87, bf16[2048,1024]{1,0:T(8,128)(2,1)} %collective-permute-done.2.sib_down.refs_3_.refs_4_), custom_call_target="tpu_custom_call" | custom-call | flops 1342177280 | bytes 6815744 | tf_op jit(solution)/shard_map/pallas_call | solution.py:325
  149.7 0.7 slice.20.refs_6_
  150.4 11.2 %all-to-all-done.5 = bf16[8,40,1024]{2,1,0:T(8,128)(2,1)S(1)} async-done(((bf16[8,40,1024]{2,1,0:T(8,128)(2,1)}), bf16[8,40,1024]{2,1,0:T(8,128)(2,1)S(1)}, u32[]{:S(2)}, u32[]{:S(2)}) %all-to-all-start.5) | async-done | bytes 655392 | tf_op jit(solution)/shard_map/all_to_all | solution.py:604
  161.6 0.9 shard_map.95
  162.5 21.2 %all_to_all.159 = bf16[8,40,1024]{2,1,0:T(8,128)(2,1)} all-to-all(bf16[8,40,1024]{2,1,0:T(8,128)(2,1)S(1)} %bitcast.71), channel_id=1, replica_groups=mesh['section'=4,'expert'=8] {'expert'}, dimensions={0} | all-to-all | bytes 1310720 | tf_op jit(solution)/shard_map/all_to_all | solution.py:604
  183.7 7.1 %shard_map.96 = (bf16[320,1024]{1,0:T(8,128)(2,1)}, bf16[320,2048]{1,0:T(8,128)(2,1)}, bf16[320,2048]{1,0:T(8,128)(2,1)}) custom-call(bf16[320,1024]{1,0:T(8,128)(2,1)} %bitcast.93, bf16[1024,2048]{1,0:T(8,128)(2,1)} %bitcast.79, bf16[1024,2048]{1,0:T(8,128)(2,1)} %collective-permute-done.1.sib_up.refs_2_.refs_3_, f32[320,2048]{1,0:T(8,128)} %shard_map.94.ag_ref), custom_call_target="tpu_custom_call" | custom-call | flops 2684354560 | bytes 10747904 | tf_op jit(solution)/shard_map/pallas_call | solution.py:325
  190.9 3.6 all-to-all-start.7
  194.4 5.4 %fusion.3.refs_7_.refs_0_ = bf16[320,1024]{1,0:T(8,128)(2,1)S(1)} fusion(bf16[320,2048]{1,0:T(8,128)(2,1)} %get-tuple-element.60, bf16[2048,1024]{1,0:T(8,128)(2,1)} %collective-permute-done.2.sib_down.refs_3_.refs_4_, pred[]{:T(512)S(6)} %eq.12, bf16[1,1,2048,1024]{3,2,1,0:T(8,128)(2,1)} %param.10), kind=kOutput, calls=%fused_computation.3 | convolution fusion | flops 1344602112 | bytes 10354689 | tf_op jit(solution)/shard_map/dot_general | solution.py:654
  199.8 11.4 %all-to-all-done.7 = bf16[8,40,1024]{2,1,0:T(8,128)(2,1)S(1)} async-done(((bf16[8,40,1024]{2,1,0:T(8,128)(2,1)}), bf16[8,40,1024]{2,1,0:T(8,128)(2,1)S(1)}, u32[]{:S(2)}, u32[]{:S(2)}) %all-to-all-start.7) | async-done | bytes 655392 | tf_op jit(solution)/shard_map/all_to_all | solution.py:604
  211.3 0.9 shard_map.97
  212.2 21.2 %all_to_all.160 = bf16[8,40,1024]{2,1,0:T(8,128)(2,1)S(1)} all-to-all(bf16[8,40,1024]{2,1,0:T(8,128)(2,1)S(1)} %bitcast.73), channel_id=1, replica_groups=mesh['section'=4,'expert'=8] {'expert'}, dimensions={0} | all-to-all | bytes 1310720 | tf_op jit(solution)/shard_map/all_to_all | solution.py:604
  233.4 5.6 %shard_map.98 = bf16[320,1024]{1,0:T(8,128)(2,1)S(1)} custom-call(bf16[320,1024]{1,0:T(8,128)(2,1)S(1)} %bitcast.58, bf16[1024,2048]{1,0:T(8,128)(2,1)} %bitcast.80, bf16[2048,1024]{1,0:T(8,128)(2,1)} %bitcast.88, bf16[1024,2048]{1,0:T(8,128)(2,1)} %collective-permute-done.1.sib_up.refs_2_.refs_3_, ...), custom_call_target="tpu_custom_call" | custom-call | flops 2684354560 | bytes 12320768 | tf_op jit(solution)/shard_map/pallas_call | solution.py:325
  239.0 20.6 %all_to_all.161 = bf16[8,40,1024]{2,1,0:T(8,128)(2,1)S(1)} all-to-all(bf16[8,40,1024]{2,1,0:T(8,128)(2,1)S(1)} %bitcast.61), channel_id=1, replica_groups=mesh['section'=4,'expert'=8] {'expert'}, dimensions={0} | all-to-all | bytes 1310720 | tf_op jit(solution)/shard_map/all_to_all | solution.py:604
  259.6 0.6 shard_map.99
  260.2 1.5 collective-permute-start.4
  261.7 5.1 %collective-permute-done.4.refs_0_.refs_1_ = bf16[128,1024]{1,0:T(8,128)(2,1)S(1)} collective-permute-done((bf16[128,1024]{1,0:T(8,128)(2,1)S(1)}, bf16[128,1024]{1,0:T(8,128)(2,1)S(1)}, u32[]{:S(2)}, u32[]{:S(2)}) %collective-permute-start.4) | collective-permute-done | bytes 262176 | tf_op jit(solution)/shard_map/ppermute | solution.py:599
  266.8 0.3 shard_map.100
  267.2 20.6 %all_to_all.162 = bf16[8,40,1024]{2,1,0:T(8,128)(2,1)S(1)} all-to-all(bf16[8,40,1024]{2,1,0:T(8,128)(2,1)S(1)} %bitcast.68), channel_id=1, replica_groups=mesh['section'=4,'expert'=8] {'expert'}, dimensions={0} | all-to-all | bytes 1310720 | tf_op jit(solution)/shard_map/all_to_all | solution.py:604
  287.8 5.8 %shard_map.101 = bf16[320,1024]{1,0:T(8,128)(2,1)S(1)} custom-call(bf16[320,1024]{1,0:T(8,128)(2,1)S(1)} %bitcast.54, bf16[320,1024]{1,0:T(8,128)(2,1)S(1)} %fusion.3.refs_7_.refs_0_, bf16[1024,2048]{1,0:T(8,128)(2,1)} %bitcast.81, bf16[2048,1024]{1,0:T(8,128)(2,1)} %bitcast.89, bf16[1024,2048]{1,0:T(8,128)(2,1)} %collective-permute-done.1.sib_up.refs_2_.refs_3_, ...), custom_call_target="tpu_custom_call" | custom-call | flops 2684354560 | bytes 12320768 | tf_op jit(solution)/shard_map/pallas_call | solution.py:325
  293.6 20.3 %all_to_all.163 = bf16[8,40,1024]{2,1,0:T(8,128)(2,1)S(1)} all-to-all(bf16[8,40,1024]{2,1,0:T(8,128)(2,1)S(1)} %bitcast.57), channel_id=1, replica_groups=mesh['section'=4,'expert'=8] {'expert'}, dimensions={0} | all-to-all | bytes 1310720 | tf_op jit(solution)/shard_map/all_to_all | solution.py:604
  313.9 0.9 shard_map.103
  314.8 20.2 %all_to_all.164 = bf16[8,40,1024]{2,1,0:T(8,128)(2,1)S(1)} all-to-all(bf16[8,40,1024]{2,1,0:T(8,128)(2,1)S(1)} %bitcast.70), channel_id=1, replica_groups=mesh['section'=4,'expert'=8] {'expert'}, dimensions={0} | all-to-all | bytes 1310720 | tf_op jit(solution)/shard_map/all_to_all | solution.py:604
  335.0 6.5 %shard_map.104 = bf16[320,1024]{1,0:T(8,128)(2,1)} custom-call(bf16[320,1024]{1,0:T(8,128)(2,1)S(1)} %bitcast.55, bf16[1024,2048]{1,0:T(8,128)(2,1)} %bitcast.82, bf16[2048,1024]{1,0:T(8,128)(2,1)} %bitcast.90, bf16[1024,2048]{1,0:T(8,128)(2,1)} %collective-permute-done.1.sib_up.refs_2_.refs_3_, ...), custom_call_target="tpu_custom_call" | custom-call | flops 2684354560 | bytes 12320768 | tf_op jit(solution)/shard_map/pallas_call | solution.py:325
  341.5 3.6 all-to-all-start.13
  345.1 0.5 shard_map.102
  345.6 0.1 select_bitcast_fusion.1
  345.7 0.1 collective-permute-start.5
  345.7 15.9 %all-to-all-done.13 = bf16[8,40,1024]{2,1,0:T(8,128)(2,1)S(1)} async-done(((bf16[8,40,1024]{2,1,0:T(8,128)(2,1)}), bf16[8,40,1024]{2,1,0:T(8,128)(2,1)S(1)}, u32[]{:S(2)}, u32[]{:S(2)}) %all-to-all-start.13) | async-done | bytes 655392 | tf_op jit(solution)/shard_map/all_to_all | solution.py:604
  361.6 0.6 shard_map.105
  362.2 0.1 select_bitcast_fusion
  362.3 0.1 collective-permute-start.6
  362.4 0.0 collective-permute-done.5
  362.4 0.9 maximum_select_fusion
  363.3 0.6 collective-permute-done.6
  363.9 0.9 maximum_select_fusion.1
Async XLA Ops:
  2.0 1.8 collective-permute-start
  3.8 27.1 %collective-permute-start.1 = (bf16[1024,2048]{1,0:T(8,128)(2,1)}, bf16[1024,2048]{1,0:T(8,128)(2,1)}, u32[]{:S(2)}, u32[]{:S(2)}) collective-permute-start(bf16[1024,2048]{1,0:T(8,128)(2,1)} %bitcast.75), channel_id=1, source_target_pairs={{0,8},{8,0},{16,24},{24,16},{1,9},{9,1},{17,25},{25,17},{2,10},{10... | collective-permute-start | bytes 12582920 | tf_op jit(solution)/shard_map/ppermute | solution.py:596
  3.9 27.0 %collective-permute-start.2 = (bf16[2048,1024]{1,0:T(8,128)(2,1)}, bf16[2048,1024]{1,0:T(8,128)(2,1)}, u32[]{:S(2)}, u32[]{:S(2)}) collective-permute-start(bf16[2048,1024]{1,0:T(8,128)(2,1)} %bitcast.83), channel_id=1, source_target_pairs={{0,8},{8,0},{16,24},{24,16},{1,9},{9,1},{17,25},{25,17},{2,10},{10... | collective-permute-start | bytes 12582920 | tf_op jit(solution)/shard_map/ppermute | solution.py:596
  4.3 0.7 copy-start
  107.2 6.6 %collective-permute-start.3 = (bf16[128,1024]{1,0:T(8,128)(2,1)S(1)}, bf16[128,1024]{1,0:T(8,128)(2,1)S(1)}, u32[]{:S(2)}, u32[]{:S(2)}) collective-permute-start(bf16[128,1024]{1,0:T(8,128)(2,1)S(1)} %shard_map.91), channel_id=1, source_target_pairs={{0,16},{8,24},{16,0},{24,8},{1,17},{9,25},{17,1},{25,9},{2,18},{10... | collective-permute-start | bytes 786440 | tf_op jit(solution)/shard_map/ppermute | solution.py:599
  141.5 20.1 %all-to-all-start.5 = ((bf16[8,40,1024]{2,1,0:T(8,128)(2,1)}), bf16[8,40,1024]{2,1,0:T(8,128)(2,1)S(1)}, u32[]{:S(2)}, u32[]{:S(2)}) async-start(bf16[8,40,1024]{2,1,0:T(8,128)(2,1)} %bitcast.19), calls=%async_computation.5 | async-start | bytes 1310720 | tf_op jit(solution)/shard_map/all_to_all | solution.py:604
  190.9 20.4 %all-to-all-start.7 = ((bf16[8,40,1024]{2,1,0:T(8,128)(2,1)}), bf16[8,40,1024]{2,1,0:T(8,128)(2,1)S(1)}, u32[]{:S(2)}, u32[]{:S(2)}) async-start(bf16[8,40,1024]{2,1,0:T(8,128)(2,1)} %bitcast.95), calls=%async_computation.7 | async-start | bytes 1310720 | tf_op jit(solution)/shard_map/all_to_all | solution.py:604
  260.2 6.6 %collective-permute-start.4 = (bf16[128,1024]{1,0:T(8,128)(2,1)S(1)}, bf16[128,1024]{1,0:T(8,128)(2,1)S(1)}, u32[]{:S(2)}, u32[]{:S(2)}) collective-permute-start(bf16[128,1024]{1,0:T(8,128)(2,1)S(1)} %shard_map.99), channel_id=1, source_target_pairs={{0,16},{8,24},{16,0},{24,8},{1,17},{9,25},{17,1},{25,9},{2,18},{10... | collective-permute-start | bytes 786440 | tf_op jit(solution)/shard_map/ppermute | solution.py:599
  341.5 20.1 %all-to-all-start.13 = ((bf16[8,40,1024]{2,1,0:T(8,128)(2,1)}), bf16[8,40,1024]{2,1,0:T(8,128)(2,1)S(1)}, u32[]{:S(2)}, u32[]{:S(2)}) async-start(bf16[8,40,1024]{2,1,0:T(8,128)(2,1)} %bitcast.37), calls=%async_computation.13 | async-start | bytes 1310720 | tf_op jit(solution)/shard_map/all_to_all | solution.py:604
  345.7 16.7 %collective-permute-start.5 = (bf16[128,1024]{1,0:T(8,128)(2,1)S(1)}, bf16[128,1024]{1,0:T(8,128)(2,1)S(1)}, u32[]{:S(2)}, u32[]{:S(2)}) collective-permute-start(bf16[128,1024]{1,0:T(8,128)(2,1)S(1)} %get-tuple-element.71), channel_id=1, source_target_pairs={{0,8},{8,0},{16,24},{24,16},{1,9},{9,1},{17,25},{25,17},{2,10},{10... | collective-permute-start | bytes 786440 | tf_op jit(solution)/shard_map/ppermute | solution.py:596
  362.3 1.6 collective-permute-start.6

commit v7 on v6

--- a/solution.py
+++ b/solution.py
@@ -522,12 +522,9 @@
     tiles, out_tiles = column_tiles(hidden, backward_cut), column_tiles(features, feature_cut)
     up_rows = row_tiles(features, feature_cut)
 
-    def body(rows_ref, own_up, sib_up, ag_ref, out_ref, slope_ref, active_ref, *refs):
-        up_buf, ag_buf, slope_buf, active_buf, pre_grad, x_ref, out_buf = refs[:7]
-        up_in, grad_in, slope_out, active_out = [TileCopies(tiles, sem) for sem in refs[7:11]]
-        rows_out = TileCopies(out_tiles, refs[11])
-        rows_in = pltpu.make_async_copy(rows_ref, x_ref, refs[12])
-        rows_in.start()
+    def body(x_ref, own_up, sib_up, ag_ref, out_ref, slope_ref, active_ref, *refs):
+        up_buf, ag_buf, slope_buf, active_buf, pre_grad = refs[:5]
+        up_in, grad_in, slope_out, active_out = [TileCopies(tiles, sem) for sem in refs[5:9]]
 
         def begin(up):
             for i in range(len(tiles)):
@@ -537,8 +534,6 @@
         start_from(parity, (own_up,), (sib_up,), begin)
         for i, at in enumerate(tiles):
             up_in.copy(own_up, up_buf, i).wait()
-            if i == 0:
-                rows_in.wait()
             pre = jnp.dot(x_ref[...], up_buf[at], preferred_element_type=f32)
             value, slope = gelu_parts(pre)
             slope_buf[at] = slope.astype(bf16)
@@ -547,13 +542,10 @@
             active_out.copy(active_buf, active_ref, i).start()
             grad_in.copy(ag_ref, ag_buf, i).wait()
             pre_grad[at] = (ag_buf[at] * slope).astype(bf16)
-        for i, (at, rows_at) in enumerate(zip(out_tiles, up_rows)):
-            out_buf[at] = lax.dot_general(
+        for at, rows_at in zip(out_tiles, up_rows):
+            out_ref[at] = lax.dot_general(
                 pre_grad[...], up_buf[rows_at], contract_last, preferred_element_type=f32
             ).astype(bf16)
-            rows_out.copy(out_buf, out_ref, i).start()
-        for i in range(len(out_tiles)):
-            rows_out.copy(out_buf, out_ref, i).wait()
         for i in range(len(tiles)):
             slope_out.copy(slope_buf, slope_ref, i).wait()
             active_out.copy(active_buf, active_ref, i).wait()
@@ -568,17 +560,14 @@
             pltpu.VMEM((slots, hidden), bf16),
             pltpu.VMEM((slots, hidden), bf16),
             pltpu.VMEM((slots, hidden), bf16),
-            pltpu.VMEM((slots, features), bf16),
-            pltpu.VMEM((slots, features), bf16),
             copy_slots(tiles),
             copy_slots(tiles),
             copy_slots(tiles),
             copy_slots(tiles),
-            copy_slots(out_tiles),
-            pltpu.SemaphoreType.DMA,
         ],
         4 * slots * features * hidden,
         2 * features * hidden + 10 * slots * hidden,
+        True,
     )
 
 

time: 366 us -> 366 us (level)
  no operation moved by 1% of the time
where the time goes in v7:
time: 366 us; the launch traced here: 365 us
  blocking collectives  232 us (63%)
  Pallas kernels  58 us (16%)
  waiting for transfers between devices  49.4 us (13%)
  starting transfers between devices  14.9 us (4%)
  matrix products  5.36 us (1%)
    all_to_all x11, blocking collectives, to_experts(): return lax.all_to_all(x, 'expert', split_axis=0, concat_axis=0, tiled=True)  232 us
    pallas_call x8, Pallas kernels, mlp_call(): pl.pallas_call(body, out_shape=out_shapes, in_specs=[first] + [any_spec]...  49.1 us
    all_to_all x3, waiting for transfers between devices, to_experts(): return lax.all_to_all(x, 'expert', split_axis=0, concat_axis=0, tiled=True)  38.5 us
    all_to_all x3, starting transfers between devices, to_experts(): return lax.all_to_all(x, 'expert', split_axis=0, concat_axis=0, tiled=True)  10.7 us
    ppermute x2, waiting for transfers between devices, shift_chips(): lax.ppermute(x, 'section', [(s, (s + 2 * by) % sections) for s in range(s...  10.2 us
    pallas_call x11, Pallas kernels, small_call(): pl.pallas_call(with_earlier, out_shape=out_shapes, in_specs=[vmem_spec] *...  7.47 us
  transfers between devices with their start and end apart: 10, of which 6 were waited for; matrix products, arithmetic and copies ran while one was open for 2% of the time, Pallas kernels for 2%

profile of v7, /device:TPU:0, one launch (start us, length us, event | category | flops | bytes accessed | tf_op | source)
XLA Modules:
  0.0 364.6 jit_solution(15436879162948877425)
XLA Ops:
  0.6 1.3 shard_map.86
  2.0 0.5 collective-permute-start
  2.5 1.2 select_bitcast_fusion.2
  3.8 0.0 collective-permute-done.refs_1_
  3.8 0.1 collective-permute-start.1
  3.9 0.4 collective-permute-start.2
  4.3 0.0 copy-start
  4.3 0.7 copy-done
  5.0 0.7 shard_map.87
  5.8 25.1 %all_to_all.154 = bf16[8,40,1024]{2,1,0:T(8,128)(2,1)} all-to-all(bf16[8,40,1024]{2,1,0:T(8,128)(2,1)S(1)} %bitcast.70), channel_id=1, replica_groups=mesh['section'=4,'expert'=8] {'expert'}, dimensions={0} | all-to-all | bytes 1310720 | tf_op jit(solution)/shard_map/all_to_all | solution.py:593
  30.9 0.0 collective-permute-done.1.sib_up.refs_2_.refs_3_
  30.9 0.0 collective-permute-done.2.sib_down.refs_3_.refs_4_
  30.9 7.4 %shard_map.88 = bf16[320,1024]{1,0:T(8,128)(2,1)} custom-call(bf16[320,1024]{1,0:T(8,128)(2,1)} %bitcast.92, bf16[1024,2048]{1,0:T(8,128)(2,1)} %bitcast.77, bf16[2048,1024]{1,0:T(8,128)(2,1)} %bitcast.85, bf16[1024,2048]{1,0:T(8,128)(2,1)} %collective-permute-done.1.sib_up.refs_2_.refs_3_, bf16[2048,1024]{1,0:T(8,128)(2,1)} %collective-permute-done.2.sib_down.refs_3_.refs_4_), custom_call_target="tpu_custom_call" | custom-call | flops 2684354560 | bytes 9699328 | tf_op jit(solution)/shard_map/pallas_call | solution.py:325
  38.3 21.2 %all_to_all.155 = bf16[8,40,1024]{2,1,0:T(8,128)(2,1)S(1)} all-to-all(bf16[8,40,1024]{2,1,0:T(8,128)(2,1)} %bitcast.94), channel_id=1, replica_groups=mesh['section'=4,'expert'=8] {'expert'}, dimensions={0} | all-to-all | bytes 1310720 | tf_op jit(solution)/shard_map/all_to_all | solution.py:593
  59.4 0.9 shard_map.89
  60.3 20.6 %all_to_all.156 = bf16[8,40,1024]{2,1,0:T(8,128)(2,1)S(1)} all-to-all(bf16[8,40,1024]{2,1,0:T(8,128)(2,1)S(1)} %bitcast.75), channel_id=1, replica_groups=mesh['section'=4,'expert'=8] {'expert'}, dimensions={0} | all-to-all | bytes 1310720 | tf_op jit(solution)/shard_map/all_to_all | solution.py:593
  80.9 5.4 %shard_map.90 = bf16[320,1024]{1,0:T(8,128)(2,1)S(1)} custom-call(bf16[320,1024]{1,0:T(8,128)(2,1)S(1)} %bitcast.60, bf16[1024,2048]{1,0:T(8,128)(2,1)} %bitcast.78, bf16[2048,1024]{1,0:T(8,128)(2,1)} %bitcast.86, bf16[1024,2048]{1,0:T(8,128)(2,1)} %collective-permute-done.1.sib_up.refs_2_.refs_3_, ...), custom_call_target="tpu_custom_call" | custom-call | flops 2684354560 | bytes 9699328 | tf_op jit(solution)/shard_map/pallas_call | solution.py:325
  86.3 20.4 %all_to_all.157 = bf16[8,40,1024]{2,1,0:T(8,128)(2,1)S(1)} all-to-all(bf16[8,40,1024]{2,1,0:T(8,128)(2,1)S(1)} %bitcast.61), channel_id=1, replica_groups=mesh['section'=4,'expert'=8] {'expert'}, dimensions={0} | all-to-all | bytes 1310720 | tf_op jit(solution)/shard_map/all_to_all | solution.py:593
  106.7 0.5 shard_map.91
  107.2 1.5 collective-permute-start.3
  108.7 5.1 %collective-permute-done.3.refs_0_ = bf16[128,1024]{1,0:T(8,128)(2,1)S(1)} collective-permute-done((bf16[128,1024]{1,0:T(8,128)(2,1)S(1)}, bf16[128,1024]{1,0:T(8,128)(2,1)S(1)}, u32[]{:S(2)}, u32[]{:S(2)}) %collective-permute-start.3) | collective-permute-done | bytes 262176 | tf_op jit(solution)/shard_map/ppermute | solution.py:588
  113.8 0.5 shard_map.92
  114.3 20.3 %all_to_all.158 = bf16[8,40,1024]{2,1,0:T(8,128)(2,1)S(1)} all-to-all(bf16[8,40,1024]{2,1,0:T(8,128)(2,1)S(1)} %bitcast.73), channel_id=1, replica_groups=mesh['section'=4,'expert'=8] {'expert'}, dimensions={0} | all-to-all | bytes 1310720 | tf_op jit(solution)/shard_map/all_to_all | solution.py:593
  134.6 6.9 %shard_map.93 = (bf16[320,1024]{1,0:T(8,128)(2,1)}, bf16[320,2048]{1,0:T(8,128)(2,1)}) custom-call(bf16[320,1024]{1,0:T(8,128)(2,1)S(1)} %bitcast.57, bf16[1024,2048]{1,0:T(8,128)(2,1)} %bitcast.79, bf16[2048,1024]{1,0:T(8,128)(2,1)} %bitcast.87, bf16[1024,2048]{1,0:T(8,128)(2,1)} %collective-permute-done.1.sib_up.refs_2_.refs_3_, ...), custom_call_target="tpu_custom_call" | custom-call | flops 2684354560 | bytes 12320768 | tf_op jit(solution)/shard_map/pallas_call | solution.py:325
  141.5 3.6 all-to-all-start.5
  145.0 4.7 %shard_map.94.ag_ref = f32[320,2048]{1,0:T(8,128)} custom-call(bf16[320,1024]{1,0:T(8,128)(2,1)} %bitcast.93, bf16[2048,1024]{1,0:T(8,128)(2,1)} %bitcast.88, bf16[2048,1024]{1,0:T(8,128)(2,1)} %collective-permute-done.2.sib_down.refs_3_.refs_4_), custom_call_target="tpu_custom_call" | custom-call | flops 1342177280 | bytes 6815744 | tf_op jit(solution)/shard_map/pallas_call | solution.py:325
  149.7 0.7 slice.20.refs_6_
  150.4 11.2 %all-to-all-done.5 = bf16[8,40,1024]{2,1,0:T(8,128)(2,1)S(1)} async-done(((bf16[8,40,1024]{2,1,0:T(8,128)(2,1)}), bf16[8,40,1024]{2,1,0:T(8,128)(2,1)S(1)}, u32[]{:S(2)}, u32[]{:S(2)}) %all-to-all-start.5) | async-done | bytes 655392 | tf_op jit(solution)/shard_map/all_to_all | solution.py:593
  161.6 0.9 shard_map.95
  162.5 21.1 %all_to_all.159 = bf16[8,40,1024]{2,1,0:T(8,128)(2,1)S(1)} all-to-all(bf16[8,40,1024]{2,1,0:T(8,128)(2,1)S(1)} %bitcast.72), channel_id=1, replica_groups=mesh['section'=4,'expert'=8] {'expert'}, dimensions={0} | all-to-all | bytes 1310720 | tf_op jit(solution)/shard_map/all_to_all | solution.py:593
  183.6 7.0 %shard_map.96 = (bf16[320,1024]{1,0:T(8,128)(2,1)}, bf16[320,2048]{1,0:T(8,128)(2,1)}, bf16[320,2048]{1,0:T(8,128)(2,1)}) custom-call(bf16[320,1024]{1,0:T(8,128)(2,1)S(1)} %bitcast.54, bf16[1024,2048]{1,0:T(8,128)(2,1)} %bitcast.80, bf16[1024,2048]{1,0:T(8,128)(2,1)} %collective-permute-done.1.sib_up.refs_2_.refs_3_, f32[320,2048]{1,0:T(8,128)} %shard_map.94.ag_ref), custom_call_target="tpu_custom_call" | custom-call | flops 2684354560 | bytes 10747904 | tf_op jit(solution)/shard_map/pallas_call | solution.py:325
  190.7 3.6 all-to-all-start.7
  194.2 5.4 %fusion.3.refs_7_.refs_0_ = bf16[320,1024]{1,0:T(8,128)(2,1)S(1)} fusion(bf16[320,2048]{1,0:T(8,128)(2,1)} %get-tuple-element.60, bf16[2048,1024]{1,0:T(8,128)(2,1)} %collective-permute-done.2.sib_down.refs_3_.refs_4_, pred[]{:T(512)S(6)} %eq.12, bf16[1,1,2048,1024]{3,2,1,0:T(8,128)(2,1)} %param.10), kind=kOutput, calls=%fused_computation.3 | convolution fusion | flops 1344602112 | bytes 10354689 | tf_op jit(solution)/shard_map/dot_general | solution.py:643
  199.6 11.4 %all-to-all-done.7 = bf16[8,40,1024]{2,1,0:T(8,128)(2,1)S(1)} async-done(((bf16[8,40,1024]{2,1,0:T(8,128)(2,1)}), bf16[8,40,1024]{2,1,0:T(8,128)(2,1)S(1)}, u32[]{:S(2)}, u32[]{:S(2)}) %all-to-all-start.7) | async-done | bytes 655392 | tf_op jit(solution)/shard_map/all_to_all | solution.py:593
  211.0 0.9 shard_map.97
  212.0 21.2 %all_to_all.160 = bf16[8,40,1024]{2,1,0:T(8,128)(2,1)S(1)} all-to-all(bf16[8,40,1024]{2,1,0:T(8,128)(2,1)S(1)} %bitcast.74), channel_id=1, replica_groups=mesh['section'=4,'expert'=8] {'expert'}, dimensions={0} | all-to-all | bytes 1310720 | tf_op jit(solution)/shard_map/all_to_all | solution.py:593
  233.2 5.6 %shard_map.98 = bf16[320,1024]{1,0:T(8,128)(2,1)S(1)} custom-call(bf16[320,1024]{1,0:T(8,128)(2,1)S(1)} %bitcast.59, bf16[1024,2048]{1,0:T(8,128)(2,1)} %bitcast.81, bf16[2048,1024]{1,0:T(8,128)(2,1)} %bitcast.89, bf16[1024,2048]{1,0:T(8,128)(2,1)} %collective-permute-done.1.sib_up.refs_2_.refs_3_, ...), custom_call_target="tpu_custom_call" | custom-call | flops 2684354560 | bytes 12320768 | tf_op jit(solution)/shard_map/pallas_call | solution.py:325
  238.8 20.6 %all_to_all.161 = bf16[8,40,1024]{2,1,0:T(8,128)(2,1)S(1)} all-to-all(bf16[8,40,1024]{2,1,0:T(8,128)(2,1)S(1)} %bitcast.62), channel_id=1, replica_groups=mesh['section'=4,'expert'=8] {'expert'}, dimensions={0} | all-to-all | bytes 1310720 | tf_op jit(solution)/shard_map/all_to_all | solution.py:593
  259.4 0.6 shard_map.99
  260.0 1.5 collective-permute-start.4
  261.5 5.1 %collective-permute-done.4.refs_0_.refs_1_ = bf16[128,1024]{1,0:T(8,128)(2,1)S(1)} collective-permute-done((bf16[128,1024]{1,0:T(8,128)(2,1)S(1)}, bf16[128,1024]{1,0:T(8,128)(2,1)S(1)}, u32[]{:S(2)}, u32[]{:S(2)}) %collective-permute-start.4) | collective-permute-done | bytes 262176 | tf_op jit(solution)/shard_map/ppermute | solution.py:588
  266.6 0.3 shard_map.100
  267.0 20.6 %all_to_all.162 = bf16[8,40,1024]{2,1,0:T(8,128)(2,1)S(1)} all-to-all(bf16[8,40,1024]{2,1,0:T(8,128)(2,1)S(1)} %bitcast.69), channel_id=1, replica_groups=mesh['section'=4,'expert'=8] {'expert'}, dimensions={0} | all-to-all | bytes 1310720 | tf_op jit(solution)/shard_map/all_to_all | solution.py:593
  287.6 5.8 %shard_map.101 = bf16[320,1024]{1,0:T(8,128)(2,1)S(1)} custom-call(bf16[320,1024]{1,0:T(8,128)(2,1)S(1)} %bitcast.55, bf16[320,1024]{1,0:T(8,128)(2,1)S(1)} %fusion.3.refs_7_.refs_0_, bf16[1024,2048]{1,0:T(8,128)(2,1)} %bitcast.82, bf16[2048,1024]{1,0:T(8,128)(2,1)} %bitcast.90, bf16[1024,2048]{1,0:T(8,128)(2,1)} %collective-permute-done.1.sib_up.refs_2_.refs_3_, ...), custom_call_target="tpu_custom_call" | custom-call | flops 2684354560 | bytes 12320768 | tf_op jit(solution)/shard_map/pallas_call | solution.py:325
  293.3 20.3 %all_to_all.163 = bf16[8,40,1024]{2,1,0:T(8,128)(2,1)S(1)} all-to-all(bf16[8,40,1024]{2,1,0:T(8,128)(2,1)S(1)} %bitcast.58), channel_id=1, replica_groups=mesh['section'=4,'expert'=8] {'expert'}, dimensions={0} | all-to-all | bytes 1310720 | tf_op jit(solution)/shard_map/all_to_all | solution.py:593
  313.6 0.9 shard_map.103
  314.6 20.2 %all_to_all.164 = bf16[8,40,1024]{2,1,0:T(8,128)(2,1)S(1)} all-to-all(bf16[8,40,1024]{2,1,0:T(8,128)(2,1)S(1)} %bitcast.71), channel_id=1, replica_groups=mesh['section'=4,'expert'=8] {'expert'}, dimensions={0} | all-to-all | bytes 1310720 | tf_op jit(solution)/shard_map/all_to_all | solution.py:593
  334.8 6.5 %shard_map.104 = bf16[320,1024]{1,0:T(8,128)(2,1)} custom-call(bf16[320,1024]{1,0:T(8,128)(2,1)S(1)} %bitcast.56, bf16[1024,2048]{1,0:T(8,128)(2,1)} %bitcast.83, bf16[2048,1024]{1,0:T(8,128)(2,1)} %bitcast.91, bf16[1024,2048]{1,0:T(8,128)(2,1)} %collective-permute-done.1.sib_up.refs_2_.refs_3_, ...), custom_call_target="tpu_custom_call" | custom-call | flops 2684354560 | bytes 12320768 | tf_op jit(solution)/shard_map/pallas_call | solution.py:325
  341.3 3.6 all-to-all-start.13
  344.9 0.5 shard_map.102
  345.4 0.1 select_bitcast_fusion.1
  345.4 0.1 collective-permute-start.5
  345.5 15.9 %all-to-all-done.13 = bf16[8,40,1024]{2,1,0:T(8,128)(2,1)S(1)} async-done(((bf16[8,40,1024]{2,1,0:T(8,128)(2,1)}), bf16[8,40,1024]{2,1,0:T(8,128)(2,1)S(1)}, u32[]{:S(2)}, u32[]{:S(2)}) %all-to-all-start.13) | async-done | bytes 655392 | tf_op jit(solution)/shard_map/all_to_all | solution.py:593
  361.4 0.6 shard_map.105
  362.0 0.1 select_bitcast_fusion
  362.1 0.1 collective-permute-start.6
  362.2 0.0 collective-permute-done.5
  362.2 0.9 maximum_select_fusion
  363.0 0.6 collective-permute-done.6
  363.7 0.9 maximum_select_fusion.1
Async XLA Ops:
  2.0 1.8 collective-permute-start
  3.8 27.1 %collective-permute-start.1 = (bf16[1024,2048]{1,0:T(8,128)(2,1)}, bf16[1024,2048]{1,0:T(8,128)(2,1)}, u32[]{:S(2)}, u32[]{:S(2)}) collective-permute-start(bf16[1024,2048]{1,0:T(8,128)(2,1)} %bitcast.76), channel_id=1, source_target_pairs={{0,8},{8,0},{16,24},{24,16},{1,9},{9,1},{17,25},{25,17},{2,10},{10... | collective-permute-start | bytes 12582920 | tf_op jit(solution)/shard_map/ppermute | solution.py:585
  3.9 27.0 %collective-permute-start.2 = (bf16[2048,1024]{1,0:T(8,128)(2,1)}, bf16[2048,1024]{1,0:T(8,128)(2,1)}, u32[]{:S(2)}, u32[]{:S(2)}) collective-permute-start(bf16[2048,1024]{1,0:T(8,128)(2,1)} %bitcast.84), channel_id=1, source_target_pairs={{0,8},{8,0},{16,24},{24,16},{1,9},{9,1},{17,25},{25,17},{2,10},{10... | collective-permute-start | bytes 12582920 | tf_op jit(solution)/shard_map/ppermute | solution.py:585
  4.3 0.7 copy-start
  107.2 6.6 %collective-permute-start.3 = (bf16[128,1024]{1,0:T(8,128)(2,1)S(1)}, bf16[128,1024]{1,0:T(8,128)(2,1)S(1)}, u32[]{:S(2)}, u32[]{:S(2)}) collective-permute-start(bf16[128,1024]{1,0:T(8,128)(2,1)S(1)} %shard_map.91), channel_id=1, source_target_pairs={{0,16},{8,24},{16,0},{24,8},{1,17},{9,25},{17,1},{25,9},{2,18},{10... | collective-permute-start | bytes 786440 | tf_op jit(solution)/shard_map/ppermute | solution.py:588
  141.5 20.1 %all-to-all-start.5 = ((bf16[8,40,1024]{2,1,0:T(8,128)(2,1)}), bf16[8,40,1024]{2,1,0:T(8,128)(2,1)S(1)}, u32[]{:S(2)}, u32[]{:S(2)}) async-start(bf16[8,40,1024]{2,1,0:T(8,128)(2,1)} %bitcast.19), calls=%async_computation.5 | async-start | bytes 1310720 | tf_op jit(solution)/shard_map/all_to_all | solution.py:593
  190.7 20.4 %all-to-all-start.7 = ((bf16[8,40,1024]{2,1,0:T(8,128)(2,1)}), bf16[8,40,1024]{2,1,0:T(8,128)(2,1)S(1)}, u32[]{:S(2)}, u32[]{:S(2)}) async-start(bf16[8,40,1024]{2,1,0:T(8,128)(2,1)} %bitcast.23), calls=%async_computation.7 | async-start | bytes 1310720 | tf_op jit(solution)/shard_map/all_to_all | solution.py:593
  260.0 6.6 %collective-permute-start.4 = (bf16[128,1024]{1,0:T(8,128)(2,1)S(1)}, bf16[128,1024]{1,0:T(8,128)(2,1)S(1)}, u32[]{:S(2)}, u32[]{:S(2)}) collective-permute-start(bf16[128,1024]{1,0:T(8,128)(2,1)S(1)} %shard_map.99), channel_id=1, source_target_pairs={{0,16},{8,24},{16,0},{24,8},{1,17},{9,25},{17,1},{25,9},{2,18},{10... | collective-permute-start | bytes 786440 | tf_op jit(solution)/shard_map/ppermute | solution.py:588
  341.3 20.1 %all-to-all-start.13 = ((bf16[8,40,1024]{2,1,0:T(8,128)(2,1)}), bf16[8,40,1024]{2,1,0:T(8,128)(2,1)S(1)}, u32[]{:S(2)}, u32[]{:S(2)}) async-start(bf16[8,40,1024]{2,1,0:T(8,128)(2,1)} %bitcast.37), calls=%async_computation.13 | async-start | bytes 1310720 | tf_op jit(solution)/shard_map/all_to_all | solution.py:593
  345.4 16.7 %collective-permute-start.5 = (bf16[128,1024]{1,0:T(8,128)(2,1)S(1)}, bf16[128,1024]{1,0:T(8,128)(2,1)S(1)}, u32[]{:S(2)}, u32[]{:S(2)}) collective-permute-start(bf16[128,1024]{1,0:T(8,128)(2,1)S(1)} %get-tuple-element.71), channel_id=1, source_target_pairs={{0,8},{8,0},{16,24},{24,16},{1,9},{9,1},{17,25},{25,17},{2,10},{10... | collective-permute-start | bytes 786440 | tf_op jit(solution)/shard_map/ppermute | solution.py:585
  362.1 1.6 collective-permute-start.6
